TPU v7x, 32 devices: a whole 2x2x4 slice. The times are simulated.
32 devices in a mesh: groups: 2 (over y), seq: 4 (over z), head: 4 (over x, core).
Axes of the slice: x: 2, y: 2, z: 4, core: 2. Of those that a mesh axis runs over, the one named last changes fastest.
Arguments:
- query: bfloat16 [8192, 1536], P(('groups', 'seq', 'head')), parts along dimension 0, may hold values from -150 to 150
- key_in: bfloat16 [8192, 1536], P(('groups', 'seq', 'head')), parts along dimension 0, may hold values from -6 to 6
- value: bfloat16 [8192, 1536], P(('groups', 'seq', 'head')), parts along dimension 0, may hold values from -6 to 6
- grad_out: bfloat16 [8192, 1536], P(('groups', 'seq', 'head')), parts along dimension 0, may hold values from -6 to 6
- pattern: int32 [16, 3], replicated, may hold values from 0 to 15, as said below
- live: int32 [16, 3], replicated, may hold values from 0 to 1, as said below
Outputs:
- attended: bfloat16 [8192, 1536], P(('groups', 'seq', 'head')), parts along dimension 0
- query_grad: bfloat16 [8192, 1536], P(('groups', 'seq', 'head')), parts along dimension 0
- key_grad: bfloat16 [8192, 1536], P(('groups', 'seq', 'head')), parts along dimension 0
- value_grad: bfloat16 [8192, 1536], P(('groups', 'seq', 'head')), parts along dimension 0
There are 2 independent parts, one for each index of `groups`. A program takes and returns all parts, laid end to end along the dimension named above; an argument that names none is the same for every part. Nothing has to cross between parts.
Inputs may be any that keep to these rules, and one draw needn't show every extreme that they name: `pattern`: each entry names a tile of the same frame-tile layer as its query tile or of the layer just before or after it; the live entries of a row are distinct; an entry that is not live names the query tile itself. Slot 0 of every row is live and names the query tile itself.
All inputs are finite; a program needn't handle non-finite values.
Results may differ from a plain program's by a relative error of at most 0.015.
Values may be sent and summed in bfloat16 or wider, within the bound.
No kernel may reach another device: no remote copies, remote signals or barrier semaphores. Data moves between devices by JAX's collectives and lax.ppermute only.
A program may use at most 128 MiB of HBM per device.

v0:
```python
import jax
import jax.numpy as jnp
from jax import lax
from jax.sharding import PartitionSpec as P

HEADS = 12
HEAD_DIM = 128


def extended_2(cells, sides, width):
    for axis, dim in sides:
        count = lax.axis_size(axis)
        ends = count - 1
        head = lax.slice_in_dim(cells, 0, width, axis=dim)
        tail = lax.slice_in_dim(cells, cells.shape[dim] - width, cells.shape[dim], axis=dim)
        cells = jnp.concatenate(
            [
                lax.ppermute(tail, axis, [(i, (i + 1) % count) for i in range(ends)]),
                cells,
                lax.ppermute(head, axis, [((i + 1) % count, i) for i in range(ends)]),
            ],
            axis=dim,
        )
    return cells


def shifted(value, axis, steps):
    count = lax.axis_size(axis)
    initial, last = (max(0, -steps), min(count, count - steps))
    return lax.ppermute(value, axis, [(source, source + steps) for source in range(initial, last)])


def head_split(rows_flat, tiles, heads):
    width = rows_flat.shape[1]
    return rows_flat.reshape(tiles, rows_flat.shape[0] // tiles, heads, width // heads).transpose(
        2, 0, 1, 3
    )


def head_join(blocks):
    heads, tiles, tile_size, head_size = blocks.shape
    return blocks.transpose(1, 2, 0, 3).reshape(tiles * tile_size, heads * head_size)


def forward_head(q_tile, g_tile, k_all, v_all, tile_ids, alive, scale):
    k_sel = k_all[tile_ids]
    v_sel = v_all[tile_ids]
    scores = jnp.einsum("aqd,ankd->aqnk", q_tile, k_sel, preferred_element_type=jnp.float32) * scale
    scores = jnp.where(alive[:, None, :, None], scores, -jnp.inf)
    peak = jnp.max(scores, axis=(2, 3), keepdims=True)
    exponent = jnp.exp(scores - peak)
    total = jnp.sum(exponent, axis=(2, 3), keepdims=True)
    weights = exponent / total
    weights_low = weights.astype(jnp.bfloat16)
    attended = jnp.einsum(
        "aqnk,ankd->aqd", weights_low, v_sel, preferred_element_type=jnp.float32
    ).astype(jnp.bfloat16)
    weight_grad = jnp.einsum("aqd,ankd->aqnk", g_tile, v_sel, preferred_element_type=jnp.float32)
    delta = jnp.sum(weights * weight_grad, axis=(2, 3), keepdims=True)
    score_grad = (weights * (weight_grad - delta) * scale).astype(jnp.bfloat16)
    query_grad = jnp.einsum(
        "aqnk,ankd->aqd", score_grad, k_sel, preferred_element_type=jnp.float32
    ).astype(jnp.bfloat16)
    onehot = (
        tile_ids[:, :, None] == jnp.arange(k_all.shape[0], dtype=jnp.int32)[None, None, :]
    ).astype(jnp.float32)
    key_slots = jnp.einsum("aqnk,aqd->ankd", score_grad, q_tile, preferred_element_type=jnp.float32)
    value_slots = jnp.einsum(
        "aqnk,aqd->ankd", weights_low, g_tile, preferred_element_type=jnp.float32
    )
    key_sums = jnp.einsum("anj,ankd->jkd", onehot, key_slots, precision=lax.Precision.HIGHEST)
    value_sums = jnp.einsum("anj,ankd->jkd", onehot, value_slots, precision=lax.Precision.HIGHEST)
    return (attended, query_grad, key_sums, value_sums)


def body(query, key_in, value, grad_out, pattern, live):
    members = lax.axis_size("head")
    heads = HEADS // members
    scale = HEAD_DIM ** (-0.5)
    queries, keys, values, out_grads = (
        lax.all_to_all(query, "head", split_axis=1, concat_axis=0, tiled=True),
        lax.all_to_all(key_in, "head", split_axis=1, concat_axis=0, tiled=True),
        lax.all_to_all(value, "head", split_axis=1, concat_axis=0, tiled=True),
        lax.all_to_all(grad_out, "head", split_axis=1, concat_axis=0, tiled=True),
    )
    tile_size = queries.shape[0] // members
    margin = members * tile_size
    seq_index = lax.axis_index("seq")
    first = seq_index * members
    extended = extended_2(jnp.stack([keys, values]), (("seq", 1),), margin)
    rows = lax.dynamic_slice_in_dim(pattern, first, members, 0)
    alive_rows = lax.dynamic_slice_in_dim(live, first, members, 0)
    tile_ids = rows - first + members
    alive = alive_rows > 0
    q_heads = head_split(queries, members, heads)
    g_heads = head_split(out_grads, members, heads)
    k_heads = head_split(extended[0], 3 * members, heads)
    v_heads = head_split(extended[1], 3 * members, heads)

    def with_partials(operands):
        return forward_head(
            operands[0], operands[1], operands[2], operands[3], tile_ids, alive, scale
        )

    attended, query_grad, key_sums, value_sums = lax.map(
        with_partials, (q_heads, g_heads, k_heads, v_heads)
    )
    grads = jnp.stack([head_join(key_sums), head_join(value_sums)])
    from_above = shifted(grads[:, :margin].astype(jnp.bfloat16), "seq", -1).astype(jnp.float32)
    from_below = shifted(grads[:, 2 * margin :].astype(jnp.bfloat16), "seq", 1).astype(jnp.float32)
    owned = grads[:, margin : 2 * margin] + from_above + from_below
    key_own = owned[0]
    value_own = owned[1]
    result = (
        lax.all_to_all(head_join(attended), "head", split_axis=0, concat_axis=1, tiled=True),
        lax.all_to_all(head_join(query_grad), "head", split_axis=0, concat_axis=1, tiled=True),
        lax.all_to_all(
            key_own.astype(jnp.bfloat16), "head", split_axis=0, concat_axis=1, tiled=True
        ),
        lax.all_to_all(
            value_own.astype(jnp.bfloat16), "head", split_axis=0, concat_axis=1, tiled=True
        ),
    )
    return (result[0], result[1], result[2], result[3])


def solution(mesh):
    placed = (
        P(("groups", "seq", "head"), None),
        P(("groups", "seq", "head"), None),
        P(("groups", "seq", "head"), None),
        P(("groups", "seq", "head"), None),
        P(),
        P(),
    )
    return jax.shard_map(
        body,
        mesh=mesh,
        in_specs=placed,
        out_specs=(
            P(("groups", "seq", "head"), None),
            P(("groups", "seq", "head"), None),
            P(("groups", "seq", "head"), None),
            P(("groups", "seq", "head"), None),
        ),
        check_vma=False,
    )
```

profile of v0, /device:TPU:0, one launch (start us, length us, event | category | flops | bytes accessed | tf_op | source)
XLA Modules:
  0.0 322.3 jit_solution(741371311791878829)
XLA Ops:
  3.0 4.2 %all-to-all-start.1 = ((bf16[256,4,384]{0,2,1:T(8,128)(2,1)}), bf16[256,4,384]{0,2,1:T(8,128)(2,1)S(1)}, u32[]{:S(2)}, u32[]{:S(2)}) async-start(bf16[256,4,384]{0,2,1:T(8,128)(2,1)} %bitcast.30), calls=%async_computation.1 | async-start | bytes 1572864 | tf_op jit(solution)/shard_map/all_to_all | solution.py:82
  8.4 10.5 %all-to-all-done.1 = bf16[256,4,384]{0,2,1:T(8,128)(2,1)S(1)} async-done(((bf16[256,4,384]{0,2,1:T(8,128)(2,1)}), bf16[256,4,384]{0,2,1:T(8,128)(2,1)S(1)}, u32[]{:S(2)}, u32[]{:S(2)}) %all-to-all-start.1) | async-done | bytes 786464 | tf_op jit(solution)/shard_map/all_to_all | solution.py:82
  18.9 3.5 %all-to-all-start.2 = ((bf16[256,4,384]{0,2,1:T(8,128)(2,1)}), bf16[256,4,384]{0,2,1:T(8,128)(2,1)S(1)}, u32[]{:S(2)}, u32[]{:S(2)}) async-start(bf16[256,4,384]{0,2,1:T(8,128)(2,1)} %bitcast.33), calls=%async_computation.2 | async-start | bytes 1572864 | tf_op jit(solution)/shard_map/all_to_all | solution.py:83
  22.7 11.2 %all-to-all-done.2 = bf16[256,4,384]{0,2,1:T(8,128)(2,1)S(1)} async-done(((bf16[256,4,384]{0,2,1:T(8,128)(2,1)}), bf16[256,4,384]{0,2,1:T(8,128)(2,1)S(1)}, u32[]{:S(2)}, u32[]{:S(2)}) %all-to-all-start.2) | async-done | bytes 786464 | tf_op jit(solution)/shard_map/all_to_all | solution.py:83
  37.0 6.0 %collective-permute-start = (bf16[2,1024,384]{2,1,0:T(8,128)(2,1)}, bf16[2,1024,384]{2,1,0:T(8,128)(2,1)}, u32[]{:S(2)}, u32[]{:S(2)}) collective-permute-start(bf16[2,1024,384]{2,1,0:T(8,128)(2,1)} %pad_maximum_fusion.1), channel_id=1, source_target_pairs={{0,4},{4,8},{8,12},{1,5},{5,9},{9,13},{2,6},{6,10},{10,14},{3,7},{... | collective-permute-start | bytes 4718600 | tf_op jit(solution)/shard_map/ppermute | solution.py:18
  49.2 25.2 %collective-permute-done.1 = bf16[2,1024,384]{2,1,0:T(8,128)(2,1)} collective-permute-done((bf16[2,1024,384]{2,1,0:T(8,128)(2,1)}, bf16[2,1024,384]{2,1,0:T(8,128)(2,1)}, u32[]{:S(2)}, u32[]{:S(2)}) %collective-permute-start.1) | collective-permute-done | bytes 1572896 | tf_op jit(solution)/shard_map/ppermute | solution.py:20
  75.6 4.6 %pad_maximum_fusion = bf16[2,3072,384]{2,1,0:T(8,128)(2,1)} fusion(bf16[2,1024,384]{2,1,0:T(8,128)(2,1)} %collective-permute-done.1, bf16[1,1024,384]{2,1,0:T(8,128)(2,1)S(1)} %bitcast.172, bf16[1,1024,384]{2,1,0:T(8,128)(2,1)S(1)} %bitcast.170, bf16[2,1024,384]{2,1,0:T(8,128)(2,1)} %collective-permute-done), kind=kLoop, calls=%fused_computation.47 | loop fusion | flops 18874368 | bytes 9437184 | tf_op jit(solution)/shard_map/concatenate | solution.py:16
  80.2 4.2 %all-to-all-start.3 = ((bf16[256,4,384]{0,2,1:T(8,128)(2,1)}), bf16[256,4,384]{0,2,1:T(8,128)(2,1)}, u32[]{:S(2)}, u32[]{:S(2)}) async-start(bf16[256,4,384]{0,2,1:T(8,128)(2,1)} %bitcast.38), calls=%async_computation.3 | async-start | bytes 1572864 | tf_op jit(solution)/shard_map/all_to_all | solution.py:84
  84.4 4.3 %fusion.37 = (bf16[1,3072,384]{2,1,0:T(8,128)(2,1)}, bf16[1,3072,384]{2,1,0:T(8,128)(2,1)S(1)}) fusion(bf16[2,3072,384]{2,1,0:T(8,128)(2,1)} %pad_maximum_fusion), kind=kLoop, calls=%fused_computation.59 | loop fusion | bytes 9437184 | tf_op jit(solution)/shard_map/slice | solution.py:98
  88.7 4.3 %copy.49 = bf16[1,3072,384]{1,2,0:T(8,128)(2,1)} copy(bf16[1,3072,384]{2,1,0:T(8,128)(2,1)} %get-tuple-element.128) | data formatting | bytes 4718592 | tf_op jit(solution)/shard_map/slice | solution.py:98
  93.0 5.4 %reshape_squeeze.7 = bf16[12,256,3,128]{1,0,3,2:T(8,128)(2,1)} reshape(bf16[1,3072,384]{1,2,0:T(8,128)(2,1)} %copy.49) | data formatting | bytes 4718592 | tf_op jit(solution)/shard_map/reshape;squeeze | solution.py:35
  98.4 4.8 %copy.53 = bf16[3,12,256,128]{3,2,1,0:T(8,128)(2,1)} copy(bf16[3,12,256,128]{2,1,3,0:T(8,128)(2,1)} %bitcast.167) | data formatting | bytes 4718592 | tf_op jit(solution)/shard_map/while | solution.py:105
  105.9 5.4 %reshape_squeeze.6 = bf16[12,256,3,128]{1,0,3,2:T(8,128)(2,1)} reshape(bf16[1,3072,384]{1,2,0:T(8,128)(2,1)} %copy.47) | data formatting | bytes 4718592 | tf_op jit(solution)/shard_map/reshape;squeeze | solution.py:35
  111.3 4.8 %copy.52 = bf16[3,12,256,128]{3,2,1,0:T(8,128)(2,1)} copy(bf16[3,12,256,128]{2,1,3,0:T(8,128)(2,1)} %bitcast.168) | data formatting | bytes 4718592 | tf_op jit(solution)/shard_map/while | solution.py:105
  116.1 92.5 %while.16 = (s32[]{:T(128)}, bf16[3,4,256,128]{2,3,0,1:T(8,128)(2,1)}, bf16[3,4,256,128]{2,3,0,1:T(8,128)(2,1)}, f32[3,12,256,128]{3,1,2,0:T(8,128)}, f32[3,12,2...) while((s32[]{:T(128)}, ...), condition=%wide.region_4.5_spmd, body=%wide.region_0.4_spmd.sunk | while | flops 1345845504 | bytes 75555744 | solution.py:105
  138.9 4.0 %bitcast_dynamic-update-slice_fusion.4 = f32[3,12,256,128]{3,1,2,0:T(8,128)} fusion(f32[3,12,256,128]{3,1,2,0:T(8,128)} %get-tuple-element.228, s32[]{:T(128)S(6)} %copy.106, f32[4,3,256,128]{3,2,1,0:T(8,128)S(1)} %fusion.83, s32[4,3]{0,1:T(4,128)S(1)} %copy.96), kind=kOutput, calls=%fused_computation.10.clone.1 | convolution fusion | flops 56623248 | bytes 3670068 | tf_op jit(solution)/shard_map/while/body/eval_jaxpr/anj,ankd->jkd/dot_general | solution.py:71
  142.9 4.0 %bitcast_dynamic-update-slice_fusion.5 = f32[3,12,256,128]{3,1,2,0:T(8,128)} fusion(f32[3,12,256,128]{3,1,2,0:T(8,128)} %get-tuple-element.229, s32[]{:T(128)S(6)} %copy.106, f32[4,3,256,128]{3,2,1,0:T(8,128)S(1)} %copy-done.1, s32[4,3]{0,1:T(4,128)S(1)} %copy.96), kind=kOutput, calls=%fused_computation.9.clone.1 | convolution fusion | flops 56623248 | bytes 3670068 | tf_op jit(solution)/shard_map/while/body/eval_jaxpr/anj,ankd->jkd/dot_general | solution.py:72
  169.8 4.0 %bitcast_dynamic-update-slice_fusion.4 = f32[3,12,256,128]{3,1,2,0:T(8,128)} fusion(f32[3,12,256,128]{3,1,2,0:T(8,128)} %get-tuple-element.228, s32[]{:T(128)S(6)} %copy.106, f32[4,3,256,128]{3,2,1,0:T(8,128)S(1)} %fusion.83, s32[4,3]{0,1:T(4,128)S(1)} %copy.96), kind=kOutput, calls=%fused_computation.10.clone.1 | convolution fusion | flops 56623248 | bytes 3670068 | tf_op jit(solution)/shard_map/while/body/eval_jaxpr/anj,ankd->jkd/dot_general | solution.py:71
  173.8 4.0 %bitcast_dynamic-update-slice_fusion.5 = f32[3,12,256,128]{3,1,2,0:T(8,128)} fusion(f32[3,12,256,128]{3,1,2,0:T(8,128)} %get-tuple-element.229, s32[]{:T(128)S(6)} %copy.106, f32[4,3,256,128]{3,2,1,0:T(8,128)S(1)} %copy-done.1, s32[4,3]{0,1:T(4,128)S(1)} %copy.96), kind=kOutput, calls=%fused_computation.9.clone.1 | convolution fusion | flops 56623248 | bytes 3670068 | tf_op jit(solution)/shard_map/while/body/eval_jaxpr/anj,ankd->jkd/dot_general | solution.py:72
  200.6 4.0 %bitcast_dynamic-update-slice_fusion.4 = f32[3,12,256,128]{3,1,2,0:T(8,128)} fusion(f32[3,12,256,128]{3,1,2,0:T(8,128)} %get-tuple-element.228, s32[]{:T(128)S(6)} %copy.106, f32[4,3,256,128]{3,2,1,0:T(8,128)S(1)} %fusion.83, s32[4,3]{0,1:T(4,128)S(1)} %copy.96), kind=kOutput, calls=%fused_computation.10.clone.1 | convolution fusion | flops 56623248 | bytes 3670068 | tf_op jit(solution)/shard_map/while/body/eval_jaxpr/anj,ankd->jkd/dot_general | solution.py:71
  204.6 4.0 %bitcast_dynamic-update-slice_fusion.5 = f32[3,12,256,128]{3,1,2,0:T(8,128)} fusion(f32[3,12,256,128]{3,1,2,0:T(8,128)} %get-tuple-element.229, s32[]{:T(128)S(6)} %copy.106, f32[4,3,256,128]{3,2,1,0:T(8,128)S(1)} %copy-done.1, s32[4,3]{0,1:T(4,128)S(1)} %copy.96), kind=kOutput, calls=%fused_computation.9.clone.1 | convolution fusion | flops 56623248 | bytes 3670068 | tf_op jit(solution)/shard_map/while/body/eval_jaxpr/anj,ankd->jkd/dot_general | solution.py:72
  208.6 6.8 %copy.58 = f32[12,256,3,128]{1,0,3,2:T(8,128)} copy(f32[12,256,3,128]{3,0,1,2:T(8,128)} %bitcast.173) | data formatting | bytes 9437184 | tf_op jit(solution)/shard_map/transpose | solution.py:42
  215.4 6.9 %stack_reshape.7 = f32[1,3072,384]{1,2,0:T(8,128)} reshape(f32[12,256,3,128]{1,0,3,2:T(8,128)} %copy.58) | data formatting | bytes 9437184 | tf_op jit(solution)/shard_map/stack;reshape | solution.py:108
  222.3 6.7 %copy.57 = f32[12,256,3,128]{1,0,3,2:T(8,128)} copy(f32[12,256,3,128]{3,0,1,2:T(8,128)} %bitcast.174) | data formatting | bytes 9437184 | tf_op jit(solution)/shard_map/transpose | solution.py:42
  228.9 6.9 %stack_reshape.6 = f32[1,3072,384]{1,2,0:T(8,128)} reshape(f32[12,256,3,128]{1,0,3,2:T(8,128)} %copy.57) | data formatting | bytes 9437184 | tf_op jit(solution)/shard_map/stack;reshape | solution.py:108
  246.3 6.2 %collective-permute-start.3 = (bf16[2,1024,384]{1,2,0:T(8,128)(2,1)S(1)}, bf16[2,1024,384]{1,2,0:T(8,128)(2,1)}, u32[]{:S(2)}, u32[]{:S(2)}) collective-permute-start(bf16[2,1024,384]{1,2,0:T(8,128)(2,1)S(1)} %get-tuple-element.127), channel_id=1, source_target_pairs={{0,4},{4,8},{8,12},{1,5},{5,9},{9,13},{2,6},{6,10},{10,14},{3,7},{... | collective-permute-start | bytes 4718600 | tf_op jit(solution)/shard_map/ppermute | solution.py:30
  252.5 14.7 %all_to_all.134 = bf16[4,256,384]{1,2,0:T(8,128)(2,1)S(1)} all-to-all(bf16[4,256,384]{1,2,0:T(8,128)(2,1)S(1)} %bitcast.184), channel_id=1, replica_groups=mesh['groups'=2,'seq'=4,'head'=4] {'head'}, dimensions={0} | all-to-all | bytes 1572864 | tf_op jit(solution)/shard_map/all_to_all | solution.py:115
  270.7 14.0 %collective-permute-done.2 = bf16[2,1024,384]{1,2,0:T(8,128)(2,1)} collective-permute-done((bf16[2,1024,384]{1,2,0:T(8,128)(2,1)}, bf16[2,1024,384]{1,2,0:T(8,128)(2,1)}, u32[]{:S(2)}, u32[]{:S(2)}) %collective-permute-start.2) | collective-permute-done | bytes 1572896 | tf_op jit(solution)/shard_map/ppermute | solution.py:30
  285.6 3.7 %fusion.35 = bf16[2,1024,384]{1,2,0:T(8,128)(2,1)S(1)} fusion(f32[2,3072,384]{1,2,0:T(8,128)} %copy-done.2, bf16[2,1024,384]{1,2,0:T(8,128)(2,1)} %collective-permute-done.3, bf16[2,1024,384]{1,2,0:T(8,128)(2,1)} %collective-permute-done.2), kind=kLoop, calls=%fused_computation.50 | loop fusion | flops 3932160 | bytes 7864320 | tf_op jit(solution)/shard_map/convert.1
  290.6 3.5 %all-to-all-start.7 = ((bf16[4,256,384]{2,1,0:T(8,128)(2,1)}), bf16[4,256,384]{2,1,0:T(8,128)(2,1)S(1)}, u32[]{:S(2)}, u32[]{:S(2)}) async-start(bf16[4,256,384]{2,1,0:T(8,128)(2,1)} %bitcast.55), calls=%async_computation.7 | async-start | bytes 1572864 | tf_op jit(solution)/shard_map/all_to_all | solution.py:120
  295.2 10.5 %all-to-all-done.7 = bf16[4,256,384]{2,1,0:T(8,128)(2,1)S(1)} async-done(((bf16[4,256,384]{2,1,0:T(8,128)(2,1)}), bf16[4,256,384]{2,1,0:T(8,128)(2,1)S(1)}, u32[]{:S(2)}, u32[]{:S(2)}) %all-to-all-start.7) | async-done | bytes 786464 | tf_op jit(solution)/shard_map/all_to_all | solution.py:120
  312.9 7.9 %all-to-all-done.6 = bf16[4,256,384]{2,1,0:T(8,128)(2,1)S(1)} async-done(((bf16[4,256,384]{2,1,0:T(8,128)(2,1)}), bf16[4,256,384]{2,1,0:T(8,128)(2,1)S(1)}, u32[]{:S(2)}, u32[]{:S(2)}) %all-to-all-start.6) | async-done | bytes 786464 | tf_op jit(solution)/shard_map/all_to_all | solution.py:117
  (149 shorter events, 111.0 us)
Async XLA Ops:
  0.6 6.6 %copy-start.8 = (bf16[256,1536]{1,0:T(8,128)(2,1)S(1)}, bf16[256,1536]{1,0:T(8,128)(2,1)}, u32[]{:S(2)}) copy-start(bf16[256,1536]{1,0:T(8,128)(2,1)} %param.10) | copy-start | bytes 2359300
  3.0 15.9 %all-to-all-start.1 = ((bf16[256,4,384]{0,2,1:T(8,128)(2,1)}), bf16[256,4,384]{0,2,1:T(8,128)(2,1)S(1)}, u32[]{:S(2)}, u32[]{:S(2)}) async-start(bf16[256,4,384]{0,2,1:T(8,128)(2,1)} %bitcast.30), calls=%async_computation.1 | async-start | bytes 1572864 | tf_op jit(solution)/shard_map/all_to_all | solution.py:82
  18.9 15.1 %all-to-all-start.2 = ((bf16[256,4,384]{0,2,1:T(8,128)(2,1)}), bf16[256,4,384]{0,2,1:T(8,128)(2,1)S(1)}, u32[]{:S(2)}, u32[]{:S(2)}) async-start(bf16[256,4,384]{0,2,1:T(8,128)(2,1)} %bitcast.33), calls=%async_computation.2 | async-start | bytes 1572864 | tf_op jit(solution)/shard_map/all_to_all | solution.py:83
  22.7 20.3 %copy-start.9 = (bf16[256,1536]{1,0:T(8,128)(2,1)S(1)}, bf16[256,1536]{1,0:T(8,128)(2,1)}, u32[]{:S(2)}) copy-start(bf16[256,1536]{1,0:T(8,128)(2,1)} %param.8) | copy-start | bytes 2359300
  34.3 13.4 %copy-start.12 = (s32[16,3]{0,1:T(4,128)S(1)}, s32[16,3]{0,1:T(4,128)}, u32[]{:S(2)}) copy-start(s32[16,3]{0,1:T(4,128)} %param.12) | copy-start | bytes 580
  34.4 13.4 %copy-start.13 = (s32[16,3]{0,1:T(4,128)S(1)}, s32[16,3]{0,1:T(4,128)}, u32[]{:S(2)}) copy-start(s32[16,3]{0,1:T(4,128)} %param.13) | copy-start | bytes 580
  34.4 13.6 %copy-start.10 = (bf16[256,1536]{1,0:T(8,128)(2,1)S(1)}, bf16[256,1536]{1,0:T(8,128)(2,1)}, u32[]{:S(2)}) copy-start(bf16[256,1536]{1,0:T(8,128)(2,1)} %param.11) | copy-start | bytes 2359300
  35.7 38.7 %collective-permute-start.1 = (bf16[2,1024,384]{2,1,0:T(8,128)(2,1)}, bf16[2,1024,384]{2,1,0:T(8,128)(2,1)}, u32[]{:S(2)}, u32[]{:S(2)}) collective-permute-start(bf16[2,1024,384]{2,1,0:T(8,128)(2,1)} %pad_maximum_fusion.1), channel_id=1, source_target_pairs={{4,0},{8,4},{12,8},{5,1},{9,5},{13,9},{6,2},{10,6},{14,10},{7,3},{... | collective-permute-start | bytes 4718600 | tf_op jit(solution)/shard_map/ppermute | solution.py:20
  37.0 38.6 %collective-permute-start = (bf16[2,1024,384]{2,1,0:T(8,128)(2,1)}, bf16[2,1024,384]{2,1,0:T(8,128)(2,1)}, u32[]{:S(2)}, u32[]{:S(2)}) collective-permute-start(bf16[2,1024,384]{2,1,0:T(8,128)(2,1)} %pad_maximum_fusion.1), channel_id=1, source_target_pairs={{0,4},{4,8},{8,12},{1,5},{5,9},{9,13},{2,6},{6,10},{10,14},{3,7},{... | collective-permute-start | bytes 4718600 | tf_op jit(solution)/shard_map/ppermute | solution.py:18
  44.2 36.1 %all-to-all-start = ((bf16[256,4,384]{0,2,1:T(8,128)(2,1)}), bf16[256,4,384]{0,2,1:T(8,128)(2,1)S(1)}, u32[]{:S(2)}, u32[]{:S(2)}) async-start(bf16[256,4,384]{0,2,1:T(8,128)(2,1)} %bitcast.26), calls=%async_computation | async-start | bytes 1572864 | tf_op jit(solution)/shard_map/all_to_all | solution.py:81
  80.2 35.9 %all-to-all-start.3 = ((bf16[256,4,384]{0,2,1:T(8,128)(2,1)}), bf16[256,4,384]{0,2,1:T(8,128)(2,1)}, u32[]{:S(2)}, u32[]{:S(2)}) async-start(bf16[256,4,384]{0,2,1:T(8,128)(2,1)} %bitcast.38), calls=%async_computation.3 | async-start | bytes 1572864 | tf_op jit(solution)/shard_map/all_to_all | solution.py:84
  121.6 2.6 copy-start.3
  128.0 3.0 copy-start.4
  136.4 6.5 %copy-start.1 = (f32[4,3,256,128]{3,2,1,0:T(8,128)S(1)}, f32[4,3,256,128]{3,2,1,0:T(8,128)}, u32[]{:S(2)}) copy-start(f32[4,3,256,128]{3,2,1,0:T(8,128)} %fusion.84) | copy-start | bytes 4718596 | tf_op jit(solution)/shard_map/while
  142.9 4.0 %copy-start.7 = (bf16[3,4,256,128]{2,3,0,1:T(8,128)(2,1)S(1)}, bf16[3,4,256,128]{2,3,0,1:T(8,128)(2,1)}, u32[]{:S(2)}) copy-start(bf16[3,4,256,128]{2,3,0,1:T(8,128)(2,1)} %copy-done.6) | copy-start | bytes 2359300 | tf_op jit(solution)/shard_map/while
  152.5 2.6 copy-start.3
  158.8 3.0 copy-start.4
  163.9 1.1 copy-start
  167.3 6.5 %copy-start.1 = (f32[4,3,256,128]{3,2,1,0:T(8,128)S(1)}, f32[4,3,256,128]{3,2,1,0:T(8,128)}, u32[]{:S(2)}) copy-start(f32[4,3,256,128]{3,2,1,0:T(8,128)} %fusion.84) | copy-start | bytes 4718596 | tf_op jit(solution)/shard_map/while
  173.8 4.0 %copy-start.7 = (bf16[3,4,256,128]{2,3,0,1:T(8,128)(2,1)S(1)}, bf16[3,4,256,128]{2,3,0,1:T(8,128)(2,1)}, u32[]{:S(2)}) copy-start(bf16[3,4,256,128]{2,3,0,1:T(8,128)(2,1)} %copy-done.6) | copy-start | bytes 2359300 | tf_op jit(solution)/shard_map/while
  183.3 2.6 copy-start.3
  189.6 3.0 copy-start.4
  198.1 6.6 %copy-start.1 = (f32[4,3,256,128]{3,2,1,0:T(8,128)S(1)}, f32[4,3,256,128]{3,2,1,0:T(8,128)}, u32[]{:S(2)}) copy-start(f32[4,3,256,128]{3,2,1,0:T(8,128)} %fusion.84) | copy-start | bytes 4718596 | tf_op jit(solution)/shard_map/while
  204.6 4.0 %copy-start.7 = (bf16[3,4,256,128]{2,3,0,1:T(8,128)(2,1)S(1)}, bf16[3,4,256,128]{2,3,0,1:T(8,128)(2,1)}, u32[]{:S(2)}) copy-start(bf16[3,4,256,128]{2,3,0,1:T(8,128)(2,1)} %copy-done.6) | copy-start | bytes 2359300 | tf_op jit(solution)/shard_map/while
  235.8 3.8 %copy-start.5 = (f32[1,3072,384]{1,2,0:T(8,128)S(1)}, f32[1,3072,384]{1,2,0:T(8,128)}, u32[]{:S(2)}) copy-start(f32[1,3072,384]{1,2,0:T(8,128)} %stack_reshape.7) | copy-start | bytes 14155780
  239.9 3.7 %copy-start.2 = (f32[2,3072,384]{1,2,0:T(8,128)}, f32[2,3072,384]{1,2,0:T(8,128)S(1)}, u32[]{:S(2)}) copy-start(f32[2,3072,384]{1,2,0:T(8,128)S(1)} %constant_dynamic-update-slice_fusion.2) | copy-start | bytes 28311556
  243.6 8.9 %copy-start.11 = (bf16[3,4,256,128]{2,3,0,1:T(8,128)(2,1)S(1)}, bf16[3,4,256,128]{2,3,0,1:T(8,128)(2,1)}, u32[]{:S(2)}) copy-start(bf16[3,4,256,128]{2,3,0,1:T(8,128)(2,1)} %get-tuple-element.64) | copy-start | bytes 2359300
  245.0 39.7 %collective-permute-start.2 = (bf16[2,1024,384]{1,2,0:T(8,128)(2,1)}, bf16[2,1024,384]{1,2,0:T(8,128)(2,1)}, u32[]{:S(2)}, u32[]{:S(2)}) collective-permute-start(bf16[2,1024,384]{1,2,0:T(8,128)(2,1)} %get-tuple-element.126), channel_id=1, source_target_pairs={{4,0},{8,4},{12,8},{5,1},{9,5},{13,9},{6,2},{10,6},{14,10},{7,3},{... | collective-permute-start | bytes 4718600 | tf_op jit(solution)/shard_map/ppermute | solution.py:30
  246.3 39.3 %collective-permute-start.3 = (bf16[2,1024,384]{1,2,0:T(8,128)(2,1)S(1)}, bf16[2,1024,384]{1,2,0:T(8,128)(2,1)}, u32[]{:S(2)}, u32[]{:S(2)}) collective-permute-start(bf16[2,1024,384]{1,2,0:T(8,128)(2,1)S(1)} %get-tuple-element.127), channel_id=1, source_target_pairs={{0,4},{4,8},{8,12},{1,5},{5,9},{9,13},{2,6},{6,10},{10,14},{3,7},{... | collective-permute-start | bytes 4718600 | tf_op jit(solution)/shard_map/ppermute | solution.py:30
  267.2 23.4 %all-to-all-start.5 = ((bf16[4,256,384]{1,2,0:T(8,128)(2,1)}), bf16[4,256,384]{1,2,0:T(8,128)(2,1)S(1)}, u32[]{:S(2)}, u32[]{:S(2)}) async-start(bf16[4,256,384]{1,2,0:T(8,128)(2,1)} %bitcast.183), calls=%async_computation.5 | async-start | bytes 1572864 | tf_op jit(solution)/shard_map/all_to_all | solution.py:116
  290.6 15.1 %all-to-all-start.7 = ((bf16[4,256,384]{2,1,0:T(8,128)(2,1)}), bf16[4,256,384]{2,1,0:T(8,128)(2,1)S(1)}, u32[]{:S(2)}, u32[]{:S(2)}) async-start(bf16[4,256,384]{2,1,0:T(8,128)(2,1)} %bitcast.55), calls=%async_computation.7 | async-start | bytes 1572864 | tf_op jit(solution)/shard_map/all_to_all | solution.py:120
  305.7 15.1 %all-to-all-start.6 = ((bf16[4,256,384]{2,1,0:T(8,128)(2,1)}), bf16[4,256,384]{2,1,0:T(8,128)(2,1)S(1)}, u32[]{:S(2)}, u32[]{:S(2)}) async-start(bf16[4,256,384]{2,1,0:T(8,128)(2,1)} %bitcast.52), calls=%async_computation.6 | async-start | bytes 1572864 | tf_op jit(solution)/shard_map/all_to_all | solution.py:117
  (5 other events, 5.0 us)
where the time goes:
time: 326 us; the launch traced here: 322 us
  local copies, waits for them, and re-layouts  111 us (34%)
  waiting for transfers between devices  81.4 us (25%)
  matrix products  57.4 us (18%)
  starting transfers between devices  40.6 us (12%)
  other arithmetic  15.9 us (5%)
  blocking collectives  14.7 us (5%)
    ppermute x1, waiting for transfers between devices, extended_2(): lax.ppermute(head, axis, [((i + 1) % count, i) for i in range(ends)])  25.2 us
    unnamed x27, local copies, waits for them, and re-layouts  17.3 us
    ppermute x2, waiting for transfers between devices, shifted(): lax.ppermute(value, axis, [(source, source + steps) for source in range(i...  14.9 us
    all_to_all x1, blocking collectives, body(): lax.all_to_all(head_join(attended), 'head', split_axis=0, concat_axis=1,...  14.7 us
    another operation x3, local copies, waits for them, and re-layouts, body(): grads = jnp.stack([head_join(key_sums), head_join(value_sums)])  14 us
    transpose x2, local copies, waits for them, and re-layouts, head_join(): blocks.transpose(1, 2, 0, 3).reshape(tiles * tile_size, heads * head_size)  13.5 us
    dynamic_update_slice x12, local copies, waits for them, and re-layouts, body(): lax.map(with_partials, (q_heads, g_heads, k_heads, v_heads))  13 us
    dot_general x3, matrix products, forward_head(): jnp.einsum('anj,ankd->jkd', onehot, value_slots, precision=lax.Precision....  12.1 us
  transfers between devices with their start and end apart: 11, of which 8 were waited for; matrix products, arithmetic and copies ran while one was open for 16% of the time, Pallas kernels for 0%

commit v1 on v0

v1 whole, which is shorter than its diff:
```python
import functools

import jax
import jax.numpy as jnp
from jax import lax
from jax.experimental import pallas as pl
from jax.experimental.pallas import tpu as pltpu
from jax.sharding import PartitionSpec as P

HEADS = 12
HEAD_DIM = 128
SLOTS = 3
SCALE = HEAD_DIM ** (-0.5)
BF = jnp.bfloat16
F32 = jnp.float32
PARAMS = pltpu.CompilerParams(vmem_limit_bytes=40 * 1024 * 1024)


def dot_nt(a, b):
    return lax.dot_general(a, b, (((1,), (1,)), ((), ())), preferred_element_type=F32)


def dot_nn(a, b):
    return lax.dot_general(a, b, (((1,), (0,)), ((), ())), preferred_element_type=F32)


def dot_tn(a, b):
    return lax.dot_general(a, b, (((0,), (0,)), ((), ())), preferred_element_type=F32)


def full(shape):
    return pl.BlockSpec(shape, lambda i, *_: (0,) * len(shape))


def cost(flops, nbytes):
    return pl.CostEstimate(flops=flops, bytes_accessed=nbytes, transcendentals=0)


class Plan:
    def __init__(self, members, tile):
        self.members = members
        self.tile = tile
        self.per = HEADS // members
        self.piece = (2, tile, HEAD_DIM)
        self.layer = (members, 2, tile, HEAD_DIM)

    def column(self, partner, chunk):
        per = self.per
        return pl.BlockSpec(
            (self.tile, HEAD_DIM), lambda i, pos: (0, (pos[1] ^ partner) * per + chunk)
        )


def pack(plan, pos, first, second):
    where = [(c, r) for c in range(plan.per) for r in range(1, plan.members)]
    count = len(where)

    def kernel(pos_ref, *refs):
        for n in range(count):
            refs[2 * count + n][0] = refs[2 * n][...]
            refs[2 * count + n][1] = refs[2 * n + 1][...]

    specs, operands = [], []
    for c, r in where:
        specs += [plan.column(r, c)] * 2
        operands += [first, second]
    out = pl.pallas_call(
        kernel,
        out_shape=[jax.ShapeDtypeStruct(plan.piece, BF)] * count,
        grid_spec=pltpu.PrefetchScalarGridSpec(
            num_scalar_prefetch=1,
            grid=(1,),
            in_specs=specs,
            out_specs=[full(plan.piece)] * count,
        ),
        compiler_params=PARAMS,
        cost_estimate=cost(0, 4 * count * plan.tile * HEAD_DIM * 2),
        name="pack",
    )(pos, *operands)
    return {key: out[n] for n, key in enumerate(where)}


def layer_of(plan, pos, chunk, key_in, value, pieces):
    def kernel(pos_ref, k_ref, v_ref, *refs):
        out = refs[-1]
        out[0, 0] = k_ref[...]
        out[0, 1] = v_ref[...]
        for r in range(1, plan.members):
            out[r] = refs[r - 1][...]

    return pl.pallas_call(
        kernel,
        out_shape=jax.ShapeDtypeStruct(plan.layer, BF),
        grid_spec=pltpu.PrefetchScalarGridSpec(
            num_scalar_prefetch=1,
            grid=(1,),
            in_specs=[plan.column(0, chunk)] * 2 + [full(plan.piece)] * (plan.members - 1),
            out_specs=full(plan.layer),
        ),
        compiler_params=PARAMS,
        cost_estimate=cost(0, 4 * plan.members * plan.tile * HEAD_DIM * 2),
        name="layer",
    )(pos, key_in, value, *pieces)


def attend(plan, pos, table, chunk, query, grad_out, qg, own, below, above):
    members, tile = plan.members, plan.tile

    def kernel(pos_ref, table_ref, q_ref, g_ref, *refs):
        qg_refs = refs[: members - 1]
        own_ref, below_ref, above_ref = refs[members - 1 : members + 2]
        odq_refs = refs[members + 2 : 2 * members + 2]
        down_ref, up_ref, sum_ref = refs[2 * members + 2 : 2 * members + 5]
        kv, qgs, odq, acc = refs[2 * members + 5 :]
        kv[pl.ds(0, members)] = below_ref[...]
        kv[pl.ds(members, members)] = own_ref[...]
        kv[pl.ds(2 * members, members)] = above_ref[...]
        qgs[0, 0] = q_ref[...]
        qgs[0, 1] = g_ref[...]
        for r in range(1, members):
            qgs[r] = qg_refs[r - 1][...]
        acc[...] = jnp.zeros_like(acc)
        seq, me = pos_ref[0], pos_ref[1]

        def place(tile_id):
            rel = tile_id - (seq - 1) * members
            return (rel // members) * members + ((rel % members) ^ me)

        def work(r, places):
            q, g = qgs[r, 0], qgs[r, 1]
            scores = [dot_nt(kv[p, 0], q) * SCALE for p in places]
            peak = functools.reduce(
                jnp.maximum, [jnp.max(s, axis=0, keepdims=True) for s in scores]
            )
            expo = [jnp.exp(s - peak) for s in scores]
            wgrad = [dot_nt(kv[p, 1], g) for p in places]
            total = sum(jnp.sum(e, axis=0, keepdims=True) for e in expo)
            mixed = sum(jnp.sum(e * w, axis=0, keepdims=True) for e, w in zip(expo, wgrad))
            inv = 1.0 / total
            delta = mixed * inv
            att_t, dq_t = 0.0, 0.0
            for p, e, w in zip(places, expo, wgrad):
                weight = e * inv
                low = weight.astype(BF)
                sgrad = (weight * (w - delta) * SCALE).astype(BF)
                att_t = att_t + dot_tn(kv[p, 1], low)
                dq_t = dq_t + dot_tn(kv[p, 0], sgrad)
                acc[p, 0] += dot_nn(sgrad, q)
                acc[p, 1] += dot_nn(low, g)
            odq[r, 0] = att_t.T.astype(BF)
            odq[r, 1] = dq_t.T.astype(BF)

        def step(r, carry):
            row = (seq * members + (r ^ me)) * 2 * SLOTS
            live = [table_ref[row + SLOTS + n] > 0 for n in range(SLOTS)]
            spots = [place(table_ref[row + n]) for n in range(SLOTS)]
            second = jnp.where(live[1], spots[1], spots[2])

            @pl.when(live[1] & live[2])
            def _():
                work(r, [spots[0], spots[1], spots[2]])

            @pl.when(live[1] ^ live[2])
            def _():
                work(r, [spots[0], second])

            @pl.when(jnp.logical_not(live[1] | live[2]))
            def _():
                work(r, [spots[0]])

            return carry

        lax.fori_loop(0, members, step, 0)
        for r in range(members):
            odq_refs[r][...] = odq[r]
        down_ref[...] = acc[pl.ds(0, members)].astype(BF)
        sum_ref[...] = acc[pl.ds(members, members)]
        up_ref[...] = acc[pl.ds(2 * members, members)].astype(BF)

    rows = members * tile * HEAD_DIM
    out = pl.pallas_call(
        kernel,
        out_shape=[jax.ShapeDtypeStruct(plan.piece, BF)] * members
        + [jax.ShapeDtypeStruct(plan.layer, BF)] * 2
        + [jax.ShapeDtypeStruct(plan.layer, F32)],
        grid_spec=pltpu.PrefetchScalarGridSpec(
            num_scalar_prefetch=2,
            grid=(1,),
            in_specs=[
                pl.BlockSpec((tile, HEAD_DIM), lambda i, p, t: (0, p[1] * plan.per + chunk))
            ]
            * 2
            + [full(plan.piece)] * (members - 1)
            + [full(plan.layer)] * 3,
            out_specs=[full(plan.piece)] * members + [full(plan.layer)] * 3,
            scratch_shapes=[
                pltpu.VMEM((3 * members, 2, tile, HEAD_DIM), BF),
                pltpu.VMEM(plan.layer, BF),
                pltpu.VMEM(plan.layer, BF),
                pltpu.VMEM((3 * members, 2, tile, HEAD_DIM), F32),
            ],
        ),
        compiler_params=PARAMS,
        cost_estimate=cost(12 * SLOTS * rows * tile * 2, 40 * rows),
        name="attend",
    )(pos, table, query, grad_out, *qg, own, below, above)
    return out[:members], out[members], out[members + 1], out[members + 2]


def owned(plan, total, from_above, from_below):
    members = plan.members

    def kernel(total_ref, above_ref, below_ref, *outs):
        for r in range(members):
            outs[r][...] = (
                total_ref[r] + above_ref[r].astype(F32) + below_ref[r].astype(F32)
            ).astype(BF)

    return pl.pallas_call(
        kernel,
        out_shape=[jax.ShapeDtypeStruct(plan.piece, BF)] * members,
        grid=(1,),
        in_specs=[full(plan.layer)] * 3,
        out_specs=[full(plan.piece)] * members,
        compiler_params=PARAMS,
        cost_estimate=cost(0, 20 * members * plan.tile * HEAD_DIM),
        name="owned",
    )(total, from_above, from_below)


def unpack(plan, pos, pieces):
    members, per = plan.members, plan.per
    where = [(c, r) for c in range(per) for r in range(members)]

    def kernel(pos_ref, *refs):
        first, second = refs[-2:]
        for n, (c, r) in enumerate(where):
            column = ((pos_ref[1] ^ r) * per + c) * HEAD_DIM
            span = pl.ds(pl.multiple_of(column, HEAD_DIM), HEAD_DIM)
            first[:, span] = refs[n][0]
            second[:, span] = refs[n][1]

    shape = (plan.tile, HEADS * HEAD_DIM)
    return pl.pallas_call(
        kernel,
        out_shape=[jax.ShapeDtypeStruct(shape, BF)] * 2,
        grid_spec=pltpu.PrefetchScalarGridSpec(
            num_scalar_prefetch=1,
            grid=(1,),
            in_specs=[full(plan.piece)] * len(where),
            out_specs=[full(shape)] * 2,
        ),
        compiler_params=PARAMS,
        cost_estimate=cost(0, 8 * plan.tile * HEADS * HEAD_DIM),
        name="unpack",
    )(pos, *[pieces[key] for key in where])


def swap(value, members, r):
    return lax.ppermute(value, "head", [(i, i ^ r) for i in range(members)])


def shifted(value, steps):
    count = lax.axis_size("seq")
    return lax.ppermute(
        value, "seq", [(i, i + steps) for i in range(count) if 0 <= i + steps < count]
    )


def body(query, key_in, value, grad_out, pattern, live):
    members = lax.axis_size("head")
    plan = Plan(members, query.shape[0])
    partners = range(1, members)
    chunks = range(plan.per)
    pos = jnp.stack([lax.axis_index("seq"), lax.axis_index("head")]).astype(jnp.int32)
    table = jnp.concatenate([pattern, live], axis=1).reshape(-1)

    kv_out = pack(plan, pos, key_in, value)
    qg_out = pack(plan, pos, query, grad_out)
    own, below, above, qg = {}, {}, {}, {}
    for c in chunks:
        got = [swap(kv_out[c, r], members, r) for r in partners]
        own[c] = layer_of(plan, pos, c, key_in, value, got)
        below[c] = shifted(own[c], 1)
        above[c] = shifted(own[c], -1)
        qg[c] = [swap(qg_out[c, r], members, r) for r in partners]
    odq, dkv = {}, {}
    for c in chunks:
        mine, down, up, total = attend(
            plan, pos, table, c, query, grad_out, qg[c], own[c], below[c], above[c]
        )
        odq[c, 0] = mine[0]
        for r in partners:
            odq[c, r] = swap(mine[r], members, r)
        sums = owned(plan, total, shifted(down, -1), shifted(up, 1))
        dkv[c, 0] = sums[0]
        for r in partners:
            dkv[c, r] = swap(sums[r], members, r)
    attended, query_grad = unpack(plan, pos, odq)
    key_grad, value_grad = unpack(plan, pos, dkv)
    return attended, query_grad, key_grad, value_grad


def solution(mesh):
    split = P(("groups", "seq", "head"), None)
    return jax.shard_map(
        body,
        mesh=mesh,
        in_specs=(split, split, split, split, P(), P()),
        out_specs=(split, split, split, split),
        check_vma=False,
    )
```

time: 326 us -> 130 us (0.40)
  local copies, waits for them, and re-layouts: 111 us -> 10.3 us
  matrix products: 57.4 us -> 0 us
  waiting for transfers between devices: 81.4 us -> 28.8 us
  Pallas kernels: 0 us -> 25.1 us
  starting transfers between devices: 40.6 us -> 64 us
  other arithmetic: 15.9 us -> 0.08 us
  blocking collectives: 14.7 us -> 0 us
    dot_general x24 -> x0, matrix products: 57.4 us -> none  [the longest x3 12.1 us: forward_head(): jnp.einsum('anj,ankd->jkd', onehot, value_slots, precision=lax.Precision....]
    ppermute x4 -> x48, starting transfers between devices: 14.7 us -> 64 us  [the longest x12 37.7 us: shifted(): lax.ppermute(value, 'seq', [(i, i + steps) for i in range(count) if 0 <=...]
    all_to_all x7 -> x0, waiting for transfers between devices: 40.1 us -> none  [the longest x1 11.2 us: body(): lax.all_to_all(value, 'head', split_axis=1, concat_axis=0, tiled=True)]
    all_to_all x7 -> x0, starting transfers between devices: 25.9 us -> none  [the longest x1 4.21 us: body(): lax.all_to_all(key_in, 'head', split_axis=1, concat_axis=0, tiled=True)]
    another operation x8 -> x0, local copies, waits for them, and re-layouts: 25.1 us -> none  [the longest x3 14 us: body(): grads = jnp.stack([head_join(key_sums), head_join(value_sums)])]
    pallas_call x0 -> x13, Pallas kernels: none -> 25.1 us  [the longest x3 17.2 us: attend(): pl.pallas_call(kernel, out_shape=[jax.ShapeDtypeStruct(plan.piece, BF)] *...]
    slice x7 -> x0, local copies, waits for them, and re-layouts: 15.1 us -> none  [the longest x2 8.53 us: body(): v_heads = head_split(extended[1], 3 * members, heads)]
    all_to_all x1 -> x0, blocking collectives: 14.7 us -> none  [body(): lax.all_to_all(head_join(attended), 'head', split_axis=0, concat_axis=1,...]
  transfers between devices with their start and end apart: 11 -> 48, of which waited for: 8 -> 14; matrix products, arithmetic and copies ran while one was open for 16% -> 0% of each run, Pallas kernels for 0% -> 17%
where the time goes in v1:
time: 130 us; the launch traced here: 129 us
  starting transfers between devices  64 us (49%)
  waiting for transfers between devices  28.8 us (22%)
  Pallas kernels  25.1 us (19%)
  local copies, waits for them, and re-layouts  10.3 us (8%)
    ppermute x12, starting transfers between devices, shifted(): lax.ppermute(value, 'seq', [(i, i + steps) for i in range(count) if 0 <=...  37.7 us
    ppermute x36, starting transfers between devices, swap(): return lax.ppermute(value, 'head', [(i, i ^ r) for i in range(members)])  26.3 us
    ppermute x36, waiting for transfers between devices, swap(): return lax.ppermute(value, 'head', [(i, i ^ r) for i in range(members)])  23.6 us
    pallas_call x3, Pallas kernels, attend(): pl.pallas_call(kernel, out_shape=[jax.ShapeDtypeStruct(plan.piece, BF)] *...  17.2 us
    unnamed x44, local copies, waits for them, and re-layouts  10.1 us
    ppermute x12, waiting for transfers between devices, shifted(): lax.ppermute(value, 'seq', [(i, i + steps) for i in range(count) if 0 <=...  5.18 us
    pallas_call x2, Pallas kernels, unpack(): pl.pallas_call(kernel, out_shape=[jax.ShapeDtypeStruct(shape, BF)] * 2, g...  3.9 us
  transfers between devices with their start and end apart: 48, of which 14 were waited for; matrix products, arithmetic and copies ran while one was open for 0% of the time, Pallas kernels for 17%

profile of v1, /device:TPU:0, one launch (start us, length us, event | category | flops | bytes accessed | tf_op | source)
XLA Modules:
  0.0 129.3 jit_solution(10832484965793591104)
XLA Ops:
  4.3 2.6 %collective-permute-start.26 = (bf16[2,256,128]{2,1,0:T(8,128)(2,1)S(1)}, bf16[2,256,128]{2,1,0:T(8,128)(2,1)S(1)}, u32[]{:S(2)}, u32[]{:S(2)}) collective-permute-start(bf16[2,256,128]{2,1,0:T(8,128)(2,1)S(1)} %get-tuple-element.83), channel_id=1, source_target_pairs={{0,2},{1,3},{2,0},{3,1},{4,6},{5,7},{6,4},{7,5},{8,10},{9,11},{10,... | collective-permute-start | bytes 393224 | tf_op jit(solution)/shard_map/ppermute | solution.py:260
  8.0 1.9 %collective-permute-start.23 = (bf16[2,256,128]{2,1,0:T(8,128)(2,1)S(1)}, bf16[2,256,128]{2,1,0:T(8,128)(2,1)S(1)}, u32[]{:S(2)}, u32[]{:S(2)}) collective-permute-start(bf16[2,256,128]{2,1,0:T(8,128)(2,1)S(1)} %get-tuple-element.80), channel_id=1, source_target_pairs={{0,2},{1,3},{2,0},{3,1},{4,6},{5,7},{6,4},{7,5},{8,10},{9,11},{10,... | collective-permute-start | bytes 393224 | tf_op jit(solution)/shard_map/ppermute | solution.py:260
  11.2 2.3 %collective-permute-done.27.refs_2_ = bf16[2,256,128]{2,1,0:T(8,128)(2,1)S(1)} collective-permute-done((bf16[2,256,128]{2,1,0:T(8,128)(2,1)S(1)}, bf16[2,256,128]{2,1,0:T(8,128)(2,1)S(1)}, u32[]{:S(2)}, u32[]{:S(2)}) %collective-permute-start.27) | collective-permute-done | bytes 131104 | tf_op jit(solution)/shard_map/ppermute | solution.py:260
  13.5 1.6 %collective-permute-start.15 = (bf16[2,256,128]{2,1,0:T(8,128)(2,1)S(1)}, bf16[2,256,128]{2,1,0:T(8,128)(2,1)S(1)}, u32[]{:S(2)}, u32[]{:S(2)}) collective-permute-start(bf16[2,256,128]{2,1,0:T(8,128)(2,1)S(1)} %get-tuple-element.73), channel_id=1, source_target_pairs={{0,2},{1,3},{2,0},{3,1},{4,6},{5,7},{6,4},{7,5},{8,10},{9,11},{10,... | collective-permute-start | bytes 393224 | tf_op jit(solution)/shard_map/ppermute | solution.py:260
  16.4 3.5 %collective-permute-start.28 = (bf16[4,2,256,128]{3,2,1,0:T(8,128)(2,1)S(1)}, bf16[4,2,256,128]{3,2,1,0:T(8,128)(2,1)S(1)}, u32[]{:S(2)}, u32[]{:S(2)}) collective-permute-start(bf16[4,2,256,128]{3,2,1,0:T(8,128)(2,1)S(1)} %layer.5.refs_3_), channel_id=1, source_target_pairs={{0,4},{4,8},{8,12},{1,5},{5,9},{9,13},{2,6},{6,10},{10,14},{3,7},{... | collective-permute-start | bytes 1572872 | tf_op jit(solution)/shard_map/ppermute | solution.py:265
  23.1 1.6 %collective-permute-start.12 = (bf16[2,256,128]{2,1,0:T(8,128)(2,1)S(1)}, bf16[2,256,128]{2,1,0:T(8,128)(2,1)S(1)}, u32[]{:S(2)}, u32[]{:S(2)}) collective-permute-start(bf16[2,256,128]{2,1,0:T(8,128)(2,1)S(1)} %get-tuple-element.70), channel_id=1, source_target_pairs={{0,2},{1,3},{2,0},{3,1},{4,6},{5,7},{6,4},{7,5},{8,10},{9,11},{10,... | collective-permute-start | bytes 393224 | tf_op jit(solution)/shard_map/ppermute | solution.py:260
  24.7 1.3 %collective-permute-done.16.refs_2_ = bf16[2,256,128]{2,1,0:T(8,128)(2,1)S(1)} collective-permute-done((bf16[2,256,128]{2,1,0:T(8,128)(2,1)S(1)}, bf16[2,256,128]{2,1,0:T(8,128)(2,1)S(1)}, u32[]{:S(2)}, u32[]{:S(2)}) %collective-permute-start.16) | collective-permute-done | bytes 131104 | tf_op jit(solution)/shard_map/ppermute | solution.py:260
  26.7 2.4 %collective-permute-done.12.refs_1_ = bf16[2,256,128]{2,1,0:T(8,128)(2,1)S(1)} collective-permute-done((bf16[2,256,128]{2,1,0:T(8,128)(2,1)S(1)}, bf16[2,256,128]{2,1,0:T(8,128)(2,1)S(1)}, u32[]{:S(2)}, u32[]{:S(2)}) %collective-permute-start.12) | collective-permute-done | bytes 131104 | tf_op jit(solution)/shard_map/ppermute | solution.py:260
  30.6 5.0 %collective-permute-start.17 = (bf16[4,2,256,128]{3,2,1,0:T(8,128)(2,1)S(1)}, bf16[4,2,256,128]{3,2,1,0:T(8,128)(2,1)}, u32[]{:S(2)}, u32[]{:S(2)}) collective-permute-start(bf16[4,2,256,128]{3,2,1,0:T(8,128)(2,1)S(1)} %layer.4.refs_3_), channel_id=1, source_target_pairs={{0,4},{4,8},{8,12},{1,5},{5,9},{9,13},{2,6},{6,10},{10,14},{3,7},{... | collective-permute-start | bytes 1572872 | tf_op jit(solution)/shard_map/ppermute | solution.py:265
  36.9 1.5 %collective-permute-start.13 = (bf16[2,256,128]{2,1,0:T(8,128)(2,1)S(1)}, bf16[2,256,128]{2,1,0:T(8,128)(2,1)S(1)}, u32[]{:S(2)}, u32[]{:S(2)}) collective-permute-start(bf16[2,256,128]{2,1,0:T(8,128)(2,1)S(1)} %get-tuple-element.71), channel_id=1, source_target_pairs={{0,3},{1,2},{2,1},{3,0},{4,7},{5,6},{6,5},{7,4},{8,11},{9,10},{10,... | collective-permute-start | bytes 393224 | tf_op jit(solution)/shard_map/ppermute | solution.py:260
  39.0 3.2 %collective-permute-done.13.refs_2_ = bf16[2,256,128]{2,1,0:T(8,128)(2,1)S(1)} collective-permute-done((bf16[2,256,128]{2,1,0:T(8,128)(2,1)S(1)}, bf16[2,256,128]{2,1,0:T(8,128)(2,1)S(1)}, u32[]{:S(2)}, u32[]{:S(2)}) %collective-permute-start.13) | collective-permute-done | bytes 131104 | tf_op jit(solution)/shard_map/ppermute | solution.py:260
  42.8 4.9 %collective-permute-start.6 = (bf16[4,2,256,128]{3,2,1,0:T(8,128)(2,1)S(1)}, bf16[4,2,256,128]{3,2,1,0:T(8,128)(2,1)}, u32[]{:S(2)}, u32[]{:S(2)}) collective-permute-start(bf16[4,2,256,128]{3,2,1,0:T(8,128)(2,1)S(1)} %layer.3.refs_3_), channel_id=1, source_target_pairs={{0,4},{4,8},{8,12},{1,5},{5,9},{9,13},{2,6},{6,10},{10,14},{3,7},{... | collective-permute-start | bytes 1572872 | tf_op jit(solution)/shard_map/ppermute | solution.py:265
  50.1 1.5 %collective-permute-start = (bf16[2,256,128]{2,1,0:T(8,128)(2,1)S(1)}, bf16[2,256,128]{2,1,0:T(8,128)(2,1)S(1)}, u32[]{:S(2)}, u32[]{:S(2)}) collective-permute-start(bf16[2,256,128]{2,1,0:T(8,128)(2,1)S(1)} %get-tuple-element.59), channel_id=1, source_target_pairs={{0,1},{1,0},{2,3},{3,2},{4,5},{5,4},{6,7},{7,6},{8,9},{9,8},{10,11... | collective-permute-start | bytes 393224 | tf_op jit(solution)/shard_map/ppermute | solution.py:260
  55.3 5.6 %attend.5 = (bf16[2,256,128]{2,1,0:T(8,128)(2,1)S(1)}, bf16[2,256,128]{2,1,0:T(8,128)(2,1)S(1)}, bf16[2,256,128]{2,1,0:T(8,128)(2,1)S(1)}, bf16[2,256,128]{2,1,0...) custom-call(s32[2]{0:T(128)S(1)} %pad_add_fusion.1.pos_ref, ...), custom_call_target="tpu_custom_call" | custom-call | flops 2415919104 | bytes 5242880 | tf_op jit(solution)/shard_map/attend/pallas_call | solution.py:181
  61.0 1.4 %collective-permute-start.1 = (bf16[2,256,128]{2,1,0:T(8,128)(2,1)S(1)}, bf16[2,256,128]{2,1,0:T(8,128)(2,1)S(1)}, u32[]{:S(2)}, u32[]{:S(2)}) collective-permute-start(bf16[2,256,128]{2,1,0:T(8,128)(2,1)S(1)} %get-tuple-element.60), channel_id=1, source_target_pairs={{0,2},{1,3},{2,0},{3,1},{4,6},{5,7},{6,4},{7,5},{8,10},{9,11},{10,... | collective-permute-start | bytes 393224 | tf_op jit(solution)/shard_map/ppermute | solution.py:260
  63.9 5.8 %attend.4 = (bf16[2,256,128]{2,1,0:T(8,128)(2,1)S(1)}, bf16[2,256,128]{2,1,0:T(8,128)(2,1)S(1)}, bf16[2,256,128]{2,1,0:T(8,128)(2,1)S(1)}, bf16[2,256,128]{2,1,0...) custom-call(s32[2]{0:T(128)S(1)} %pad_add_fusion.1.pos_ref, ...), custom_call_target="tpu_custom_call" | custom-call | flops 2415919104 | bytes 5242880 | tf_op jit(solution)/shard_map/attend/pallas_call | solution.py:181
  70.4 1.4 %collective-permute-start.31 = (bf16[2,256,128]{2,1,0:T(8,128)(2,1)S(1)}, bf16[2,256,128]{2,1,0:T(8,128)(2,1)S(1)}, u32[]{:S(2)}, u32[]{:S(2)}) collective-permute-start(bf16[2,256,128]{2,1,0:T(8,128)(2,1)S(1)} %get-tuple-element.87), channel_id=1, source_target_pairs={{0,2},{1,3},{2,0},{3,1},{4,6},{5,7},{6,4},{7,5},{8,10},{9,11},{10,... | collective-permute-start | bytes 393224 | tf_op jit(solution)/shard_map/ppermute | solution.py:260
  72.5 6.4 %collective-permute-start.44 = (bf16[4,2,256,128]{3,2,1,0:T(8,128)(2,1)S(1)}, bf16[4,2,256,128]{3,2,1,0:T(8,128)(2,1)S(1)}, u32[]{:S(2)}, u32[]{:S(2)}) collective-permute-start(bf16[4,2,256,128]{3,2,1,0:T(8,128)(2,1)S(1)} %get-tuple-element.107), channel_id=1, source_target_pairs={{0,4},{4,8},{8,12},{1,5},{5,9},{9,13},{2,6},{6,10},{10,14},{3,7},{... | collective-permute-start | bytes 1572872 | tf_op jit(solution)/shard_map/ppermute | solution.py:265
  80.2 5.0 %collective-permute-start.39 = (bf16[4,2,256,128]{3,2,1,0:T(8,128)(2,1)S(1)}, bf16[4,2,256,128]{3,2,1,0:T(8,128)(2,1)S(1)}, u32[]{:S(2)}, u32[]{:S(2)}) collective-permute-start(bf16[4,2,256,128]{3,2,1,0:T(8,128)(2,1)S(1)} %get-tuple-element.100), channel_id=1, source_target_pairs={{0,4},{4,8},{8,12},{1,5},{5,9},{9,13},{2,6},{6,10},{10,14},{3,7},{... | collective-permute-start | bytes 1572872 | tf_op jit(solution)/shard_map/ppermute | solution.py:265
  85.2 1.7 %collective-permute-start.20 = (bf16[2,256,128]{2,1,0:T(8,128)(2,1)S(1)}, bf16[2,256,128]{2,1,0:T(8,128)(2,1)S(1)}, u32[]{:S(2)}, u32[]{:S(2)}) collective-permute-start(bf16[2,256,128]{2,1,0:T(8,128)(2,1)S(1)} %get-tuple-element.77), channel_id=1, source_target_pairs={{0,2},{1,3},{2,0},{3,1},{4,6},{5,7},{6,4},{7,5},{8,10},{9,11},{10,... | collective-permute-start | bytes 393224 | tf_op jit(solution)/shard_map/ppermute | solution.py:260
  86.9 5.8 %attend.3 = (bf16[2,256,128]{2,1,0:T(8,128)(2,1)S(1)}, bf16[2,256,128]{2,1,0:T(8,128)(2,1)S(1)}, bf16[2,256,128]{2,1,0:T(8,128)(2,1)S(1)}, bf16[2,256,128]{2,1,0...) custom-call(s32[2]{0:T(128)S(1)} %pad_add_fusion.1.pos_ref, ...), custom_call_target="tpu_custom_call" | custom-call | flops 2415919104 | bytes 5242880 | tf_op jit(solution)/shard_map/attend/pallas_call | solution.py:181
  94.0 5.3 %collective-permute-start.34 = (bf16[4,2,256,128]{3,2,1,0:T(8,128)(2,1)S(1)}, bf16[4,2,256,128]{3,2,1,0:T(8,128)(2,1)S(1)}, u32[]{:S(2)}, u32[]{:S(2)}) collective-permute-start(bf16[4,2,256,128]{3,2,1,0:T(8,128)(2,1)S(1)} %get-tuple-element.93), channel_id=1, source_target_pairs={{0,4},{4,8},{8,12},{1,5},{5,9},{9,13},{2,6},{6,10},{10,14},{3,7},{... | collective-permute-start | bytes 1572872 | tf_op jit(solution)/shard_map/ppermute | solution.py:265
  99.4 1.7 %collective-permute-start.10 = (bf16[2,256,128]{2,1,0:T(8,128)(2,1)S(1)}, bf16[2,256,128]{2,1,0:T(8,128)(2,1)S(1)}, u32[]{:S(2)}, u32[]{:S(2)}) collective-permute-start(bf16[2,256,128]{2,1,0:T(8,128)(2,1)S(1)} %get-tuple-element.68), channel_id=1, source_target_pairs={{0,3},{1,2},{2,1},{3,0},{4,7},{5,6},{6,5},{7,4},{8,11},{9,10},{10,... | collective-permute-start | bytes 393224 | tf_op jit(solution)/shard_map/ppermute | solution.py:260
  102.7 2.3 %collective-permute-done.21.refs_7_ = bf16[2,256,128]{2,1,0:T(8,128)(2,1)S(1)} collective-permute-done((bf16[2,256,128]{2,1,0:T(8,128)(2,1)S(1)}, bf16[2,256,128]{2,1,0:T(8,128)(2,1)S(1)}, u32[]{:S(2)}, u32[]{:S(2)}) %collective-permute-start.21) | collective-permute-done | bytes 131104 | tf_op jit(solution)/shard_map/ppermute | solution.py:260
  105.4 2.2 %collective-permute-done.10.refs_3_ = bf16[2,256,128]{2,1,0:T(8,128)(2,1)S(1)} collective-permute-done((bf16[2,256,128]{2,1,0:T(8,128)(2,1)S(1)}, bf16[2,256,128]{2,1,0:T(8,128)(2,1)S(1)}, u32[]{:S(2)}, u32[]{:S(2)}) %collective-permute-start.10) | collective-permute-done | bytes 131104 | tf_op jit(solution)/shard_map/ppermute | solution.py:260
  109.5 3.3 %collective-permute-done.34.below_ref = bf16[4,2,256,128]{3,2,1,0:T(8,128)(2,1)S(1)} collective-permute-done((bf16[4,2,256,128]{3,2,1,0:T(8,128)(2,1)S(1)}, bf16[4,2,256,128]{3,2,1,0:T(8,128)(2,1)S(1)}, u32[]{:S(2)}, u32[]{:S(2)}) %collective-permute-start.34) | collective-permute-done | bytes 524320 | tf_op jit(solution)/shard_map/ppermute | solution.py:265
  113.0 1.6 %collective-permute-start.41 = (bf16[2,256,128]{2,1,0:T(8,128)(2,1)S(1)}, bf16[2,256,128]{2,1,0:T(8,128)(2,1)S(1)}, u32[]{:S(2)}, u32[]{:S(2)}) collective-permute-start(bf16[2,256,128]{2,1,0:T(8,128)(2,1)S(1)} %get-tuple-element.103), channel_id=1, source_target_pairs={{0,2},{1,3},{2,0},{3,1},{4,6},{5,7},{6,4},{7,5},{8,10},{9,11},{10,... | collective-permute-start | bytes 393224 | tf_op jit(solution)/shard_map/ppermute | solution.py:260
  117.7 2.0 %unpack.2 = (bf16[256,1536]{1,0:T(8,128)(2,1)}, bf16[256,1536]{1,0:T(8,128)(2,1)}) custom-call(s32[2]{0:T(128)S(1)} %pad_add_fusion.1.pos_ref, bf16[2,256,128]{2,1,0:T(8,128)(2,1)S(1)} %get-tuple-element.65.refs_0_, bf16[2,256,128]{2,1,0:T(8,128)(2,1)S(1)} %collective-permute-done.8.refs_1_, bf16[2,256,128]{2,1,0:T(8,128)(2,1)S(1)} %collective-permute-done.9.refs_2_, ...), custom_call_target="tpu_custom_call" | custom-call | bytes 3145728 | tf_op jit(solution)/shard_map/unpack/pallas_call | solution.py:244
  119.6 2.1 %collective-permute-done.42.refs_7_ = bf16[2,256,128]{2,1,0:T(8,128)(2,1)S(1)} collective-permute-done((bf16[2,256,128]{2,1,0:T(8,128)(2,1)S(1)}, bf16[2,256,128]{2,1,0:T(8,128)(2,1)S(1)}, u32[]{:S(2)}, u32[]{:S(2)}) %collective-permute-start.42) | collective-permute-done | bytes 131104 | tf_op jit(solution)/shard_map/ppermute | solution.py:260
  121.7 3.3 %collective-permute-done.36.refs_2_ = bf16[2,256,128]{2,1,0:T(8,128)(2,1)S(1)} collective-permute-done((bf16[2,256,128]{2,1,0:T(8,128)(2,1)S(1)}, bf16[2,256,128]{2,1,0:T(8,128)(2,1)S(1)}, u32[]{:S(2)}, u32[]{:S(2)}) %collective-permute-start.36) | collective-permute-done | bytes 131104 | tf_op jit(solution)/shard_map/ppermute | solution.py:260
  125.0 2.3 %collective-permute-done.37.refs_3_ = bf16[2,256,128]{2,1,0:T(8,128)(2,1)S(1)} collective-permute-done((bf16[2,256,128]{2,1,0:T(8,128)(2,1)S(1)}, bf16[2,256,128]{2,1,0:T(8,128)(2,1)S(1)}, u32[]{:S(2)}, u32[]{:S(2)}) %collective-permute-start.37) | collective-permute-done | bytes 131104 | tf_op jit(solution)/shard_map/ppermute | solution.py:260
  127.4 2.0 %unpack.3 = (bf16[256,1536]{1,0:T(8,128)(2,1)}, bf16[256,1536]{1,0:T(8,128)(2,1)}) custom-call(s32[2]{0:T(128)S(1)} %pad_add_fusion.1.pos_ref, bf16[2,256,128]{2,1,0:T(8,128)(2,1)S(1)} %get-tuple-element.94.refs_0_, bf16[2,256,128]{2,1,0:T(8,128)(2,1)S(1)} %collective-permute-done.35.refs_1_, bf16[2,256,128]{2,1,0:T(8,128)(2,1)S(1)} %collective-permute-done.36.refs_2_, ...), custom_call_target="tpu_custom_call" | custom-call | bytes 3145728 | tf_op jit(solution)/shard_map/unpack/pallas_call | solution.py:244
  (125 shorter events, 33.9 us)
Async XLA Ops:
  7.8 7.9 %collective-permute-start.22 = (bf16[2,256,128]{2,1,0:T(8,128)(2,1)S(1)}, bf16[2,256,128]{2,1,0:T(8,128)(2,1)S(1)}, u32[]{:S(2)}, u32[]{:S(2)}) collective-permute-start(bf16[2,256,128]{2,1,0:T(8,128)(2,1)S(1)} %get-tuple-element.79), channel_id=1, source_target_pairs={{0,1},{1,0},{2,3},{3,2},{4,5},{5,4},{6,7},{7,6},{8,9},{9,8},{10,11... | collective-permute-start | bytes 393224 | tf_op jit(solution)/shard_map/ppermute | solution.py:260
  8.0 11.8 %collective-permute-start.23 = (bf16[2,256,128]{2,1,0:T(8,128)(2,1)S(1)}, bf16[2,256,128]{2,1,0:T(8,128)(2,1)S(1)}, u32[]{:S(2)}, u32[]{:S(2)}) collective-permute-start(bf16[2,256,128]{2,1,0:T(8,128)(2,1)S(1)} %get-tuple-element.80), channel_id=1, source_target_pairs={{0,2},{1,3},{2,0},{3,1},{4,6},{5,7},{6,4},{7,5},{8,10},{9,11},{10,... | collective-permute-start | bytes 393224 | tf_op jit(solution)/shard_map/ppermute | solution.py:260
  10.0 10.9 %collective-permute-start.24 = (bf16[2,256,128]{2,1,0:T(8,128)(2,1)S(1)}, bf16[2,256,128]{2,1,0:T(8,128)(2,1)S(1)}, u32[]{:S(2)}, u32[]{:S(2)}) collective-permute-start(bf16[2,256,128]{2,1,0:T(8,128)(2,1)S(1)} %get-tuple-element.81), channel_id=1, source_target_pairs={{0,3},{1,2},{2,1},{3,0},{4,7},{5,6},{6,5},{7,4},{8,11},{9,10},{10,... | collective-permute-start | bytes 393224 | tf_op jit(solution)/shard_map/ppermute | solution.py:260
  11.2 10.6 %collective-permute-start.14 = (bf16[2,256,128]{2,1,0:T(8,128)(2,1)S(1)}, bf16[2,256,128]{2,1,0:T(8,128)(2,1)S(1)}, u32[]{:S(2)}, u32[]{:S(2)}) collective-permute-start(bf16[2,256,128]{2,1,0:T(8,128)(2,1)S(1)} %get-tuple-element.72), channel_id=1, source_target_pairs={{0,1},{1,0},{2,3},{3,2},{4,5},{5,4},{6,7},{7,6},{8,9},{9,8},{10,11... | collective-permute-start | bytes 393224 | tf_op jit(solution)/shard_map/ppermute | solution.py:260
  13.5 9.6 %collective-permute-start.15 = (bf16[2,256,128]{2,1,0:T(8,128)(2,1)S(1)}, bf16[2,256,128]{2,1,0:T(8,128)(2,1)S(1)}, u32[]{:S(2)}, u32[]{:S(2)}) collective-permute-start(bf16[2,256,128]{2,1,0:T(8,128)(2,1)S(1)} %get-tuple-element.73), channel_id=1, source_target_pairs={{0,2},{1,3},{2,0},{3,1},{4,6},{5,7},{6,4},{7,5},{8,10},{9,11},{10,... | collective-permute-start | bytes 393224 | tf_op jit(solution)/shard_map/ppermute | solution.py:260
  16.4 31.4 %collective-permute-start.28 = (bf16[4,2,256,128]{3,2,1,0:T(8,128)(2,1)S(1)}, bf16[4,2,256,128]{3,2,1,0:T(8,128)(2,1)S(1)}, u32[]{:S(2)}, u32[]{:S(2)}) collective-permute-start(bf16[4,2,256,128]{3,2,1,0:T(8,128)(2,1)S(1)} %layer.5.refs_3_), channel_id=1, source_target_pairs={{0,4},{4,8},{8,12},{1,5},{5,9},{9,13},{2,6},{6,10},{10,14},{3,7},{... | collective-permute-start | bytes 1572872 | tf_op jit(solution)/shard_map/ppermute | solution.py:265
  21.8 28.2 %collective-permute-start.29 = (bf16[4,2,256,128]{3,2,1,0:T(8,128)(2,1)S(1)}, bf16[4,2,256,128]{3,2,1,0:T(8,128)(2,1)}, u32[]{:S(2)}, u32[]{:S(2)}) collective-permute-start(bf16[4,2,256,128]{3,2,1,0:T(8,128)(2,1)S(1)} %layer.5.refs_3_), channel_id=1, source_target_pairs={{4,0},{8,4},{12,8},{5,1},{9,5},{13,9},{6,2},{10,6},{14,10},{7,3},{... | collective-permute-start | bytes 1572872 | tf_op jit(solution)/shard_map/ppermute | solution.py:265
  26.5 9.1 %collective-permute-start.4 = (bf16[2,256,128]{2,1,0:T(8,128)(2,1)S(1)}, bf16[2,256,128]{2,1,0:T(8,128)(2,1)S(1)}, u32[]{:S(2)}, u32[]{:S(2)}) collective-permute-start(bf16[2,256,128]{2,1,0:T(8,128)(2,1)S(1)} %get-tuple-element.63), channel_id=1, source_target_pairs={{0,2},{1,3},{2,0},{3,1},{4,6},{5,7},{6,4},{7,5},{8,10},{9,11},{10,... | collective-permute-start | bytes 393224 | tf_op jit(solution)/shard_map/ppermute | solution.py:260
  29.8 7.1 %collective-permute-start.5 = (bf16[2,256,128]{2,1,0:T(8,128)(2,1)S(1)}, bf16[2,256,128]{2,1,0:T(8,128)(2,1)S(1)}, u32[]{:S(2)}, u32[]{:S(2)}) collective-permute-start(bf16[2,256,128]{2,1,0:T(8,128)(2,1)S(1)} %get-tuple-element.64), channel_id=1, source_target_pairs={{0,3},{1,2},{2,1},{3,0},{4,7},{5,6},{6,5},{7,4},{8,11},{9,10},{10,... | collective-permute-start | bytes 393224 | tf_op jit(solution)/shard_map/ppermute | solution.py:260
  30.6 31.8 %collective-permute-start.17 = (bf16[4,2,256,128]{3,2,1,0:T(8,128)(2,1)S(1)}, bf16[4,2,256,128]{3,2,1,0:T(8,128)(2,1)}, u32[]{:S(2)}, u32[]{:S(2)}) collective-permute-start(bf16[4,2,256,128]{3,2,1,0:T(8,128)(2,1)S(1)} %layer.4.refs_3_), channel_id=1, source_target_pairs={{0,4},{4,8},{8,12},{1,5},{5,9},{9,13},{2,6},{6,10},{10,14},{3,7},{... | collective-permute-start | bytes 1572872 | tf_op jit(solution)/shard_map/ppermute | solution.py:265
  35.6 27.0 %collective-permute-start.18 = (bf16[4,2,256,128]{3,2,1,0:T(8,128)(2,1)S(1)}, bf16[4,2,256,128]{3,2,1,0:T(8,128)(2,1)}, u32[]{:S(2)}, u32[]{:S(2)}) collective-permute-start(bf16[4,2,256,128]{3,2,1,0:T(8,128)(2,1)S(1)} %layer.4.refs_3_), channel_id=1, source_target_pairs={{4,0},{8,4},{12,8},{5,1},{9,5},{13,9},{6,2},{10,6},{14,10},{7,3},{... | collective-permute-start | bytes 1572872 | tf_op jit(solution)/shard_map/ppermute | solution.py:265
  42.8 28.9 %collective-permute-start.6 = (bf16[4,2,256,128]{3,2,1,0:T(8,128)(2,1)S(1)}, bf16[4,2,256,128]{3,2,1,0:T(8,128)(2,1)}, u32[]{:S(2)}, u32[]{:S(2)}) collective-permute-start(bf16[4,2,256,128]{3,2,1,0:T(8,128)(2,1)S(1)} %layer.3.refs_3_), channel_id=1, source_target_pairs={{0,4},{4,8},{8,12},{1,5},{5,9},{9,13},{2,6},{6,10},{10,14},{3,7},{... | collective-permute-start | bytes 1572872 | tf_op jit(solution)/shard_map/ppermute | solution.py:265
  48.5 23.3 %collective-permute-start.7 = (bf16[4,2,256,128]{3,2,1,0:T(8,128)(2,1)S(1)}, bf16[4,2,256,128]{3,2,1,0:T(8,128)(2,1)}, u32[]{:S(2)}, u32[]{:S(2)}) collective-permute-start(bf16[4,2,256,128]{3,2,1,0:T(8,128)(2,1)S(1)} %layer.3.refs_3_), channel_id=1, source_target_pairs={{4,0},{8,4},{12,8},{5,1},{9,5},{13,9},{6,2},{10,6},{14,10},{7,3},{... | collective-permute-start | bytes 1572872 | tf_op jit(solution)/shard_map/ppermute | solution.py:265
  50.1 10.9 %collective-permute-start = (bf16[2,256,128]{2,1,0:T(8,128)(2,1)S(1)}, bf16[2,256,128]{2,1,0:T(8,128)(2,1)S(1)}, u32[]{:S(2)}, u32[]{:S(2)}) collective-permute-start(bf16[2,256,128]{2,1,0:T(8,128)(2,1)S(1)} %get-tuple-element.59), channel_id=1, source_target_pairs={{0,1},{1,0},{2,3},{3,2},{4,5},{5,4},{6,7},{7,6},{8,9},{9,8},{10,11... | collective-permute-start | bytes 393224 | tf_op jit(solution)/shard_map/ppermute | solution.py:260
  61.0 8.7 %collective-permute-start.1 = (bf16[2,256,128]{2,1,0:T(8,128)(2,1)S(1)}, bf16[2,256,128]{2,1,0:T(8,128)(2,1)S(1)}, u32[]{:S(2)}, u32[]{:S(2)}) collective-permute-start(bf16[2,256,128]{2,1,0:T(8,128)(2,1)S(1)} %get-tuple-element.60), channel_id=1, source_target_pairs={{0,2},{1,3},{2,0},{3,1},{4,6},{5,7},{6,4},{7,5},{8,10},{9,11},{10,... | collective-permute-start | bytes 393224 | tf_op jit(solution)/shard_map/ppermute | solution.py:260
  62.4 8.0 %collective-permute-start.2 = (bf16[2,256,128]{2,1,0:T(8,128)(2,1)S(1)}, bf16[2,256,128]{2,1,0:T(8,128)(2,1)S(1)}, u32[]{:S(2)}, u32[]{:S(2)}) collective-permute-start(bf16[2,256,128]{2,1,0:T(8,128)(2,1)S(1)} %get-tuple-element.61), channel_id=1, source_target_pairs={{0,3},{1,2},{2,1},{3,0},{4,7},{5,6},{6,5},{7,4},{8,11},{9,10},{10,... | collective-permute-start | bytes 393224 | tf_op jit(solution)/shard_map/ppermute | solution.py:260
  62.6 31.4 %collective-permute-start.43 = (bf16[4,2,256,128]{3,2,1,0:T(8,128)(2,1)S(1)}, bf16[4,2,256,128]{3,2,1,0:T(8,128)(2,1)S(1)}, u32[]{:S(2)}, u32[]{:S(2)}) collective-permute-start(bf16[4,2,256,128]{3,2,1,0:T(8,128)(2,1)S(1)} %get-tuple-element.106), channel_id=1, source_target_pairs={{4,0},{8,4},{12,8},{5,1},{9,5},{13,9},{6,2},{10,6},{14,10},{7,3},{... | collective-permute-start | bytes 1572872 | tf_op jit(solution)/shard_map/ppermute | solution.py:265
  70.4 8.5 %collective-permute-start.31 = (bf16[2,256,128]{2,1,0:T(8,128)(2,1)S(1)}, bf16[2,256,128]{2,1,0:T(8,128)(2,1)S(1)}, u32[]{:S(2)}, u32[]{:S(2)}) collective-permute-start(bf16[2,256,128]{2,1,0:T(8,128)(2,1)S(1)} %get-tuple-element.87), channel_id=1, source_target_pairs={{0,2},{1,3},{2,0},{3,1},{4,6},{5,7},{6,4},{7,5},{8,10},{9,11},{10,... | collective-permute-start | bytes 393224 | tf_op jit(solution)/shard_map/ppermute | solution.py:260
  71.8 8.5 %collective-permute-start.32 = (bf16[2,256,128]{2,1,0:T(8,128)(2,1)S(1)}, bf16[2,256,128]{2,1,0:T(8,128)(2,1)S(1)}, u32[]{:S(2)}, u32[]{:S(2)}) collective-permute-start(bf16[2,256,128]{2,1,0:T(8,128)(2,1)S(1)} %get-tuple-element.88), channel_id=1, source_target_pairs={{0,3},{1,2},{2,1},{3,0},{4,7},{5,6},{6,5},{7,4},{8,11},{9,10},{10,... | collective-permute-start | bytes 393224 | tf_op jit(solution)/shard_map/ppermute | solution.py:260
  71.8 13.4 %collective-permute-start.19 = (bf16[2,256,128]{2,1,0:T(8,128)(2,1)S(1)}, bf16[2,256,128]{2,1,0:T(8,128)(2,1)S(1)}, u32[]{:S(2)}, u32[]{:S(2)}) collective-permute-start(bf16[2,256,128]{2,1,0:T(8,128)(2,1)S(1)} %get-tuple-element.76), channel_id=1, source_target_pairs={{0,1},{1,0},{2,3},{3,2},{4,5},{5,4},{6,7},{7,6},{8,9},{9,8},{10,11... | collective-permute-start | bytes 393224 | tf_op jit(solution)/shard_map/ppermute | solution.py:260
  72.5 26.8 %collective-permute-start.44 = (bf16[4,2,256,128]{3,2,1,0:T(8,128)(2,1)S(1)}, bf16[4,2,256,128]{3,2,1,0:T(8,128)(2,1)S(1)}, u32[]{:S(2)}, u32[]{:S(2)}) collective-permute-start(bf16[4,2,256,128]{3,2,1,0:T(8,128)(2,1)S(1)} %get-tuple-element.107), channel_id=1, source_target_pairs={{0,4},{4,8},{8,12},{1,5},{5,9},{9,13},{2,6},{6,10},{10,14},{3,7},{... | collective-permute-start | bytes 1572872 | tf_op jit(solution)/shard_map/ppermute | solution.py:265
  78.9 20.5 %collective-permute-start.38 = (bf16[4,2,256,128]{3,2,1,0:T(8,128)(2,1)S(1)}, bf16[4,2,256,128]{3,2,1,0:T(8,128)(2,1)S(1)}, u32[]{:S(2)}, u32[]{:S(2)}) collective-permute-start(bf16[4,2,256,128]{3,2,1,0:T(8,128)(2,1)S(1)} %get-tuple-element.99), channel_id=1, source_target_pairs={{4,0},{8,4},{12,8},{5,1},{9,5},{13,9},{6,2},{10,6},{14,10},{7,3},{... | collective-permute-start | bytes 1572872 | tf_op jit(solution)/shard_map/ppermute | solution.py:265
  80.2 22.2 %collective-permute-start.39 = (bf16[4,2,256,128]{3,2,1,0:T(8,128)(2,1)S(1)}, bf16[4,2,256,128]{3,2,1,0:T(8,128)(2,1)S(1)}, u32[]{:S(2)}, u32[]{:S(2)}) collective-permute-start(bf16[4,2,256,128]{3,2,1,0:T(8,128)(2,1)S(1)} %get-tuple-element.100), channel_id=1, source_target_pairs={{0,4},{4,8},{8,12},{1,5},{5,9},{9,13},{2,6},{6,10},{10,14},{3,7},{... | collective-permute-start | bytes 1572872 | tf_op jit(solution)/shard_map/ppermute | solution.py:265
  85.2 7.5 %collective-permute-start.20 = (bf16[2,256,128]{2,1,0:T(8,128)(2,1)S(1)}, bf16[2,256,128]{2,1,0:T(8,128)(2,1)S(1)}, u32[]{:S(2)}, u32[]{:S(2)}) collective-permute-start(bf16[2,256,128]{2,1,0:T(8,128)(2,1)S(1)} %get-tuple-element.77), channel_id=1, source_target_pairs={{0,2},{1,3},{2,0},{3,1},{4,6},{5,7},{6,4},{7,5},{8,10},{9,11},{10,... | collective-permute-start | bytes 393224 | tf_op jit(solution)/shard_map/ppermute | solution.py:260
  92.7 16.4 %collective-permute-start.33 = (bf16[4,2,256,128]{3,2,1,0:T(8,128)(2,1)S(1)}, bf16[4,2,256,128]{3,2,1,0:T(8,128)(2,1)S(1)}, u32[]{:S(2)}, u32[]{:S(2)}) collective-permute-start(bf16[4,2,256,128]{3,2,1,0:T(8,128)(2,1)S(1)} %get-tuple-element.92), channel_id=1, source_target_pairs={{4,0},{8,4},{12,8},{5,1},{9,5},{13,9},{6,2},{10,6},{14,10},{7,3},{... | collective-permute-start | bytes 1572872 | tf_op jit(solution)/shard_map/ppermute | solution.py:265
  94.0 18.7 %collective-permute-start.34 = (bf16[4,2,256,128]{3,2,1,0:T(8,128)(2,1)S(1)}, bf16[4,2,256,128]{3,2,1,0:T(8,128)(2,1)S(1)}, u32[]{:S(2)}, u32[]{:S(2)}) collective-permute-start(bf16[4,2,256,128]{3,2,1,0:T(8,128)(2,1)S(1)} %get-tuple-element.93), channel_id=1, source_target_pairs={{0,4},{4,8},{8,12},{1,5},{5,9},{9,13},{2,6},{6,10},{10,14},{3,7},{... | collective-permute-start | bytes 1572872 | tf_op jit(solution)/shard_map/ppermute | solution.py:265
  99.4 8.2 %collective-permute-start.10 = (bf16[2,256,128]{2,1,0:T(8,128)(2,1)S(1)}, bf16[2,256,128]{2,1,0:T(8,128)(2,1)S(1)}, u32[]{:S(2)}, u32[]{:S(2)}) collective-permute-start(bf16[2,256,128]{2,1,0:T(8,128)(2,1)S(1)} %get-tuple-element.68), channel_id=1, source_target_pairs={{0,3},{1,2},{2,1},{3,0},{4,7},{5,6},{6,5},{7,4},{8,11},{9,10},{10,... | collective-permute-start | bytes 393224 | tf_op jit(solution)/shard_map/ppermute | solution.py:260
  105.1 7.9 %collective-permute-start.9 = (bf16[2,256,128]{2,1,0:T(8,128)(2,1)S(1)}, bf16[2,256,128]{2,1,0:T(8,128)(2,1)S(1)}, u32[]{:S(2)}, u32[]{:S(2)}) collective-permute-start(bf16[2,256,128]{2,1,0:T(8,128)(2,1)S(1)} %get-tuple-element.67), channel_id=1, source_target_pairs={{0,2},{1,3},{2,0},{3,1},{4,6},{5,7},{6,4},{7,5},{8,10},{9,11},{10,... | collective-permute-start | bytes 393224 | tf_op jit(solution)/shard_map/ppermute | solution.py:260
  107.6 7.3 %collective-permute-start.46 = (bf16[2,256,128]{2,1,0:T(8,128)(2,1)S(1)}, bf16[2,256,128]{2,1,0:T(8,128)(2,1)S(1)}, u32[]{:S(2)}, u32[]{:S(2)}) collective-permute-start(bf16[2,256,128]{2,1,0:T(8,128)(2,1)S(1)} %get-tuple-element.110), channel_id=1, source_target_pairs={{0,2},{1,3},{2,0},{3,1},{4,6},{5,7},{6,4},{7,5},{8,10},{9,11},{10,... | collective-permute-start | bytes 393224 | tf_op jit(solution)/shard_map/ppermute | solution.py:260
  114.6 7.1 %collective-permute-start.42 = (bf16[2,256,128]{2,1,0:T(8,128)(2,1)S(1)}, bf16[2,256,128]{2,1,0:T(8,128)(2,1)S(1)}, u32[]{:S(2)}, u32[]{:S(2)}) collective-permute-start(bf16[2,256,128]{2,1,0:T(8,128)(2,1)S(1)} %get-tuple-element.104), channel_id=1, source_target_pairs={{0,3},{1,2},{2,1},{3,0},{4,7},{5,6},{6,5},{7,4},{8,11},{9,10},{10,... | collective-permute-start | bytes 393224 | tf_op jit(solution)/shard_map/ppermute | solution.py:260
  116.0 9.1 %collective-permute-start.36 = (bf16[2,256,128]{2,1,0:T(8,128)(2,1)S(1)}, bf16[2,256,128]{2,1,0:T(8,128)(2,1)S(1)}, u32[]{:S(2)}, u32[]{:S(2)}) collective-permute-start(bf16[2,256,128]{2,1,0:T(8,128)(2,1)S(1)} %get-tuple-element.96), channel_id=1, source_target_pairs={{0,2},{1,3},{2,0},{3,1},{4,6},{5,7},{6,4},{7,5},{8,10},{9,11},{10,... | collective-permute-start | bytes 393224 | tf_op jit(solution)/shard_map/ppermute | solution.py:260
  116.8 10.6 %collective-permute-start.37 = (bf16[2,256,128]{2,1,0:T(8,128)(2,1)S(1)}, bf16[2,256,128]{2,1,0:T(8,128)(2,1)S(1)}, u32[]{:S(2)}, u32[]{:S(2)}) collective-permute-start(bf16[2,256,128]{2,1,0:T(8,128)(2,1)S(1)} %get-tuple-element.97), channel_id=1, source_target_pairs={{0,3},{1,2},{2,1},{3,0},{4,7},{5,6},{6,5},{7,4},{8,11},{9,10},{10,... | collective-permute-start | bytes 393224 | tf_op jit(solution)/shard_map/ppermute | solution.py:260
  (38 other events, 181.3 us)

commit v2 on v1

v2 whole, which is shorter than its diff:
```python
import functools

import jax
import jax.numpy as jnp
from jax import lax
from jax.experimental import pallas as pl
from jax.experimental.pallas import tpu as pltpu
from jax.sharding import PartitionSpec as P

HEADS = 12
HEAD_DIM = 128
SLOTS = 3
SCALE = HEAD_DIM ** (-0.5)
BF = jnp.bfloat16
F32 = jnp.float32
MIB = 1024 * 1024
FULL = 60 * MIB
PARAMS = pltpu.CompilerParams(vmem_limit_bytes=20 * MIB)
ANYWHERE = pl.BlockSpec(memory_space=pl.ANY)
IN_HBM = pl.BlockSpec(memory_space=pltpu.HBM)


def dot_nt(a, b):
    return lax.dot_general(a, b, (((1,), (1,)), ((), ())), preferred_element_type=F32)


def dot_nn(a, b):
    return lax.dot_general(a, b, (((1,), (0,)), ((), ())), preferred_element_type=F32)


def dot_tn(a, b):
    return lax.dot_general(a, b, (((0,), (0,)), ((), ())), preferred_element_type=F32)


def full(shape):
    return pl.BlockSpec(shape, lambda i, *_: (0,) * len(shape))


def entry(index, *shape):
    return pl.BlockSpec((1,) + shape, lambda i, *_: (index,) + (0,) * len(shape))


def cost(flops, nbytes):
    return pl.CostEstimate(flops=flops, bytes_accessed=nbytes, transcendentals=0)


class Plan:
    def __init__(self, tile):
        self.tile = tile
        self.per = HEADS // 4
        self.piece = (2, tile, HEAD_DIM)
        self.layer = (4,) + self.piece


def move(plan, pos, inputs, shapes, moves, name, into=(), after=(), limit=2 * MIB):
    given, kept = len(inputs), len(into)
    extra = len(after)

    def kernel(pos_ref, *refs):
        sems = refs[-1]
        outs = refs[given + kept + extra : -1]

        def view(ref, where):
            if where[:1] == ("head",):
                column = ((pos_ref[1] ^ where[1]) * plan.per + where[2]) * HEAD_DIM
                return ref.at[:, pl.ds(pl.multiple_of(column, HEAD_DIM), HEAD_DIM)]
            return ref.at[where] if where else ref

        copies = [
            pltpu.make_async_copy(view(refs[a], u), view(outs[b], v), sems.at[n])
            for n, (a, u, b, v) in enumerate(moves)
        ]
        for copy in copies:
            copy.start()
        for copy in copies:
            copy.wait()

    specs = [IN_HBM if x.ndim == 2 else ANYWHERE for x in inputs] + [IN_HBM] * kept + [ANYWHERE] * extra
    return pl.pallas_call(
        kernel,
        out_shape=[jax.ShapeDtypeStruct(shape, BF) for shape in shapes],
        grid_spec=pltpu.PrefetchScalarGridSpec(
            num_scalar_prefetch=1,
            grid=(1,),
            in_specs=specs,
            out_specs=[IN_HBM if len(shape) == 2 else ANYWHERE for shape in shapes],
            scratch_shapes=[pltpu.SemaphoreType.DMA((len(moves),))],
        ),
        input_output_aliases={1 + given + n: n for n in range(kept)},
        compiler_params=pltpu.CompilerParams(vmem_limit_bytes=limit),
        cost_estimate=cost(0, 0),
        name=name,
    )(pos, *inputs, *into, *after)


def attend(plan, pos, table, chunk, query, grad_out, blocks):
    tile = plan.tile
    count = len(blocks)

    def kernel(pos_ref, table_ref, q_ref, g_ref, *refs):
        nears, fars = refs[:3], refs[3:6]
        qg_near, qg_far = refs[6:8]
        first, near, far, halo_a, halo_b, sum_ref = refs[count : count + 6]
        kv, qgs, odq, acc = refs[count + 6 :]
        for n in range(3):
            kv[pl.ds(4 * n, 2)] = nears[n][0]
            kv[pl.ds(4 * n + 2, 2)] = fars[n][0]
        qgs[0, 0] = q_ref[...]
        qgs[0, 1] = g_ref[...]
        qgs[1] = qg_near[0]
        qgs[pl.ds(2, 2)] = qg_far[0]
        acc[...] = jnp.zeros_like(acc)
        seq, me = pos_ref[0], pos_ref[1]

        def place(tile_id):
            rel = tile_id - (seq - 1) * 4
            turn = jnp.where((rel // 4 > 1) ^ (seq % 2 > 0), 1, 2)
            return jnp.where(rel // 4 == 1, 0, turn) * 4 + ((rel % 4) ^ me)

        def work(r, places):
            q, g = qgs[r, 0], qgs[r, 1]
            scores = [dot_nt(kv[p, 0], q) * SCALE for p in places]
            peak = functools.reduce(
                jnp.maximum, [jnp.max(s, axis=0, keepdims=True) for s in scores]
            )
            expo = [jnp.exp(s - peak) for s in scores]
            wgrad = [dot_nt(kv[p, 1], g) for p in places]
            total = sum(jnp.sum(e, axis=0, keepdims=True) for e in expo)
            mixed = sum(jnp.sum(e * w, axis=0, keepdims=True) for e, w in zip(expo, wgrad))
            inv = 1.0 / total
            delta = mixed * inv
            att_t, dq_t = 0.0, 0.0
            for p, e, w in zip(places, expo, wgrad):
                weight = e * inv
                low = weight.astype(BF)
                sgrad = (weight * (w - delta) * SCALE).astype(BF)
                att_t = att_t + dot_tn(kv[p, 1], low)
                dq_t = dq_t + dot_tn(kv[p, 0], sgrad)
                acc[p, 0] += dot_nn(sgrad, q)
                acc[p, 1] += dot_nn(low, g)
            odq[r, 0] = att_t.T.astype(BF)
            odq[r, 1] = dq_t.T.astype(BF)

        def step(r, carry):
            row = (seq * 4 + (r ^ me)) * 2 * SLOTS
            live = [table_ref[row + SLOTS + n] > 0 for n in range(SLOTS)]
            spots = [place(table_ref[row + n]) for n in range(SLOTS)]
            second = jnp.where(live[1], spots[1], spots[2])

            @pl.when(live[1] & live[2])
            def _():
                work(r, [spots[0], spots[1], spots[2]])

            @pl.when(live[1] ^ live[2])
            def _():
                work(r, [spots[0], second])

            @pl.when(jnp.logical_not(live[1] | live[2]))
            def _():
                work(r, [spots[0]])

            return carry

        lax.fori_loop(0, 4, step, 0)
        first[...] = odq[0]
        near[...] = odq[1]
        far[...] = odq[pl.ds(2, 2)]
        sum_ref[...] = acc[pl.ds(0, 4)]
        halo_a[...] = acc[pl.ds(4, 4)].astype(BF)
        halo_b[...] = acc[pl.ds(8, 4)].astype(BF)

    column = pl.BlockSpec((tile, HEAD_DIM), lambda i, p, t: (0, p[1] * plan.per + chunk))
    shapes = [plan.piece, plan.piece, (2,) + plan.piece, plan.layer, plan.layer]
    rows = 4 * tile * HEAD_DIM
    return pl.pallas_call(
        kernel,
        out_shape=[jax.ShapeDtypeStruct(shape, BF) for shape in shapes]
        + [jax.ShapeDtypeStruct(plan.layer, F32)],
        grid_spec=pltpu.PrefetchScalarGridSpec(
            num_scalar_prefetch=2,
            grid=(1,),
            in_specs=[column] * 2 + [spec for _, spec in blocks],
            out_specs=[full(shape) for shape in shapes + [plan.layer]],
            scratch_shapes=[
                pltpu.VMEM((12,) + plan.piece, BF),
                pltpu.VMEM(plan.layer, BF),
                pltpu.VMEM(plan.layer, BF),
                pltpu.VMEM((12,) + plan.piece, F32),
            ],
        ),
        compiler_params=PARAMS,
        cost_estimate=cost(60 * SLOTS * rows * tile, 40 * rows),
        name="attend",
    )(pos, table, query, grad_out, *[array for array, _ in blocks])


def owned(plan, pos, total, halos):
    def kernel(pos_ref, total_ref, halo_a, halo_b, first, near, far):
        for r in range(4):
            grads = total_ref[r]
            for n, halo in enumerate((halo_a, halo_b)):
                grads += jnp.where(pos_ref[2 + n] > 0, halo[r].astype(F32), 0.0)
            if r < 2:
                (first, near)[r][...] = grads.astype(BF)
            else:
                far[r - 2] = grads.astype(BF)

    shapes = [plan.piece, plan.piece, (2,) + plan.piece]
    return pl.pallas_call(
        kernel,
        out_shape=[jax.ShapeDtypeStruct(shape, BF) for shape in shapes],
        grid_spec=pltpu.PrefetchScalarGridSpec(
            num_scalar_prefetch=1,
            grid=(1,),
            in_specs=[full(plan.layer)] * 3,
            out_specs=[full(shape) for shape in shapes],
        ),
        compiler_params=PARAMS,
        cost_estimate=cost(0, 20 * 4 * plan.tile * HEAD_DIM),
        name="owned",
    )(pos, total, *halos)


def swap(value, r):
    return lax.ppermute(value, "head", [(i, i ^ r) for i in range(4)])


def exchange(value, turn):
    count = lax.axis_size("seq")
    pairs = []
    for s in range(count):
        other = s + 1 if s % 2 == turn else s - 1
        for h in range(4):
            there = other * 4 + h if 0 <= other < count else s * 4 + (h ^ 1)
            pairs.append((s * 4 + h, there))
    return lax.ppermute(value, ("seq", "head"), pairs)


def body(query, key_in, value, grad_out, pattern, live):
    plan = Plan(query.shape[0])
    per, piece = plan.per, plan.piece
    chunks = range(per)
    count = lax.axis_size("seq")
    seq = lax.axis_index("seq")
    met = []
    for turn in range(2):
        other = jnp.where(seq % 2 == turn, seq + 1, seq - 1)
        met.append((other >= 0) & (other < count))
    pos = jnp.stack([seq, lax.axis_index("head"), *met]).astype(jnp.int32)
    table = jnp.concatenate([pattern, live], axis=1).reshape(-1)

    def pick(r, c, out, *at):
        return [(a, ("head", r, c), out, at + (a,)) for a in range(2)]

    every, here, there = list(chunks), [key_in, value], [query, grad_out]

    def for_near(pair, name):
        moves = [m for n, r in enumerate((1, 3)) for c in every for m in pick(r, c, 0, n * per + c)]
        return swap(move(plan, pos, pair, [(2 * per,) + piece], moves, name)[0], 1)

    def for_far(pair, got, group, name, after=()):
        moves = []
        for n, c in enumerate(group):
            moves += pick(2, c, 0, n, 0)
            moves.append((2, (per + c,), 0, (n, 1)))
        shapes = [(len(group), 2) + piece]
        return move(plan, pos, [*pair, got], shapes, moves, name, after=after)[0]

    kv_got = for_near(here, "kv_for_near")
    qg_got = for_near(there, "qg_for_near")
    kv_parts, qg_parts = [every[:-1], every[-1:]], [every[:1], every[1:]]
    message = for_far(here, kv_got, kv_parts[0], "kv_for_far")
    far = [swap(message, 2)]
    moves = [m for c in every for m in pick(0, c, 0, c, 0)]
    moves += [(2, (c,), 0, (c, 1)) for c in every]
    near = move(plan, pos, [*here, kv_got], [(per, 2) + piece], moves, "kv_near", after=[message])[0]
    nears = [near] + [exchange(near, turn) for turn in range(2)]
    far.append(swap(for_far(here, kv_got, kv_parts[1], "kv_for_far", after=far[:1]), 2))
    fars = [[m] + [exchange(m, turn) for turn in range(2)] for m in far]
    qg_fars = [
        swap(for_far(there, qg_got, part, "qg_for_far", after=far[n : n + 1]), 2)
        for n, part in enumerate(qg_parts)
    ]

    odq, dkv = [], []
    for c in chunks:
        pair = (2,) + piece
        blocks = [(array, entry(c, *pair)) for array in nears]
        for arrays, parts in ((fars, kv_parts), ([[x] for x in qg_fars], qg_parts)):
            n = 0 if c in parts[0] else 1
            blocks += [(array, entry(c - parts[n][0], *pair)) for array in arrays[n]]
        blocks.insert(6, (qg_got, entry(c, *piece)))
        *mine, halo_a, halo_b, total = attend(plan, pos, table, c, query, grad_out, blocks)
        odq.append(mine[:2] + [swap(mine[2], 2)])
        halos = [exchange(halo, turn) for turn, halo in enumerate((halo_a, halo_b))]
        dkv.append(owned(plan, pos, total, halos))

    def onward(group, name, after=()):
        moves = []
        for c in range(len(group)):
            moves += [(2 * c, (), 0, (c, 0)), (2 * c + 1, (1,), 0, (c, 1))]
        inputs = [x for _, near, far in group for x in (near, far)]
        shapes = [(len(group), 2) + piece]
        return swap(move(plan, pos, inputs, shapes, moves, name, after=after)[0], 1)

    def columns(where):
        return [
            (a, view + (b,), b, ("head", r, c)) for a, view, r, c in where for b in range(2)
        ]

    shapes = [(plan.tile, HEADS * HEAD_DIM)] * 2

    def spread(group, got):
        inputs, where = [got], []
        for c, (first, _, far) in enumerate(group):
            where += [(0, (c, 0), 1, c), (0, (c, 1), 3, c)]
            where += [(len(inputs), (), 0, c), (len(inputs) + 1, (0,), 2, c)]
            inputs += [first, far]
        return inputs, where

    inputs, where = spread(odq, onward(odq, "odq_near", [dkv[-2][0]]))
    attended, query_grad = move(plan, pos, inputs, shapes, columns(where), "odq_out")

    early = [[first, near, swap(far, 2)] for first, near, far in dkv[:-1]]
    inputs, where = spread(early, onward(early, "dkv_near"))
    grads = move(plan, pos, inputs, shapes, columns(where), "dkv_early")
    first, near, far = dkv[-1]
    inputs = [first, swap(near, 1), swap(far[0], 2), swap(far[1], 3)]
    where = [(r, (), r, per - 1) for r in range(4)]
    key_grad, value_grad = move(plan, pos, inputs, shapes, columns(where), "dkv_out", into=grads)
    return attended, query_grad, key_grad, value_grad


def solution(mesh):
    split = P(("groups", "seq", "head"), None)
    return jax.shard_map(
        body,
        mesh=mesh,
        in_specs=(split, split, split, split, P(), P()),
        out_specs=(split, split, split, split),
        check_vma=False,
    )
```

time: 130 us -> 106 us (0.82)
  starting transfers between devices: 64 us -> 26.6 us
  waiting for transfers between devices: 28.8 us -> 39.8 us
  Pallas kernels: 25.1 us -> 34.4 us
  local copies, waits for them, and re-layouts: 10.3 us -> 2.49 us
    ppermute x48 -> x28, starting transfers between devices: 64 us -> 26.6 us  [the longest x16 15.3 us: swap(): return lax.ppermute(value, 'head', [(i, i ^ r) for i in range(4)])]
    ppermute x48 -> x28, waiting for transfers between devices: 28.8 us -> 39.8 us  [the longest x16 32.5 us: swap(): return lax.ppermute(value, 'head', [(i, i ^ r) for i in range(4)])]
    pallas_call x13 -> x18, Pallas kernels: 25.1 us -> 34.4 us  [the longest x3 17.6 us: attend(): pl.pallas_call(kernel, out_shape=[jax.ShapeDtypeStruct(shape, BF) for sha...]
    unnamed x44 -> x16, local copies, waits for them, and re-layouts: 10.1 us -> 2.3 us
  transfers between devices with their start and end apart: 48 -> 28, of which waited for: 14 -> 11; matrix products, arithmetic and copies ran while one was open for 0% -> 0% of each run, Pallas kernels for 17% -> 31%
where the time goes in v2:
time: 106 us; the launch traced here: 104 us
  waiting for transfers between devices  39.8 us (38%)
  Pallas kernels  34.4 us (32%)
  starting transfers between devices  26.6 us (25%)
  local copies, waits for them, and re-layouts  2.49 us (2%)
    ppermute x16, waiting for transfers between devices, swap(): return lax.ppermute(value, 'head', [(i, i ^ r) for i in range(4)])  32.5 us
    pallas_call x3, Pallas kernels, attend(): pl.pallas_call(kernel, out_shape=[jax.ShapeDtypeStruct(shape, BF) for sha...  17.6 us
    ppermute x16, starting transfers between devices, swap(): return lax.ppermute(value, 'head', [(i, i ^ r) for i in range(4)])  15.3 us
    pallas_call x12, Pallas kernels, move(): pl.pallas_call(kernel, out_shape=[jax.ShapeDtypeStruct(shape, BF) for sha...  14.4 us
    ppermute x12, starting transfers between devices, exchange(): return lax.ppermute(value, ('seq', 'head'), pairs)  11.2 us
    ppermute x12, waiting for transfers between devices, exchange(): return lax.ppermute(value, ('seq', 'head'), pairs)  7.29 us
    pallas_call x3, Pallas kernels, owned(): pl.pallas_call(kernel, out_shape=[jax.ShapeDtypeStruct(shape, BF) for sha...  2.32 us
    unnamed x16, local copies, waits for them, and re-layouts  2.3 us
  transfers between devices with their start and end apart: 28, of which 11 were waited for; matrix products, arithmetic and copies ran while one was open for 0% of the time, Pallas kernels for 31%

profile of v2, /device:TPU:0, one launch (start us, length us, event | category | flops | bytes accessed | tf_op | source)
XLA Modules:
  0.0 104.2 jit_solution(16411942755410801265)
XLA Ops:
  0.7 1.1 %copy-done = bf16[256,1536]{1,0:T(8,128)(2,1)S(1)} copy-done((bf16[256,1536]{1,0:T(8,128)(2,1)S(1)}, bf16[256,1536]{1,0:T(8,128)(2,1)}, u32[]{:S(2)}) %copy-start) | copy-done | bytes 786456
  1.9 1.1 %copy-done.2 = bf16[256,1536]{1,0:T(8,128)(2,1)S(1)} copy-done((bf16[256,1536]{1,0:T(8,128)(2,1)S(1)}, bf16[256,1536]{1,0:T(8,128)(2,1)}, u32[]{:S(2)}) %copy-start.2) | copy-done | bytes 786456
  7.3 2.9 %collective-permute-start.3 = (bf16[2,2,2,256,128]{4,3,2,1,0:T(8,128)(2,1)S(1)}, bf16[2,2,2,256,128]{4,3,2,1,0:T(8,128)(2,1)S(1)}, u32[]{:S(2)}, u32[]{:S(2)}) collective-permute-start(bf16[2,2,2,256,128]{4,3,2,1,0:T(8,128)(2,1)S(1)} %kv_for_far.2.refs_3_), channel_id=1, source_target_pairs={{0,2},{1,3},{2,0},{3,1},{4,6},{5,7},{6,4},{7,5},{8,10},{9,11},{10,... | collective-permute-start | bytes 1572872 | tf_op jit(solution)/shard_map/ppermute | solution.py:225
  10.2 1.5 %kv_near.1.refs_0_ = bf16[3,2,2,256,128]{4,3,2,1,0:T(8,128)(2,1)} custom-call(s32[4]{0:T(128)S(1)} %pad_add_fusion.1.pos_ref, bf16[256,1536]{1,0:T(8,128)(2,1)S(1)} %copy-done.1, bf16[256,1536]{1,0:T(8,128)(2,1)S(1)} %copy-done.3, bf16[6,2,256,128]{3,2,1,0:T(8,128)(2,1)S(1)} %collective-permute-done.refs_2_, bf16[2,2,2,256,128]{4,3,2,1,0:T(8,128)(2,1)S(1)} %kv_for_far.2.refs_3_), custom_call_target="tpu_custom_call" | custom-call | tf_op jit(solution)/shard_map/kv_near/pallas_call | solution.py:79
  11.7 1.6 %collective-permute-start.1 = (bf16[3,2,2,256,128]{4,3,2,1,0:T(8,128)(2,1)}, bf16[3,2,2,256,128]{4,3,2,1,0:T(8,128)(2,1)}, u32[]{:S(2)}, u32[]{:S(2)}) collective-permute-start(bf16[3,2,2,256,128]{4,3,2,1,0:T(8,128)(2,1)} %kv_near.1.refs_0_), channel_id=1, source_target_pairs={{0,4},{1,5},{2,6},{3,7},{4,0},{5,1},{6,2},{7,3},{8,12},{9,13},{10,... | collective-permute-start | bytes 2359304 | tf_op jit(solution)/shard_map/ppermute | solution.py:236
  13.4 9.1 %collective-permute-done.3.refs_3_ = bf16[2,2,2,256,128]{4,3,2,1,0:T(8,128)(2,1)S(1)} collective-permute-done((bf16[2,2,2,256,128]{4,3,2,1,0:T(8,128)(2,1)S(1)}, bf16[2,2,2,256,128]{4,3,2,1,0:T(8,128)(2,1)S(1)}, u32[]{:S(2)}, u32[]{:S(2)}) %collective-permute-start.3) | collective-permute-done | bytes 524320 | tf_op jit(solution)/shard_map/ppermute | solution.py:225
  23.3 1.8 %collective-permute-start.9 = (bf16[1,2,2,256,128]{4,3,2,1,0:T(8,128)(2,1)S(1)}, bf16[1,2,2,256,128]{4,3,2,1,0:T(8,128)(2,1)S(1)}, u32[]{:S(2)}, u32[]{:S(2)}) collective-permute-start(bf16[1,2,2,256,128]{4,3,2,1,0:T(8,128)(2,1)S(1)} %kv_for_far.3), channel_id=1, source_target_pairs={{0,2},{1,3},{2,0},{3,1},{4,6},{5,7},{6,4},{7,5},{8,10},{9,11},{10,... | collective-permute-start | bytes 786440 | tf_op jit(solution)/shard_map/ppermute | solution.py:225
  25.1 1.6 %collective-permute-start.4 = (bf16[2,2,2,256,128]{4,3,2,1,0:T(8,128)(2,1)S(1)}, bf16[2,2,2,256,128]{4,3,2,1,0:T(8,128)(2,1)}, u32[]{:S(2)}, u32[]{:S(2)}) collective-permute-start(bf16[2,2,2,256,128]{4,3,2,1,0:T(8,128)(2,1)S(1)} %collective-permute-done.3.refs_3_), channel_id=1, source_target_pairs={{0,4},{1,5},{2,6},{3,7},{4,0},{5,1},{6,2},{7,3},{8,12},{9,13},{10,... | collective-permute-start | bytes 1572872 | tf_op jit(solution)/shard_map/ppermute | solution.py:236
  27.4 3.8 %collective-permute-done.9.refs_3_ = bf16[1,2,2,256,128]{4,3,2,1,0:T(8,128)(2,1)S(1)} collective-permute-done((bf16[1,2,2,256,128]{4,3,2,1,0:T(8,128)(2,1)S(1)}, bf16[1,2,2,256,128]{4,3,2,1,0:T(8,128)(2,1)S(1)}, u32[]{:S(2)}, u32[]{:S(2)}) %collective-permute-start.9) | collective-permute-done | bytes 262176 | tf_op jit(solution)/shard_map/ppermute | solution.py:225
  31.3 1.4 %collective-permute-start.7 = (bf16[1,2,2,256,128]{4,3,2,1,0:T(8,128)(2,1)S(1)}, bf16[1,2,2,256,128]{4,3,2,1,0:T(8,128)(2,1)}, u32[]{:S(2)}, u32[]{:S(2)}) collective-permute-start(bf16[1,2,2,256,128]{4,3,2,1,0:T(8,128)(2,1)S(1)} %qg_for_far.2), channel_id=1, source_target_pairs={{0,2},{1,3},{2,0},{3,1},{4,6},{5,7},{6,4},{7,5},{8,10},{9,11},{10,... | collective-permute-start | bytes 786440 | tf_op jit(solution)/shard_map/ppermute | solution.py:225
  33.9 4.6 %collective-permute-done.7.refs_7_ = bf16[1,2,2,256,128]{4,3,2,1,0:T(8,128)(2,1)} collective-permute-done((bf16[1,2,2,256,128]{4,3,2,1,0:T(8,128)(2,1)S(1)}, bf16[1,2,2,256,128]{4,3,2,1,0:T(8,128)(2,1)}, u32[]{:S(2)}, u32[]{:S(2)}) %collective-permute-start.7) | collective-permute-done | bytes 262176 | tf_op jit(solution)/shard_map/ppermute | solution.py:225
  39.6 1.6 %collective-permute-start.12 = (bf16[1,2,2,256,128]{4,3,2,1,0:T(8,128)(2,1)S(1)}, bf16[1,2,2,256,128]{4,3,2,1,0:T(8,128)(2,1)S(1)}, u32[]{:S(2)}, u32[]{:S(2)}) collective-permute-start(bf16[1,2,2,256,128]{4,3,2,1,0:T(8,128)(2,1)S(1)} %collective-permute-done.9.refs_3_), channel_id=1, source_target_pairs={{0,4},{1,5},{2,6},{3,7},{4,0},{5,1},{6,2},{7,3},{8,12},{9,13},{10,... | collective-permute-start | bytes 786440 | tf_op jit(solution)/shard_map/ppermute | solution.py:236
  41.2 2.6 %collective-permute-done.4.refs_4_ = bf16[2,2,2,256,128]{4,3,2,1,0:T(8,128)(2,1)} collective-permute-done((bf16[2,2,2,256,128]{4,3,2,1,0:T(8,128)(2,1)S(1)}, bf16[2,2,2,256,128]{4,3,2,1,0:T(8,128)(2,1)}, u32[]{:S(2)}, u32[]{:S(2)}) %collective-permute-start.4) | collective-permute-done | bytes 524320 | tf_op jit(solution)/shard_map/ppermute | solution.py:236
  43.8 6.0 %attend.3 = (bf16[2,256,128]{2,1,0:T(8,128)(2,1)S(1)}, bf16[2,256,128]{2,1,0:T(8,128)(2,1)S(1)}, bf16[2,2,256,128]{3,2,1,0:T(8,128)(2,1)S(1)}, bf16[4,2,256,128]...) custom-call(s32[4]{0:T(128)S(1)} %pad_add_fusion.1.pos_ref, ...), custom_call_target="tpu_custom_call" | custom-call | flops 6039797760 | bytes 5242880 | tf_op jit(solution)/shard_map/attend/pallas_call | solution.py:175
  49.8 2.5 %collective-permute-start.23 = (bf16[4,2,256,128]{3,2,1,0:T(8,128)(2,1)S(1)}, bf16[4,2,256,128]{3,2,1,0:T(8,128)(2,1)S(1)}, u32[]{:S(2)}, u32[]{:S(2)}) collective-permute-start(bf16[4,2,256,128]{3,2,1,0:T(8,128)(2,1)S(1)} %get-tuple-element.59), channel_id=1, source_target_pairs={{0,4},{1,5},{2,6},{3,7},{4,0},{5,1},{6,2},{7,3},{8,12},{9,13},{10,... | collective-permute-start | bytes 1572872 | tf_op jit(solution)/shard_map/ppermute | solution.py:236
  52.8 5.9 %attend.4 = (bf16[2,256,128]{2,1,0:T(8,128)(2,1)S(1)}, bf16[2,256,128]{2,1,0:T(8,128)(2,1)S(1)}, bf16[2,2,256,128]{3,2,1,0:T(8,128)(2,1)S(1)}, bf16[4,2,256,128]...) custom-call(s32[4]{0:T(128)S(1)} %pad_add_fusion.1.pos_ref, ...), custom_call_target="tpu_custom_call" | custom-call | flops 6039797760 | bytes 5242880 | tf_op jit(solution)/shard_map/attend/pallas_call | solution.py:175
  58.8 2.2 %collective-permute-start.15 = (bf16[4,2,256,128]{3,2,1,0:T(8,128)(2,1)S(1)}, bf16[4,2,256,128]{3,2,1,0:T(8,128)(2,1)S(1)}, u32[]{:S(2)}, u32[]{:S(2)}) collective-permute-start(bf16[4,2,256,128]{3,2,1,0:T(8,128)(2,1)S(1)} %get-tuple-element.44), channel_id=1, source_target_pairs={{0,4},{1,5},{2,6},{3,7},{4,0},{5,1},{6,2},{7,3},{8,12},{9,13},{10,... | collective-permute-start | bytes 1572872 | tf_op jit(solution)/shard_map/ppermute | solution.py:236
  60.9 5.7 %attend.5 = (bf16[2,256,128]{2,1,0:T(8,128)(2,1)S(1)}, bf16[2,256,128]{2,1,0:T(8,128)(2,1)S(1)}, bf16[2,2,256,128]{3,2,1,0:T(8,128)(2,1)S(1)}, bf16[4,2,256,128]...) custom-call(s32[4]{0:T(128)S(1)} %pad_add_fusion.1.pos_ref, ...), custom_call_target="tpu_custom_call" | custom-call | flops 6039797760 | bytes 5242880 | tf_op jit(solution)/shard_map/attend/pallas_call | solution.py:175
  66.7 1.6 %collective-permute-start.14 = (bf16[2,2,256,128]{3,2,1,0:T(8,128)(2,1)S(1)}, bf16[2,2,256,128]{3,2,1,0:T(8,128)(2,1)S(1)}, u32[]{:S(2)}, u32[]{:S(2)}) collective-permute-start(bf16[2,2,256,128]{3,2,1,0:T(8,128)(2,1)S(1)} %get-tuple-element.42), channel_id=1, source_target_pairs={{0,2},{1,3},{2,0},{3,1},{4,6},{5,7},{6,4},{7,5},{8,10},{9,11},{10,... | collective-permute-start | bytes 786440 | tf_op jit(solution)/shard_map/ppermute | solution.py:225
  68.8 4.7 %collective-permute-done.15.halo_a = bf16[4,2,256,128]{3,2,1,0:T(8,128)(2,1)S(1)} collective-permute-done((bf16[4,2,256,128]{3,2,1,0:T(8,128)(2,1)S(1)}, bf16[4,2,256,128]{3,2,1,0:T(8,128)(2,1)S(1)}, u32[]{:S(2)}, u32[]{:S(2)}) %collective-permute-start.15) | collective-permute-done | bytes 524320 | tf_op jit(solution)/shard_map/ppermute | solution.py:236
  73.5 1.7 %collective-permute-start.18 = (bf16[4,2,256,128]{3,2,1,0:T(8,128)(2,1)S(1)}, bf16[4,2,256,128]{3,2,1,0:T(8,128)(2,1)S(1)}, u32[]{:S(2)}, u32[]{:S(2)}) collective-permute-start(bf16[4,2,256,128]{3,2,1,0:T(8,128)(2,1)S(1)} %get-tuple-element.53), channel_id=1, source_target_pairs={{0,4},{1,5},{2,6},{3,7},{4,0},{5,1},{6,2},{7,3},{8,12},{9,13},{10,... | collective-permute-start | bytes 1572872 | tf_op jit(solution)/shard_map/ppermute | solution.py:236
  77.4 1.5 %collective-permute-start.26 = (bf16[2,2,256,128]{3,2,1,0:T(8,128)(2,1)S(1)}, bf16[2,2,256,128]{3,2,1,0:T(8,128)(2,1)S(1)}, u32[]{:S(2)}, u32[]{:S(2)}) collective-permute-start(bf16[2,2,256,128]{3,2,1,0:T(8,128)(2,1)S(1)} %get-tuple-element.64), channel_id=1, source_target_pairs={{0,2},{1,3},{2,0},{3,1},{4,6},{5,7},{6,4},{7,5},{8,10},{9,11},{10,... | collective-permute-start | bytes 786440 | tf_op jit(solution)/shard_map/ppermute | solution.py:225
  78.9 2.6 %collective-permute-done.11.refs_3_.refs_4_ = bf16[2,2,256,128]{3,2,1,0:T(8,128)(2,1)S(1)} collective-permute-done((bf16[2,2,256,128]{3,2,1,0:T(8,128)(2,1)S(1)}, bf16[2,2,256,128]{3,2,1,0:T(8,128)(2,1)S(1)}, u32[]{:S(2)}, u32[]{:S(2)}) %collective-permute-start.11) | collective-permute-done | bytes 262176 | tf_op jit(solution)/shard_map/ppermute | solution.py:225
  81.5 1.6 %odq_near.1 = bf16[3,2,2,256,128]{4,3,2,1,0:T(8,128)(2,1)S(1)} custom-call(s32[4]{0:T(128)S(1)} %pad_add_fusion.1.pos_ref, bf16[2,256,128]{2,1,0:T(8,128)(2,1)S(1)} %get-tuple-element.37.refs_0_, bf16[2,2,256,128]{3,2,1,0:T(8,128)(2,1)S(1)} %collective-permute-done.8.refs_1_.refs_2_, bf16[2,256,128]{2,1,0:T(8,128)(2,1)S(1)} %get-tuple-element.39.refs_2_, ...), custom_call_target="tpu_custom_call" | custom-call | tf_op jit(solution)/shard_map/odq_near/pallas_call | solution.py:79
  83.2 3.9 %collective-permute-done.25.refs_1_.refs_2_ = bf16[2,2,256,128]{3,2,1,0:T(8,128)(2,1)S(1)} collective-permute-done((bf16[2,2,256,128]{3,2,1,0:T(8,128)(2,1)S(1)}, bf16[2,2,256,128]{3,2,1,0:T(8,128)(2,1)S(1)}, u32[]{:S(2)}, u32[]{:S(2)}) %collective-permute-start.25) | collective-permute-done | bytes 262176 | tf_op jit(solution)/shard_map/ppermute | solution.py:225
  87.1 5.2 %collective-permute-done.26.refs_3_.refs_4_ = bf16[2,2,256,128]{3,2,1,0:T(8,128)(2,1)S(1)} collective-permute-done((bf16[2,2,256,128]{3,2,1,0:T(8,128)(2,1)S(1)}, bf16[2,2,256,128]{3,2,1,0:T(8,128)(2,1)S(1)}, u32[]{:S(2)}, u32[]{:S(2)}) %collective-permute-start.26) | collective-permute-done | bytes 262176 | tf_op jit(solution)/shard_map/ppermute | solution.py:225
  92.3 1.3 %dkv_near.1 = bf16[2,2,2,256,128]{4,3,2,1,0:T(8,128)(2,1)S(1)} custom-call(s32[4]{0:T(128)S(1)} %pad_add_fusion.1.pos_ref, bf16[2,256,128]{2,1,0:T(8,128)(2,1)S(1)} %get-tuple-element.61.refs_0_, bf16[2,2,256,128]{3,2,1,0:T(8,128)(2,1)S(1)} %collective-permute-done.25.refs_1_.refs_2_, bf16[2,256,128]{2,1,0:T(8,128)(2,1)S(1)} %get-tuple-element.63.refs_2_, ...), custom_call_target="tpu_custom_call" | custom-call | tf_op jit(solution)/shard_map/dkv_near/pallas_call | solution.py:79
  94.5 1.6 %collective-permute-start.21 = (bf16[2,256,128]{2,1,0:T(8,128)(2,1)S(1)}, bf16[2,256,128]{2,1,0:T(8,128)(2,1)S(1)}, u32[]{:S(2)}, u32[]{:S(2)}) collective-permute-start(bf16[2,256,128]{2,1,0:T(8,128)(2,1)S(1)} %get-tuple-element.71), channel_id=1, source_target_pairs={{0,2},{1,3},{2,0},{3,1},{4,6},{5,7},{6,4},{7,5},{8,10},{9,11},{10,... | collective-permute-start | bytes 393224 | tf_op jit(solution)/shard_map/ppermute | solution.py:225
  96.7 1.6 %dkv_early.1 = (bf16[256,1536]{1,0:T(8,128)(2,1)}, bf16[256,1536]{1,0:T(8,128)(2,1)}) custom-call(s32[4]{0:T(128)S(1)} %pad_add_fusion.1.pos_ref, bf16[2,2,2,256,128]{4,3,2,1,0:T(8,128)(2,1)S(1)} %collective-permute-done.27.refs_0_, bf16[2,256,128]{2,1,0:T(8,128)(2,1)S(1)} %get-tuple-element.65.refs_1_, ...), custom_call_target="tpu_custom_call" | custom-call | tf_op jit(solution)/shard_map/dkv_early/pallas_call | solution.py:79
  98.4 1.9 %odq_out.1 = (bf16[256,1536]{1,0:T(8,128)(2,1)}, bf16[256,1536]{1,0:T(8,128)(2,1)}) custom-call(s32[4]{0:T(128)S(1)} %pad_add_fusion.1.pos_ref, bf16[3,2,2,256,128]{4,3,2,1,0:T(8,128)(2,1)S(1)} %collective-permute-done.17.refs_0_, bf16[2,256,128]{2,1,0:T(8,128)(2,1)S(1)} %get-tuple-element.47.refs_1_, ...), custom_call_target="tpu_custom_call" | custom-call | tf_op jit(solution)/shard_map/odq_out/pallas_call | solution.py:79
  100.9 2.0 %collective-permute-done.22.refs_3_ = bf16[2,256,128]{2,1,0:T(8,128)(2,1)S(1)} collective-permute-done((bf16[2,256,128]{2,1,0:T(8,128)(2,1)S(1)}, bf16[2,256,128]{2,1,0:T(8,128)(2,1)S(1)}, u32[]{:S(2)}, u32[]{:S(2)}) %collective-permute-start.22) | collective-permute-done | bytes 131104 | tf_op jit(solution)/shard_map/ppermute | solution.py:225
  102.9 1.4 %dkv_out.1 = (bf16[256,1536]{1,0:T(8,128)(2,1)}, bf16[256,1536]{1,0:T(8,128)(2,1)}) custom-call(s32[4]{0:T(128)S(1)} %pad_add_fusion.1.pos_ref, bf16[2,256,128]{2,1,0:T(8,128)(2,1)S(1)} %get-tuple-element.55.refs_0_, bf16[2,256,128]{2,1,0:T(8,128)(2,1)S(1)} %collective-permute-done.20.refs_1_, ...), custom_call_target="tpu_custom_call", output_to_operand_aliasing={{0}: (5, {}), {1}: (6, {})} | custom-call | tf_op jit(solution)/shard_map/dkv_out/pallas_call | solution.py:79
  (63 shorter events, 13.6 us)
Async XLA Ops:
  3.8 2.5 %copy-start.1 = (bf16[256,1536]{1,0:T(8,128)(2,1)S(1)}, bf16[256,1536]{1,0:T(8,128)(2,1)}, u32[]{:S(2)}) copy-start(bf16[256,1536]{1,0:T(8,128)(2,1)} %refs_0_.12) | copy-start | bytes 2359300
  3.9 2.4 %copy-start.3 = (bf16[256,1536]{1,0:T(8,128)(2,1)S(1)}, bf16[256,1536]{1,0:T(8,128)(2,1)}, u32[]{:S(2)}) copy-start(bf16[256,1536]{1,0:T(8,128)(2,1)} %refs_1_.12) | copy-start | bytes 2359300
  3.9 2.4 %collective-permute-start = (bf16[6,2,256,128]{3,2,1,0:T(8,128)(2,1)S(1)}, bf16[6,2,256,128]{3,2,1,0:T(8,128)(2,1)S(1)}, u32[]{:S(2)}, u32[]{:S(2)}) collective-permute-start(bf16[6,2,256,128]{3,2,1,0:T(8,128)(2,1)S(1)} %kv_for_near.1), channel_id=1, source_target_pairs={{0,1},{1,0},{2,3},{3,2},{4,5},{5,4},{6,7},{7,6},{8,9},{9,8},{10,11... | collective-permute-start | bytes 2359304 | tf_op jit(solution)/shard_map/ppermute | solution.py:225
  5.2 21.4 %collective-permute-start.6 = (bf16[6,2,256,128]{3,2,1,0:T(8,128)(2,1)S(1)}, bf16[6,2,256,128]{3,2,1,0:T(8,128)(2,1)S(1)}, u32[]{:S(2)}, u32[]{:S(2)}) collective-permute-start(bf16[6,2,256,128]{3,2,1,0:T(8,128)(2,1)S(1)} %qg_for_near.1), channel_id=1, source_target_pairs={{0,1},{1,0},{2,3},{3,2},{4,5},{5,4},{6,7},{7,6},{8,9},{9,8},{10,11... | collective-permute-start | bytes 2359304 | tf_op jit(solution)/shard_map/ppermute | solution.py:225
  7.3 15.2 %collective-permute-start.3 = (bf16[2,2,2,256,128]{4,3,2,1,0:T(8,128)(2,1)S(1)}, bf16[2,2,2,256,128]{4,3,2,1,0:T(8,128)(2,1)S(1)}, u32[]{:S(2)}, u32[]{:S(2)}) collective-permute-start(bf16[2,2,2,256,128]{4,3,2,1,0:T(8,128)(2,1)S(1)} %kv_for_far.2.refs_3_), channel_id=1, source_target_pairs={{0,2},{1,3},{2,0},{3,1},{4,6},{5,7},{6,4},{7,5},{8,10},{9,11},{10,... | collective-permute-start | bytes 1572872 | tf_op jit(solution)/shard_map/ppermute | solution.py:225
  11.7 27.9 %collective-permute-start.1 = (bf16[3,2,2,256,128]{4,3,2,1,0:T(8,128)(2,1)}, bf16[3,2,2,256,128]{4,3,2,1,0:T(8,128)(2,1)}, u32[]{:S(2)}, u32[]{:S(2)}) collective-permute-start(bf16[3,2,2,256,128]{4,3,2,1,0:T(8,128)(2,1)} %kv_near.1.refs_0_), channel_id=1, source_target_pairs={{0,4},{1,5},{2,6},{3,7},{4,0},{5,1},{6,2},{7,3},{8,12},{9,13},{10,... | collective-permute-start | bytes 2359304 | tf_op jit(solution)/shard_map/ppermute | solution.py:236
  13.4 27.8 %collective-permute-start.2 = (bf16[3,2,2,256,128]{4,3,2,1,0:T(8,128)(2,1)}, bf16[3,2,2,256,128]{4,3,2,1,0:T(8,128)(2,1)}, u32[]{:S(2)}, u32[]{:S(2)}) collective-permute-start(bf16[3,2,2,256,128]{4,3,2,1,0:T(8,128)(2,1)} %kv_near.1.refs_0_), channel_id=1, source_target_pairs={{0,1},{1,0},{2,3},{3,2},{4,8},{5,9},{6,10},{7,11},{8,4},{9,5},{10,... | collective-permute-start | bytes 2359304 | tf_op jit(solution)/shard_map/ppermute | solution.py:236
  23.2 9.5 %copy-start.6 = (s32[16,3]{0,1:T(4,128)S(1)}, s32[16,3]{0,1:T(4,128)}, u32[]{:S(2)}) copy-start(s32[16,3]{0,1:T(4,128)} %param.11) | copy-start | bytes 580
  23.2 9.4 %copy-start.7 = (s32[16,3]{0,1:T(4,128)S(1)}, s32[16,3]{0,1:T(4,128)}, u32[]{:S(2)}) copy-start(s32[16,3]{0,1:T(4,128)} %param.10) | copy-start | bytes 580
  23.3 8.0 %collective-permute-start.9 = (bf16[1,2,2,256,128]{4,3,2,1,0:T(8,128)(2,1)S(1)}, bf16[1,2,2,256,128]{4,3,2,1,0:T(8,128)(2,1)S(1)}, u32[]{:S(2)}, u32[]{:S(2)}) collective-permute-start(bf16[1,2,2,256,128]{4,3,2,1,0:T(8,128)(2,1)S(1)} %kv_for_far.3), channel_id=1, source_target_pairs={{0,2},{1,3},{2,0},{3,1},{4,6},{5,7},{6,4},{7,5},{8,10},{9,11},{10,... | collective-permute-start | bytes 786440 | tf_op jit(solution)/shard_map/ppermute | solution.py:225
  25.1 18.7 %collective-permute-start.4 = (bf16[2,2,2,256,128]{4,3,2,1,0:T(8,128)(2,1)S(1)}, bf16[2,2,2,256,128]{4,3,2,1,0:T(8,128)(2,1)}, u32[]{:S(2)}, u32[]{:S(2)}) collective-permute-start(bf16[2,2,2,256,128]{4,3,2,1,0:T(8,128)(2,1)S(1)} %collective-permute-done.3.refs_3_), channel_id=1, source_target_pairs={{0,4},{1,5},{2,6},{3,7},{4,0},{5,1},{6,2},{7,3},{8,12},{9,13},{10,... | collective-permute-start | bytes 1572872 | tf_op jit(solution)/shard_map/ppermute | solution.py:236
  26.6 17.1 %collective-permute-start.5 = (bf16[2,2,2,256,128]{4,3,2,1,0:T(8,128)(2,1)S(1)}, bf16[2,2,2,256,128]{4,3,2,1,0:T(8,128)(2,1)}, u32[]{:S(2)}, u32[]{:S(2)}) collective-permute-start(bf16[2,2,2,256,128]{4,3,2,1,0:T(8,128)(2,1)S(1)} %collective-permute-done.3.refs_3_), channel_id=1, source_target_pairs={{0,1},{1,0},{2,3},{3,2},{4,8},{5,9},{6,10},{7,11},{8,4},{9,5},{10,... | collective-permute-start | bytes 1572872 | tf_op jit(solution)/shard_map/ppermute | solution.py:236
  31.3 7.3 %collective-permute-start.7 = (bf16[1,2,2,256,128]{4,3,2,1,0:T(8,128)(2,1)S(1)}, bf16[1,2,2,256,128]{4,3,2,1,0:T(8,128)(2,1)}, u32[]{:S(2)}, u32[]{:S(2)}) collective-permute-start(bf16[1,2,2,256,128]{4,3,2,1,0:T(8,128)(2,1)S(1)} %qg_for_far.2), channel_id=1, source_target_pairs={{0,2},{1,3},{2,0},{3,1},{4,6},{5,7},{6,4},{7,5},{8,10},{9,11},{10,... | collective-permute-start | bytes 786440 | tf_op jit(solution)/shard_map/ppermute | solution.py:225
  38.5 13.8 %collective-permute-start.10 = (bf16[2,2,2,256,128]{4,3,2,1,0:T(8,128)(2,1)S(1)}, bf16[2,2,2,256,128]{4,3,2,1,0:T(8,128)(2,1)S(1)}, u32[]{:S(2)}, u32[]{:S(2)}) collective-permute-start(bf16[2,2,2,256,128]{4,3,2,1,0:T(8,128)(2,1)S(1)} %qg_for_far.3), channel_id=1, source_target_pairs={{0,2},{1,3},{2,0},{3,1},{4,6},{5,7},{6,4},{7,5},{8,10},{9,11},{10,... | collective-permute-start | bytes 1572872 | tf_op jit(solution)/shard_map/ppermute | solution.py:225
  39.6 19.2 %collective-permute-start.12 = (bf16[1,2,2,256,128]{4,3,2,1,0:T(8,128)(2,1)S(1)}, bf16[1,2,2,256,128]{4,3,2,1,0:T(8,128)(2,1)S(1)}, u32[]{:S(2)}, u32[]{:S(2)}) collective-permute-start(bf16[1,2,2,256,128]{4,3,2,1,0:T(8,128)(2,1)S(1)} %collective-permute-done.9.refs_3_), channel_id=1, source_target_pairs={{0,4},{1,5},{2,6},{3,7},{4,0},{5,1},{6,2},{7,3},{8,12},{9,13},{10,... | collective-permute-start | bytes 786440 | tf_op jit(solution)/shard_map/ppermute | solution.py:236
  41.2 19.8 %collective-permute-start.13 = (bf16[1,2,2,256,128]{4,3,2,1,0:T(8,128)(2,1)S(1)}, bf16[1,2,2,256,128]{4,3,2,1,0:T(8,128)(2,1)S(1)}, u32[]{:S(2)}, u32[]{:S(2)}) collective-permute-start(bf16[1,2,2,256,128]{4,3,2,1,0:T(8,128)(2,1)S(1)} %collective-permute-done.9.refs_3_), channel_id=1, source_target_pairs={{0,1},{1,0},{2,3},{3,2},{4,8},{5,9},{6,10},{7,11},{8,4},{9,5},{10,... | collective-permute-start | bytes 786440 | tf_op jit(solution)/shard_map/ppermute | solution.py:236
  49.8 16.9 %collective-permute-start.23 = (bf16[4,2,256,128]{3,2,1,0:T(8,128)(2,1)S(1)}, bf16[4,2,256,128]{3,2,1,0:T(8,128)(2,1)S(1)}, u32[]{:S(2)}, u32[]{:S(2)}) collective-permute-start(bf16[4,2,256,128]{3,2,1,0:T(8,128)(2,1)S(1)} %get-tuple-element.59), channel_id=1, source_target_pairs={{0,4},{1,5},{2,6},{3,7},{4,0},{5,1},{6,2},{7,3},{8,12},{9,13},{10,... | collective-permute-start | bytes 1572872 | tf_op jit(solution)/shard_map/ppermute | solution.py:236
  52.3 16.0 %collective-permute-start.24 = (bf16[4,2,256,128]{3,2,1,0:T(8,128)(2,1)S(1)}, bf16[4,2,256,128]{3,2,1,0:T(8,128)(2,1)S(1)}, u32[]{:S(2)}, u32[]{:S(2)}) collective-permute-start(bf16[4,2,256,128]{3,2,1,0:T(8,128)(2,1)S(1)} %get-tuple-element.60), channel_id=1, source_target_pairs={{0,1},{1,0},{2,3},{3,2},{4,8},{5,9},{6,10},{7,11},{8,4},{9,5},{10,... | collective-permute-start | bytes 1572872 | tf_op jit(solution)/shard_map/ppermute | solution.py:236
  52.3 24.5 %collective-permute-start.8 = (bf16[2,2,256,128]{3,2,1,0:T(8,128)(2,1)S(1)}, bf16[2,2,256,128]{3,2,1,0:T(8,128)(2,1)S(1)}, u32[]{:S(2)}, u32[]{:S(2)}) collective-permute-start(bf16[2,2,256,128]{3,2,1,0:T(8,128)(2,1)S(1)} %get-tuple-element.38), channel_id=1, source_target_pairs={{0,2},{1,3},{2,0},{3,1},{4,6},{5,7},{6,4},{7,5},{8,10},{9,11},{10,... | collective-permute-start | bytes 786440 | tf_op jit(solution)/shard_map/ppermute | solution.py:225
  58.8 14.7 %collective-permute-start.15 = (bf16[4,2,256,128]{3,2,1,0:T(8,128)(2,1)S(1)}, bf16[4,2,256,128]{3,2,1,0:T(8,128)(2,1)S(1)}, u32[]{:S(2)}, u32[]{:S(2)}) collective-permute-start(bf16[4,2,256,128]{3,2,1,0:T(8,128)(2,1)S(1)} %get-tuple-element.44), channel_id=1, source_target_pairs={{0,4},{1,5},{2,6},{3,7},{4,0},{5,1},{6,2},{7,3},{8,12},{9,13},{10,... | collective-permute-start | bytes 1572872 | tf_op jit(solution)/shard_map/ppermute | solution.py:236
  60.9 14.3 %collective-permute-start.16 = (bf16[4,2,256,128]{3,2,1,0:T(8,128)(2,1)S(1)}, bf16[4,2,256,128]{3,2,1,0:T(8,128)(2,1)S(1)}, u32[]{:S(2)}, u32[]{:S(2)}) collective-permute-start(bf16[4,2,256,128]{3,2,1,0:T(8,128)(2,1)S(1)} %get-tuple-element.45), channel_id=1, source_target_pairs={{0,1},{1,0},{2,3},{3,2},{4,8},{5,9},{6,10},{7,11},{8,4},{9,5},{10,... | collective-permute-start | bytes 1572872 | tf_op jit(solution)/shard_map/ppermute | solution.py:236
  66.7 10.7 %collective-permute-start.14 = (bf16[2,2,256,128]{3,2,1,0:T(8,128)(2,1)S(1)}, bf16[2,2,256,128]{3,2,1,0:T(8,128)(2,1)S(1)}, u32[]{:S(2)}, u32[]{:S(2)}) collective-permute-start(bf16[2,2,256,128]{3,2,1,0:T(8,128)(2,1)S(1)} %get-tuple-element.42), channel_id=1, source_target_pairs={{0,2},{1,3},{2,0},{3,1},{4,6},{5,7},{6,4},{7,5},{8,10},{9,11},{10,... | collective-permute-start | bytes 786440 | tf_op jit(solution)/shard_map/ppermute | solution.py:225
  68.3 13.2 %collective-permute-start.11 = (bf16[2,2,256,128]{3,2,1,0:T(8,128)(2,1)S(1)}, bf16[2,2,256,128]{3,2,1,0:T(8,128)(2,1)S(1)}, u32[]{:S(2)}, u32[]{:S(2)}) collective-permute-start(bf16[2,2,256,128]{3,2,1,0:T(8,128)(2,1)S(1)} %get-tuple-element.40), channel_id=1, source_target_pairs={{0,2},{1,3},{2,0},{3,1},{4,6},{5,7},{6,4},{7,5},{8,10},{9,11},{10,... | collective-permute-start | bytes 786440 | tf_op jit(solution)/shard_map/ppermute | solution.py:225
  73.5 20.2 %collective-permute-start.18 = (bf16[4,2,256,128]{3,2,1,0:T(8,128)(2,1)S(1)}, bf16[4,2,256,128]{3,2,1,0:T(8,128)(2,1)S(1)}, u32[]{:S(2)}, u32[]{:S(2)}) collective-permute-start(bf16[4,2,256,128]{3,2,1,0:T(8,128)(2,1)S(1)} %get-tuple-element.53), channel_id=1, source_target_pairs={{0,4},{1,5},{2,6},{3,7},{4,0},{5,1},{6,2},{7,3},{8,12},{9,13},{10,... | collective-permute-start | bytes 1572872 | tf_op jit(solution)/shard_map/ppermute | solution.py:236
  75.2 18.5 %collective-permute-start.19 = (bf16[4,2,256,128]{3,2,1,0:T(8,128)(2,1)S(1)}, bf16[4,2,256,128]{3,2,1,0:T(8,128)(2,1)S(1)}, u32[]{:S(2)}, u32[]{:S(2)}) collective-permute-start(bf16[4,2,256,128]{3,2,1,0:T(8,128)(2,1)S(1)} %get-tuple-element.54), channel_id=1, source_target_pairs={{0,1},{1,0},{2,3},{3,2},{4,8},{5,9},{6,10},{7,11},{8,4},{9,5},{10,... | collective-permute-start | bytes 1572872 | tf_op jit(solution)/shard_map/ppermute | solution.py:236
  76.8 10.3 %collective-permute-start.25 = (bf16[2,2,256,128]{3,2,1,0:T(8,128)(2,1)S(1)}, bf16[2,2,256,128]{3,2,1,0:T(8,128)(2,1)S(1)}, u32[]{:S(2)}, u32[]{:S(2)}) collective-permute-start(bf16[2,2,256,128]{3,2,1,0:T(8,128)(2,1)S(1)} %get-tuple-element.62), channel_id=1, source_target_pairs={{0,2},{1,3},{2,0},{3,1},{4,6},{5,7},{6,4},{7,5},{8,10},{9,11},{10,... | collective-permute-start | bytes 786440 | tf_op jit(solution)/shard_map/ppermute | solution.py:225
  77.4 14.9 %collective-permute-start.26 = (bf16[2,2,256,128]{3,2,1,0:T(8,128)(2,1)S(1)}, bf16[2,2,256,128]{3,2,1,0:T(8,128)(2,1)S(1)}, u32[]{:S(2)}, u32[]{:S(2)}) collective-permute-start(bf16[2,2,256,128]{3,2,1,0:T(8,128)(2,1)S(1)} %get-tuple-element.64), channel_id=1, source_target_pairs={{0,2},{1,3},{2,0},{3,1},{4,6},{5,7},{6,4},{7,5},{8,10},{9,11},{10,... | collective-permute-start | bytes 786440 | tf_op jit(solution)/shard_map/ppermute | solution.py:225
  83.1 15.3 %collective-permute-start.17 = (bf16[3,2,2,256,128]{4,3,2,1,0:T(8,128)(2,1)S(1)}, bf16[3,2,2,256,128]{4,3,2,1,0:T(8,128)(2,1)S(1)}, u32[]{:S(2)}, u32[]{:S(2)}) collective-permute-start(bf16[3,2,2,256,128]{4,3,2,1,0:T(8,128)(2,1)S(1)} %odq_near.1), channel_id=1, source_target_pairs={{0,1},{1,0},{2,3},{3,2},{4,5},{5,4},{6,7},{7,6},{8,9},{9,8},{10,11... | collective-permute-start | bytes 2359304 | tf_op jit(solution)/shard_map/ppermute | solution.py:225
  93.6 3.1 %collective-permute-start.27 = (bf16[2,2,2,256,128]{4,3,2,1,0:T(8,128)(2,1)S(1)}, bf16[2,2,2,256,128]{4,3,2,1,0:T(8,128)(2,1)S(1)}, u32[]{:S(2)}, u32[]{:S(2)}) collective-permute-start(bf16[2,2,2,256,128]{4,3,2,1,0:T(8,128)(2,1)S(1)} %dkv_near.1), channel_id=1, source_target_pairs={{0,1},{1,0},{2,3},{3,2},{4,5},{5,4},{6,7},{7,6},{8,9},{9,8},{10,11... | collective-permute-start | bytes 1572872 | tf_op jit(solution)/shard_map/ppermute | solution.py:225
  94.5 6.4 %collective-permute-start.21 = (bf16[2,256,128]{2,1,0:T(8,128)(2,1)S(1)}, bf16[2,256,128]{2,1,0:T(8,128)(2,1)S(1)}, u32[]{:S(2)}, u32[]{:S(2)}) collective-permute-start(bf16[2,256,128]{2,1,0:T(8,128)(2,1)S(1)} %get-tuple-element.71), channel_id=1, source_target_pairs={{0,2},{1,3},{2,0},{3,1},{4,6},{5,7},{6,4},{7,5},{8,10},{9,11},{10,... | collective-permute-start | bytes 393224 | tf_op jit(solution)/shard_map/ppermute | solution.py:225
  96.1 6.8 %collective-permute-start.22 = (bf16[2,256,128]{2,1,0:T(8,128)(2,1)S(1)}, bf16[2,256,128]{2,1,0:T(8,128)(2,1)S(1)}, u32[]{:S(2)}, u32[]{:S(2)}) collective-permute-start(bf16[2,256,128]{2,1,0:T(8,128)(2,1)S(1)} %get-tuple-element.70), channel_id=1, source_target_pairs={{0,3},{1,2},{2,1},{3,0},{4,7},{5,6},{6,5},{7,4},{8,11},{9,10},{10,... | collective-permute-start | bytes 393224 | tf_op jit(solution)/shard_map/ppermute | solution.py:225
  96.4 6.4 %collective-permute-start.20 = (bf16[2,256,128]{2,1,0:T(8,128)(2,1)S(1)}, bf16[2,256,128]{2,1,0:T(8,128)(2,1)S(1)}, u32[]{:S(2)}, u32[]{:S(2)}) collective-permute-start(bf16[2,256,128]{2,1,0:T(8,128)(2,1)S(1)} %get-tuple-element.56), channel_id=1, source_target_pairs={{0,1},{1,0},{2,3},{3,2},{4,5},{5,4},{6,7},{7,6},{8,9},{9,8},{10,11... | collective-permute-start | bytes 393224 | tf_op jit(solution)/shard_map/ppermute | solution.py:225
  (4 other events, 5.0 us)

commit v3 on v2

--- a/solution.py
+++ b/solution.py
@@ -14,10 +14,9 @@
 BF = jnp.bfloat16
 F32 = jnp.float32
 MIB = 1024 * 1024
-FULL = 60 * MIB
+TOKEN = (16, HEAD_DIM)
 PARAMS = pltpu.CompilerParams(vmem_limit_bytes=20 * MIB)
 ANYWHERE = pl.BlockSpec(memory_space=pl.ANY)
-IN_HBM = pl.BlockSpec(memory_space=pltpu.HBM)
 
 
 def dot_nt(a, b):
@@ -38,6 +37,10 @@
 
 def entry(index, *shape):
     return pl.BlockSpec((1,) + shape, lambda i, *_: (index,) + (0,) * len(shape))
+
+
+def part(*index):
+    return lambda i, *_: index + (0, 0, 0)
 
 
 def cost(flops, nbytes):
@@ -52,7 +55,7 @@
         self.layer = (4,) + self.piece
 
 
-def move(plan, pos, inputs, shapes, moves, name, into=(), after=(), limit=2 * MIB):
+def move(plan, pos, inputs, shapes, moves, name, into=(), after=()):
     given, kept = len(inputs), len(into)
     extra = len(after)
 
@@ -75,26 +78,26 @@
         for copy in copies:
             copy.wait()
 
-    specs = [IN_HBM if x.ndim == 2 else ANYWHERE for x in inputs] + [IN_HBM] * kept + [ANYWHERE] * extra
     return pl.pallas_call(
         kernel,
         out_shape=[jax.ShapeDtypeStruct(shape, BF) for shape in shapes],
         grid_spec=pltpu.PrefetchScalarGridSpec(
             num_scalar_prefetch=1,
             grid=(1,),
-            in_specs=specs,
-            out_specs=[IN_HBM if len(shape) == 2 else ANYWHERE for shape in shapes],
+            in_specs=[ANYWHERE] * (given + kept + extra),
+            out_specs=[ANYWHERE] * len(shapes),
             scratch_shapes=[pltpu.SemaphoreType.DMA((len(moves),))],
         ),
         input_output_aliases={1 + given + n: n for n in range(kept)},
-        compiler_params=pltpu.CompilerParams(vmem_limit_bytes=limit),
+        compiler_params=pltpu.CompilerParams(vmem_limit_bytes=2 * MIB),
         cost_estimate=cost(0, 0),
         name=name,
     )(pos, *inputs, *into, *after)
 
 
-def attend(plan, pos, table, chunk, query, grad_out, blocks):
+def attend(plan, pos, table, chunk, query, grad_out, blocks, after=()):
     tile = plan.tile
+    blocks = blocks + [(array, ANYWHERE) for array in after]
     count = len(blocks)
 
     def kernel(pos_ref, table_ref, q_ref, g_ref, *refs):
@@ -194,8 +197,13 @@
     )(pos, table, query, grad_out, *[array for array, _ in blocks])
 
 
-def owned(plan, pos, total, halos):
-    def kernel(pos_ref, total_ref, halo_a, halo_b, first, near, far):
+def owned(plan, pos, total, halos, riders=(), after=()):
+    count = len(riders)
+
+    def kernel(pos_ref, total_ref, halo_a, halo_b, *refs):
+        first, near, far = refs[-4:-1]
+        for n in range(count):
+            far[pl.ds(2 * n, 2)] = refs[n][...]
         for r in range(4):
             grads = total_ref[r]
             for n, halo in enumerate((halo_a, halo_b)):
@@ -203,22 +211,24 @@
             if r < 2:
                 (first, near)[r][...] = grads.astype(BF)
             else:
-                far[r - 2] = grads.astype(BF)
-
-    shapes = [plan.piece, plan.piece, (2,) + plan.piece]
+                far[2 * count + r - 2] = grads.astype(BF)
+
+    shapes = [plan.piece, plan.piece, (2 * count + 2,) + plan.piece]
     return pl.pallas_call(
         kernel,
-        out_shape=[jax.ShapeDtypeStruct(shape, BF) for shape in shapes],
+        out_shape=[jax.ShapeDtypeStruct(shape, BF) for shape in shapes + [TOKEN]],
         grid_spec=pltpu.PrefetchScalarGridSpec(
             num_scalar_prefetch=1,
             grid=(1,),
-            in_specs=[full(plan.layer)] * 3,
-            out_specs=[full(shape) for shape in shapes],
+            in_specs=[full(plan.layer)] * 3
+            + [full((2,) + plan.piece)] * count
+            + [ANYWHERE] * len(after),
+            out_specs=[full(shape) for shape in shapes] + [ANYWHERE],
         ),
         compiler_params=PARAMS,
-        cost_estimate=cost(0, 20 * 4 * plan.tile * HEAD_DIM),
+        cost_estimate=cost(0, 0),
         name="owned",
-    )(pos, total, *halos)
+    )(pos, total, *halos, *riders, *after)
 
 
 def swap(value, r):
@@ -264,42 +274,54 @@
             moves += pick(2, c, 0, n, 0)
             moves.append((2, (per + c,), 0, (n, 1)))
         shapes = [(len(group), 2) + piece]
-        return move(plan, pos, [*pair, got], shapes, moves, name, after=after)[0]
+        return swap(move(plan, pos, [*pair, got], shapes, moves, name, after=after)[0], 2)
 
     kv_got = for_near(here, "kv_for_near")
-    qg_got = for_near(there, "qg_for_near")
-    kv_parts, qg_parts = [every[:-1], every[-1:]], [every[:1], every[1:]]
-    message = for_far(here, kv_got, kv_parts[0], "kv_for_far")
-    far = [swap(message, 2)]
     moves = [m for c in every for m in pick(0, c, 0, c, 0)]
     moves += [(2, (c,), 0, (c, 1)) for c in every]
-    near = move(plan, pos, [*here, kv_got], [(per, 2) + piece], moves, "kv_near", after=[message])[0]
-    nears = [near] + [exchange(near, turn) for turn in range(2)]
-    far.append(swap(for_far(here, kv_got, kv_parts[1], "kv_for_far", after=far[:1]), 2))
+    own = move(plan, pos, [*here, kv_got], [(per, 2) + piece], moves, "kv_near")[0]
+    nears = [own] + [exchange(own, turn) for turn in range(2)]
+    kv_parts, qg_parts = [every[:-1], every[-1:]], [every[:1], every[1:]]
+    far = [for_far(here, kv_got, kv_parts[0], "kv_for_far", after=[own])]
+    qg_got = for_near(there, "qg_for_near")
+    qg_fars = [for_far(there, qg_got, qg_parts[0], "qg_for_far", after=far)]
+    far.append(for_far(here, kv_got, kv_parts[1], "kv_for_far", after=far))
+    qg_fars.append(for_far(there, qg_got, qg_parts[1], "qg_for_far", after=far[1:]))
     fars = [[m] + [exchange(m, turn) for turn in range(2)] for m in far]
-    qg_fars = [
-        swap(for_far(there, qg_got, part, "qg_for_far", after=far[n : n + 1]), 2)
-        for n, part in enumerate(qg_parts)
-    ]
-
-    odq, dkv = [], []
-    for c in chunks:
+
+    odq, sums = [], []
+    for c in every:
         pair = (2,) + piece
+        k, q = int(c not in kv_parts[0]), int(c not in qg_parts[0])
         blocks = [(array, entry(c, *pair)) for array in nears]
-        for arrays, parts in ((fars, kv_parts), ([[x] for x in qg_fars], qg_parts)):
-            n = 0 if c in parts[0] else 1
-            blocks += [(array, entry(c - parts[n][0], *pair)) for array in arrays[n]]
-        blocks.insert(6, (qg_got, entry(c, *piece)))
-        *mine, halo_a, halo_b, total = attend(plan, pos, table, c, query, grad_out, blocks)
-        odq.append(mine[:2] + [swap(mine[2], 2)])
+        blocks += [(array, entry(c - kv_parts[k][0], *pair)) for array in fars[k]]
+        blocks += [(qg_got, entry(c, *piece)), (qg_fars[q], entry(c - qg_parts[q][0], *pair))]
+        wait = [odq[0][2][0]] if c == every[-1] else []
+        *mine, halo_a, halo_b, total = attend(
+            plan, pos, table, c, query, grad_out, blocks, after=wait
+        )
+        if c < every[-1]:
+            mine[2] = [swap(mine[2], 2), 0]
+        odq.append(mine)
         halos = [exchange(halo, turn) for turn, halo in enumerate((halo_a, halo_b))]
-        dkv.append(owned(plan, pos, total, halos))
-
-    def onward(group, name, after=()):
-        moves = []
-        for c in range(len(group)):
-            moves += [(2 * c, (), 0, (c, 0)), (2 * c + 1, (1,), 0, (c, 1))]
-        inputs = [x for _, near, far in group for x in (near, far)]
+        sums.append((total, halos))
+    dkv, tokens = [], []
+    for c in every:
+        riders = [odq[-1][2]] if c == 0 else []
+        wait = [odq[-2][2][0]] if c == 0 else []
+        first, near, far, token = owned(plan, pos, *sums[c], riders, wait)
+        if c < every[-1]:
+            far = swap(far, 2)
+        if c == 0:
+            odq[-1][2] = [far, 0]
+        dkv.append([first, near, [far, 2 * len(riders)]])
+        tokens.append(token)
+
+    def onward(group, name, after):
+        moves, inputs = [], []
+        for c, (_, near, (far, at)) in enumerate(group):
+            moves += [(2 * c, (), 0, (c, 0)), (2 * c + 1, (at + 1,), 0, (c, 1))]
+            inputs += [near, far]
         shapes = [(len(group), 2) + piece]
         return swap(move(plan, pos, inputs, shapes, moves, name, after=after)[0], 1)
 
@@ -312,22 +334,21 @@
 
     def spread(group, got):
         inputs, where = [got], []
-        for c, (first, _, far) in enumerate(group):
+        for c, (first, _, (far, at)) in enumerate(group):
             where += [(0, (c, 0), 1, c), (0, (c, 1), 3, c)]
-            where += [(len(inputs), (), 0, c), (len(inputs) + 1, (0,), 2, c)]
+            where += [(len(inputs), (), 0, c), (len(inputs) + 1, (at,), 2, c)]
             inputs += [first, far]
         return inputs, where
 
-    inputs, where = spread(odq, onward(odq, "odq_near", [dkv[-2][0]]))
-    attended, query_grad = move(plan, pos, inputs, shapes, columns(where), "odq_out")
-
-    early = [[first, near, swap(far, 2)] for first, near, far in dkv[:-1]]
-    inputs, where = spread(early, onward(early, "dkv_near"))
+    inputs, where = spread(odq, onward(odq, "odq_near", tokens[-2:-1]))
+    attended, query_grad, token = move(plan, pos, inputs, shapes + [TOKEN], columns(where), "odq_out")
+
+    inputs, where = spread(dkv[:-1], onward(dkv[:-1], "dkv_near", tokens[-1:]))
     grads = move(plan, pos, inputs, shapes, columns(where), "dkv_early")
-    first, near, far = dkv[-1]
+    first, near, (far, _) = dkv[-1]
     inputs = [first, swap(near, 1), swap(far[0], 2), swap(far[1], 3)]
     where = [(r, (), r, per - 1) for r in range(4)]
-    key_grad, value_grad = move(plan, pos, inputs, shapes, columns(where), "dkv_out", into=grads)
+    key_grad, value_grad = move(plan, pos, inputs, shapes, columns(where), "dkv_out", into=grads, after=[token])
     return attended, query_grad, key_grad, value_grad
 
 

time: 106 us -> 101 us (0.953)
  waiting for transfers between devices: 39.8 us -> 34.2 us
  starting transfers between devices: 26.6 us -> 27.9 us
    ppermute x12, waiting for transfers between devices: 7.29 us -> 2.76 us  [exchange(): return lax.ppermute(value, ('seq', 'head'), pairs)]
    ppermute x16 -> x15, waiting for transfers between devices: 32.5 us -> 31.5 us  [swap(): return lax.ppermute(value, 'head', [(i, i ^ r) for i in range(4)])]
    ppermute x16 -> x15, starting transfers between devices: 15.3 us -> 16.2 us  [swap(): return lax.ppermute(value, 'head', [(i, i ^ r) for i in range(4)])]
  transfers between devices with their start and end apart: 28 -> 27, of which waited for: 11 -> 11; matrix products, arithmetic and copies ran while one was open for 0% -> 0% of each run, Pallas kernels for 31% -> 32%
where the time goes in v3:
time: 101 us; the launch traced here: 100 us
  Pallas kernels  34.6 us (34%)
  waiting for transfers between devices  34.2 us (34%)
  starting transfers between devices  27.9 us (28%)
  local copies, waits for them, and re-layouts  2.49 us (2%)
    ppermute x15, waiting for transfers between devices, swap(): return lax.ppermute(value, 'head', [(i, i ^ r) for i in range(4)])  31.5 us
    pallas_call x3, Pallas kernels, attend(): pl.pallas_call(kernel, out_shape=[jax.ShapeDtypeStruct(shape, BF) for sha...  17.5 us
    ppermute x15, starting transfers between devices, swap(): return lax.ppermute(value, 'head', [(i, i ^ r) for i in range(4)])  16.2 us
    pallas_call x12, Pallas kernels, move(): pl.pallas_call(kernel, out_shape=[jax.ShapeDtypeStruct(shape, BF) for sha...  14.7 us
    ppermute x12, starting transfers between devices, exchange(): return lax.ppermute(value, ('seq', 'head'), pairs)  11.7 us
    ppermute x12, waiting for transfers between devices, exchange(): return lax.ppermute(value, ('seq', 'head'), pairs)  2.76 us
    pallas_call x3, Pallas kernels, owned(): pl.pallas_call(kernel, out_shape=[jax.ShapeDtypeStruct(shape, BF) for sha...  2.33 us
    unnamed x16, local copies, waits for them, and re-layouts  2.3 us
  transfers between devices with their start and end apart: 27, of which 11 were waited for; matrix products, arithmetic and copies ran while one was open for 0% of the time, Pallas kernels for 32%

profile of v3, /device:TPU:0, one launch (start us, length us, event | category | flops | bytes accessed | tf_op | source)
XLA Modules:
  0.0 100.2 jit_solution(13011635239704992446)
XLA Ops:
  0.7 1.1 %copy-done = bf16[256,1536]{1,0:T(8,128)(2,1)S(1)} copy-done((bf16[256,1536]{1,0:T(8,128)(2,1)S(1)}, bf16[256,1536]{1,0:T(8,128)(2,1)}, u32[]{:S(2)}) %copy-start) | copy-done | bytes 786456
  6.3 1.2 %kv_near.1.refs_3_.refs_0_ = bf16[3,2,2,256,128]{4,3,2,1,0:T(8,128)(2,1)S(1)} custom-call(s32[4]{0:T(128)S(1)} %pad_add_fusion.1.pos_ref, bf16[256,1536]{1,0:T(8,128)(2,1)S(1)} %copy-done.1, bf16[256,1536]{1,0:T(8,128)(2,1)S(1)} %copy-done.3, bf16[6,2,256,128]{3,2,1,0:T(8,128)(2,1)S(1)} %collective-permute-done.refs_2_), custom_call_target="tpu_custom_call" | custom-call | tf_op jit(solution)/shard_map/kv_near/pallas_call | solution.py:81
  8.5 2.9 %collective-permute-start.3 = (bf16[2,2,2,256,128]{4,3,2,1,0:T(8,128)(2,1)S(1)}, bf16[2,2,2,256,128]{4,3,2,1,0:T(8,128)(2,1)}, u32[]{:S(2)}, u32[]{:S(2)}) collective-permute-start(bf16[2,2,2,256,128]{4,3,2,1,0:T(8,128)(2,1)S(1)} %kv_for_far.2), channel_id=1, source_target_pairs={{0,2},{1,3},{2,0},{3,1},{4,6},{5,7},{6,4},{7,5},{8,10},{9,11},{10,... | collective-permute-start | bytes 1572872 | tf_op jit(solution)/shard_map/ppermute | solution.py:235
  11.5 1.6 %collective-permute-start.1 = (bf16[3,2,2,256,128]{4,3,2,1,0:T(8,128)(2,1)S(1)}, bf16[3,2,2,256,128]{4,3,2,1,0:T(8,128)(2,1)}, u32[]{:S(2)}, u32[]{:S(2)}) collective-permute-start(bf16[3,2,2,256,128]{4,3,2,1,0:T(8,128)(2,1)S(1)} %kv_near.1.refs_3_.refs_0_), channel_id=1, source_target_pairs={{0,4},{1,5},{2,6},{3,7},{4,0},{5,1},{6,2},{7,3},{8,12},{9,13},{10,... | collective-permute-start | bytes 2359304 | tf_op jit(solution)/shard_map/ppermute | solution.py:246
  13.0 10.8 %collective-permute-done.3.refs_3_ = bf16[2,2,2,256,128]{4,3,2,1,0:T(8,128)(2,1)} collective-permute-done((bf16[2,2,2,256,128]{4,3,2,1,0:T(8,128)(2,1)S(1)}, bf16[2,2,2,256,128]{4,3,2,1,0:T(8,128)(2,1)}, u32[]{:S(2)}, u32[]{:S(2)}) %collective-permute-start.3) | collective-permute-done | bytes 524320 | tf_op jit(solution)/shard_map/ppermute | solution.py:235
  24.6 1.8 %collective-permute-start.9 = (bf16[1,2,2,256,128]{4,3,2,1,0:T(8,128)(2,1)S(1)}, bf16[1,2,2,256,128]{4,3,2,1,0:T(8,128)(2,1)S(1)}, u32[]{:S(2)}, u32[]{:S(2)}) collective-permute-start(bf16[1,2,2,256,128]{4,3,2,1,0:T(8,128)(2,1)S(1)} %kv_for_far.3), channel_id=1, source_target_pairs={{0,2},{1,3},{2,0},{3,1},{4,6},{5,7},{6,4},{7,5},{8,10},{9,11},{10,... | collective-permute-start | bytes 786440 | tf_op jit(solution)/shard_map/ppermute | solution.py:235
  26.4 1.6 %collective-permute-start.4 = (bf16[2,2,2,256,128]{4,3,2,1,0:T(8,128)(2,1)}, bf16[2,2,2,256,128]{4,3,2,1,0:T(8,128)(2,1)}, u32[]{:S(2)}, u32[]{:S(2)}) collective-permute-start(bf16[2,2,2,256,128]{4,3,2,1,0:T(8,128)(2,1)} %collective-permute-done.3.refs_3_), channel_id=1, source_target_pairs={{0,4},{1,5},{2,6},{3,7},{4,0},{5,1},{6,2},{7,3},{8,12},{9,13},{10,... | collective-permute-start | bytes 1572872 | tf_op jit(solution)/shard_map/ppermute | solution.py:246
  28.0 1.3 %qg_for_far.2 = bf16[1,2,2,256,128]{4,3,2,1,0:T(8,128)(2,1)} custom-call(s32[4]{0:T(128)S(1)} %pad_add_fusion.1.pos_ref, bf16[256,1536]{1,0:T(8,128)(2,1)S(1)} %copy-done.4, bf16[256,1536]{1,0:T(8,128)(2,1)S(1)} %copy-done.5, bf16[6,2,256,128]{3,2,1,0:T(8,128)(2,1)S(1)} %collective-permute-done.6.refs_2_.refs_6_, ...), custom_call_target="tpu_custom_call" | custom-call | tf_op jit(solution)/shard_map/qg_for_far/pallas_call | solution.py:81
  29.3 3.2 %collective-permute-done.9.refs_3_ = bf16[1,2,2,256,128]{4,3,2,1,0:T(8,128)(2,1)S(1)} collective-permute-done((bf16[1,2,2,256,128]{4,3,2,1,0:T(8,128)(2,1)S(1)}, bf16[1,2,2,256,128]{4,3,2,1,0:T(8,128)(2,1)S(1)}, u32[]{:S(2)}, u32[]{:S(2)}) %collective-permute-start.9) | collective-permute-done | bytes 262176 | tf_op jit(solution)/shard_map/ppermute | solution.py:235
  32.5 1.4 %collective-permute-start.7 = (bf16[1,2,2,256,128]{4,3,2,1,0:T(8,128)(2,1)}, bf16[1,2,2,256,128]{4,3,2,1,0:T(8,128)(2,1)}, u32[]{:S(2)}, u32[]{:S(2)}) collective-permute-start(bf16[1,2,2,256,128]{4,3,2,1,0:T(8,128)(2,1)} %qg_for_far.2), channel_id=1, source_target_pairs={{0,2},{1,3},{2,0},{3,1},{4,6},{5,7},{6,4},{7,5},{8,10},{9,11},{10,... | collective-permute-start | bytes 786440 | tf_op jit(solution)/shard_map/ppermute | solution.py:235
  35.1 4.7 %collective-permute-done.7.refs_7_ = bf16[1,2,2,256,128]{4,3,2,1,0:T(8,128)(2,1)} collective-permute-done((bf16[1,2,2,256,128]{4,3,2,1,0:T(8,128)(2,1)}, bf16[1,2,2,256,128]{4,3,2,1,0:T(8,128)(2,1)}, u32[]{:S(2)}, u32[]{:S(2)}) %collective-permute-start.7) | collective-permute-done | bytes 262176 | tf_op jit(solution)/shard_map/ppermute | solution.py:235
  40.9 1.6 %collective-permute-start.12 = (bf16[1,2,2,256,128]{4,3,2,1,0:T(8,128)(2,1)S(1)}, bf16[1,2,2,256,128]{4,3,2,1,0:T(8,128)(2,1)S(1)}, u32[]{:S(2)}, u32[]{:S(2)}) collective-permute-start(bf16[1,2,2,256,128]{4,3,2,1,0:T(8,128)(2,1)S(1)} %collective-permute-done.9.refs_3_), channel_id=1, source_target_pairs={{0,4},{1,5},{2,6},{3,7},{4,0},{5,1},{6,2},{7,3},{8,12},{9,13},{10,... | collective-permute-start | bytes 786440 | tf_op jit(solution)/shard_map/ppermute | solution.py:246
  43.2 6.0 %attend.3 = (bf16[2,256,128]{2,1,0:T(8,128)(2,1)S(1)}, bf16[2,256,128]{2,1,0:T(8,128)(2,1)S(1)}, bf16[2,2,256,128]{3,2,1,0:T(8,128)(2,1)S(1)}, bf16[4,2,256,128]...) custom-call(s32[4]{0:T(128)S(1)} %pad_add_fusion.1.pos_ref, ...), custom_call_target="tpu_custom_call" | custom-call | flops 6039797760 | bytes 5242880 | tf_op jit(solution)/shard_map/attend/pallas_call | solution.py:178
  49.3 2.8 %collective-permute-start.14 = (bf16[4,2,256,128]{3,2,1,0:T(8,128)(2,1)S(1)}, bf16[4,2,256,128]{3,2,1,0:T(8,128)(2,1)S(1)}, u32[]{:S(2)}, u32[]{:S(2)}) collective-permute-start(bf16[4,2,256,128]{3,2,1,0:T(8,128)(2,1)S(1)} %get-tuple-element.46), channel_id=1, source_target_pairs={{0,4},{1,5},{2,6},{3,7},{4,0},{5,1},{6,2},{7,3},{8,12},{9,13},{10,... | collective-permute-start | bytes 1572872 | tf_op jit(solution)/shard_map/ppermute | solution.py:246
  52.1 5.9 %attend.4 = (bf16[2,256,128]{2,1,0:T(8,128)(2,1)S(1)}, bf16[2,256,128]{2,1,0:T(8,128)(2,1)S(1)}, bf16[2,2,256,128]{3,2,1,0:T(8,128)(2,1)S(1)}, bf16[4,2,256,128]...) custom-call(s32[4]{0:T(128)S(1)} %pad_add_fusion.1.pos_ref, ...), custom_call_target="tpu_custom_call" | custom-call | flops 6039797760 | bytes 5242880 | tf_op jit(solution)/shard_map/attend/pallas_call | solution.py:178
  58.0 2.4 %collective-permute-start.17 = (bf16[4,2,256,128]{3,2,1,0:T(8,128)(2,1)S(1)}, bf16[4,2,256,128]{3,2,1,0:T(8,128)(2,1)S(1)}, u32[]{:S(2)}, u32[]{:S(2)}) collective-permute-start(bf16[4,2,256,128]{3,2,1,0:T(8,128)(2,1)S(1)} %get-tuple-element.51), channel_id=1, source_target_pairs={{0,4},{1,5},{2,6},{3,7},{4,0},{5,1},{6,2},{7,3},{8,12},{9,13},{10,... | collective-permute-start | bytes 1572872 | tf_op jit(solution)/shard_map/ppermute | solution.py:246
  60.4 1.6 %collective-permute-start.11 = (bf16[2,2,256,128]{3,2,1,0:T(8,128)(2,1)S(1)}, bf16[2,2,256,128]{3,2,1,0:T(8,128)(2,1)S(1)}, u32[]{:S(2)}, u32[]{:S(2)}) collective-permute-start(bf16[2,2,256,128]{3,2,1,0:T(8,128)(2,1)S(1)} %get-tuple-element.43), channel_id=1, source_target_pairs={{0,2},{1,3},{2,0},{3,1},{4,6},{5,7},{6,4},{7,5},{8,10},{9,11},{10,... | collective-permute-start | bytes 786440 | tf_op jit(solution)/shard_map/ppermute | solution.py:235
  61.9 5.7 %attend.5 = (bf16[2,256,128]{2,1,0:T(8,128)(2,1)S(1)}, bf16[2,256,128]{2,1,0:T(8,128)(2,1)S(1)}, bf16[2,2,256,128]{3,2,1,0:T(8,128)(2,1)S(1)}, bf16[4,2,256,128]...) custom-call(s32[4]{0:T(128)S(1)} %pad_add_fusion.1.pos_ref, ...), custom_call_target="tpu_custom_call" | custom-call | flops 6039797760 | bytes 5242880 | tf_op jit(solution)/shard_map/attend/pallas_call | solution.py:178
  67.6 1.5 %collective-permute-done.11.refs_1_.refs_3_.refs_4_ = bf16[2,2,256,128]{3,2,1,0:T(8,128)(2,1)S(1)} collective-permute-done((bf16[2,2,256,128]{3,2,1,0:T(8,128)(2,1)S(1)}, bf16[2,2,256,128]{3,2,1,0:T(8,128)(2,1)S(1)}, u32[]{:S(2)}, u32[]{:S(2)}) %collective-permute-start.11) | collective-permute-done | bytes 262176 | tf_op jit(solution)/shard_map/ppermute | solution.py:235
  69.9 1.6 %collective-permute-start.16 = (bf16[4,2,256,128]{3,2,1,0:T(8,128)(2,1)S(1)}, bf16[4,2,256,128]{3,2,1,0:T(8,128)(2,1)S(1)}, u32[]{:S(2)}, u32[]{:S(2)}) collective-permute-start(bf16[4,2,256,128]{3,2,1,0:T(8,128)(2,1)S(1)} %get-tuple-element.49), channel_id=1, source_target_pairs={{0,2},{1,3},{2,0},{3,1},{4,6},{5,7},{6,4},{7,5},{8,10},{9,11},{10,... | collective-permute-start | bytes 1572872 | tf_op jit(solution)/shard_map/ppermute | solution.py:235
  71.4 1.9 %collective-permute-start.20 = (bf16[4,2,256,128]{3,2,1,0:T(8,128)(2,1)S(1)}, bf16[4,2,256,128]{3,2,1,0:T(8,128)(2,1)S(1)}, u32[]{:S(2)}, u32[]{:S(2)}) collective-permute-start(bf16[4,2,256,128]{3,2,1,0:T(8,128)(2,1)S(1)} %get-tuple-element.60), channel_id=1, source_target_pairs={{0,4},{1,5},{2,6},{3,7},{4,0},{5,1},{6,2},{7,3},{8,12},{9,13},{10,... | collective-permute-start | bytes 1572872 | tf_op jit(solution)/shard_map/ppermute | solution.py:246
  73.3 2.0 %collective-permute-done.17.halo_a = bf16[4,2,256,128]{3,2,1,0:T(8,128)(2,1)S(1)} collective-permute-done((bf16[4,2,256,128]{3,2,1,0:T(8,128)(2,1)S(1)}, bf16[4,2,256,128]{3,2,1,0:T(8,128)(2,1)S(1)}, u32[]{:S(2)}, u32[]{:S(2)}) %collective-permute-start.17) | collective-permute-done | bytes 524320 | tf_op jit(solution)/shard_map/ppermute | solution.py:246
  76.1 2.4 %collective-permute-start.25 = (bf16[2,2,256,128]{3,2,1,0:T(8,128)(2,1)S(1)}, bf16[2,2,256,128]{3,2,1,0:T(8,128)(2,1)S(1)}, u32[]{:S(2)}, u32[]{:S(2)}) collective-permute-start(bf16[2,2,256,128]{3,2,1,0:T(8,128)(2,1)S(1)} %get-tuple-element.67), channel_id=1, source_target_pairs={{0,2},{1,3},{2,0},{3,1},{4,6},{5,7},{6,4},{7,5},{8,10},{9,11},{10,... | collective-permute-start | bytes 786440 | tf_op jit(solution)/shard_map/ppermute | solution.py:235
  78.5 6.3 %collective-permute-done.16.refs_5_.refs_6_.refs_1_.refs_2_ = bf16[4,2,256,128]{3,2,1,0:T(8,128)(2,1)S(1)} collective-permute-done((bf16[4,2,256,128]{3,2,1,0:T(8,128)(2,1)S(1)}, bf16[4,2,256,128]{3,2,1,0:T(8,128)(2,1)S(1)}, u32[]{:S(2)}, u32[]{:S(2)}) %collective-permute-start.16) | collective-permute-done | bytes 524320 | tf_op jit(solution)/shard_map/ppermute | solution.py:235
  84.8 1.6 %odq_near.1 = bf16[3,2,2,256,128]{4,3,2,1,0:T(8,128)(2,1)S(1)} custom-call(s32[4]{0:T(128)S(1)} %pad_add_fusion.1.pos_ref, bf16[2,256,128]{2,1,0:T(8,128)(2,1)S(1)} %get-tuple-element.40.refs_0_, bf16[2,2,256,128]{3,2,1,0:T(8,128)(2,1)S(1)} %collective-permute-done.8.refs_8_.refs_1_.refs_2_, bf16[2,256,128]{2,1,0:T(8,128)(2,1)S(1)} %get-tuple-element.42.refs_2_, ...), custom_call_target="tpu_custom_call" | custom-call | tf_op jit(solution)/shard_map/odq_near/pallas_call | solution.py:81
  87.3 1.8 %collective-permute-done.25.refs_3_.refs_4_ = bf16[2,2,256,128]{3,2,1,0:T(8,128)(2,1)S(1)} collective-permute-done((bf16[2,2,256,128]{3,2,1,0:T(8,128)(2,1)S(1)}, bf16[2,2,256,128]{3,2,1,0:T(8,128)(2,1)S(1)}, u32[]{:S(2)}, u32[]{:S(2)}) %collective-permute-start.25) | collective-permute-done | bytes 262176 | tf_op jit(solution)/shard_map/ppermute | solution.py:235
  89.0 1.3 %dkv_near.1 = bf16[2,2,2,256,128]{4,3,2,1,0:T(8,128)(2,1)S(1)} custom-call(s32[4]{0:T(128)S(1)} %pad_add_fusion.1.pos_ref, bf16[2,256,128]{2,1,0:T(8,128)(2,1)S(1)} %get-tuple-element.65.refs_0_, bf16[4,2,256,128]{3,2,1,0:T(8,128)(2,1)S(1)} %collective-permute-done.16.refs_5_.refs_6_.refs_1_.refs_2_, bf16[2,256,128]{2,1,0:T(8,128)(2,1)S(1)} %get-tuple-element.66.refs_2_, ...), custom_call_target="tpu_custom_call" | custom-call | tf_op jit(solution)/shard_map/dkv_near/pallas_call | solution.py:81
  90.4 1.6 %collective-permute-start.23 = (bf16[2,256,128]{2,1,0:T(8,128)(2,1)S(1)}, bf16[2,256,128]{2,1,0:T(8,128)(2,1)S(1)}, u32[]{:S(2)}, u32[]{:S(2)}) collective-permute-start(bf16[2,256,128]{2,1,0:T(8,128)(2,1)S(1)} %get-tuple-element.77), channel_id=1, source_target_pairs={{0,2},{1,3},{2,0},{3,1},{4,6},{5,7},{6,4},{7,5},{8,10},{9,11},{10,... | collective-permute-start | bytes 393224 | tf_op jit(solution)/shard_map/ppermute | solution.py:235
  92.6 1.6 %dkv_early.1 = (bf16[256,1536]{1,0:T(8,128)(2,1)}, bf16[256,1536]{1,0:T(8,128)(2,1)}) custom-call(s32[4]{0:T(128)S(1)} %pad_add_fusion.1.pos_ref, bf16[2,2,2,256,128]{4,3,2,1,0:T(8,128)(2,1)S(1)} %collective-permute-done.26.refs_0_, bf16[2,256,128]{2,1,0:T(8,128)(2,1)S(1)} %get-tuple-element.69.refs_1_, ...), custom_call_target="tpu_custom_call" | custom-call | tf_op jit(solution)/shard_map/dkv_early/pallas_call | solution.py:81
  94.3 1.9 %odq_out.1 = (bf16[256,1536]{1,0:T(8,128)(2,1)}, bf16[256,1536]{1,0:T(8,128)(2,1)}, bf16[16,128]{1,0:T(8,128)(2,1)S(1)}) custom-call(s32[4]{0:T(128)S(1)} %pad_add_fusion.1.pos_ref, bf16[3,2,2,256,128]{4,3,2,1,0:T(8,128)(2,1)S(1)} %collective-permute-done.19.refs_0_, bf16[2,256,128]{2,1,0:T(8,128)(2,1)S(1)} %get-tuple-element.54.refs_1_, ...), custom_call_target="tpu_custom_call" | custom-call | tf_op jit(solution)/shard_map/odq_out/pallas_call | solution.py:81
  96.8 2.0 %collective-permute-done.24.refs_3_ = bf16[2,256,128]{2,1,0:T(8,128)(2,1)S(1)} collective-permute-done((bf16[2,256,128]{2,1,0:T(8,128)(2,1)S(1)}, bf16[2,256,128]{2,1,0:T(8,128)(2,1)S(1)}, u32[]{:S(2)}, u32[]{:S(2)}) %collective-permute-start.24) | collective-permute-done | bytes 131104 | tf_op jit(solution)/shard_map/ppermute | solution.py:235
  98.8 1.4 %dkv_out.1 = (bf16[256,1536]{1,0:T(8,128)(2,1)}, bf16[256,1536]{1,0:T(8,128)(2,1)}) custom-call(s32[4]{0:T(128)S(1)} %pad_add_fusion.1.pos_ref, bf16[2,256,128]{2,1,0:T(8,128)(2,1)S(1)} %get-tuple-element.62.refs_0_, bf16[2,256,128]{2,1,0:T(8,128)(2,1)S(1)} %collective-permute-done.22.refs_1_, ...), custom_call_target="tpu_custom_call", output_to_operand_aliasing={{0}: (5, {}), {1}: (6, {})} | custom-call | tf_op jit(solution)/shard_map/dkv_out/pallas_call | solution.py:81
  (61 shorter events, 13.1 us)
Async XLA Ops:
  3.0 1.4 %copy-start.5 = (bf16[256,1536]{1,0:T(8,128)(2,1)S(1)}, bf16[256,1536]{1,0:T(8,128)(2,1)}, u32[]{:S(2)}) copy-start(bf16[256,1536]{1,0:T(8,128)(2,1)} %g_ref.5) | copy-start | bytes 2359300
  3.8 2.5 %copy-start.1 = (bf16[256,1536]{1,0:T(8,128)(2,1)S(1)}, bf16[256,1536]{1,0:T(8,128)(2,1)}, u32[]{:S(2)}) copy-start(bf16[256,1536]{1,0:T(8,128)(2,1)} %refs_0_.12) | copy-start | bytes 2359300
  3.9 2.4 %copy-start.3 = (bf16[256,1536]{1,0:T(8,128)(2,1)S(1)}, bf16[256,1536]{1,0:T(8,128)(2,1)}, u32[]{:S(2)}) copy-start(bf16[256,1536]{1,0:T(8,128)(2,1)} %refs_1_.12) | copy-start | bytes 2359300
  3.9 2.4 %collective-permute-start = (bf16[6,2,256,128]{3,2,1,0:T(8,128)(2,1)S(1)}, bf16[6,2,256,128]{3,2,1,0:T(8,128)(2,1)S(1)}, u32[]{:S(2)}, u32[]{:S(2)}) collective-permute-start(bf16[6,2,256,128]{3,2,1,0:T(8,128)(2,1)S(1)} %kv_for_near.1), channel_id=1, source_target_pairs={{0,1},{1,0},{2,3},{3,2},{4,5},{5,4},{6,7},{7,6},{8,9},{9,8},{10,11... | collective-permute-start | bytes 2359304 | tf_op jit(solution)/shard_map/ppermute | solution.py:235
  5.2 22.8 %collective-permute-start.6 = (bf16[6,2,256,128]{3,2,1,0:T(8,128)(2,1)S(1)}, bf16[6,2,256,128]{3,2,1,0:T(8,128)(2,1)S(1)}, u32[]{:S(2)}, u32[]{:S(2)}) collective-permute-start(bf16[6,2,256,128]{3,2,1,0:T(8,128)(2,1)S(1)} %qg_for_near.1), channel_id=1, source_target_pairs={{0,1},{1,0},{2,3},{3,2},{4,5},{5,4},{6,7},{7,6},{8,9},{9,8},{10,11... | collective-permute-start | bytes 2359304 | tf_op jit(solution)/shard_map/ppermute | solution.py:235
  8.5 15.3 %collective-permute-start.3 = (bf16[2,2,2,256,128]{4,3,2,1,0:T(8,128)(2,1)S(1)}, bf16[2,2,2,256,128]{4,3,2,1,0:T(8,128)(2,1)}, u32[]{:S(2)}, u32[]{:S(2)}) collective-permute-start(bf16[2,2,2,256,128]{4,3,2,1,0:T(8,128)(2,1)S(1)} %kv_for_far.2), channel_id=1, source_target_pairs={{0,2},{1,3},{2,0},{3,1},{4,6},{5,7},{6,4},{7,5},{8,10},{9,11},{10,... | collective-permute-start | bytes 1572872 | tf_op jit(solution)/shard_map/ppermute | solution.py:235
  11.5 29.5 %collective-permute-start.1 = (bf16[3,2,2,256,128]{4,3,2,1,0:T(8,128)(2,1)S(1)}, bf16[3,2,2,256,128]{4,3,2,1,0:T(8,128)(2,1)}, u32[]{:S(2)}, u32[]{:S(2)}) collective-permute-start(bf16[3,2,2,256,128]{4,3,2,1,0:T(8,128)(2,1)S(1)} %kv_near.1.refs_3_.refs_0_), channel_id=1, source_target_pairs={{0,4},{1,5},{2,6},{3,7},{4,0},{5,1},{6,2},{7,3},{8,12},{9,13},{10,... | collective-permute-start | bytes 2359304 | tf_op jit(solution)/shard_map/ppermute | solution.py:246
  13.0 29.5 %collective-permute-start.2 = (bf16[3,2,2,256,128]{4,3,2,1,0:T(8,128)(2,1)S(1)}, bf16[3,2,2,256,128]{4,3,2,1,0:T(8,128)(2,1)}, u32[]{:S(2)}, u32[]{:S(2)}) collective-permute-start(bf16[3,2,2,256,128]{4,3,2,1,0:T(8,128)(2,1)S(1)} %kv_near.1.refs_3_.refs_0_), channel_id=1, source_target_pairs={{0,1},{1,0},{2,3},{3,2},{4,8},{5,9},{6,10},{7,11},{8,4},{9,5},{10,... | collective-permute-start | bytes 2359304 | tf_op jit(solution)/shard_map/ppermute | solution.py:246
  24.6 9.4 %copy-start.6 = (s32[16,3]{0,1:T(4,128)S(1)}, s32[16,3]{0,1:T(4,128)}, u32[]{:S(2)}) copy-start(s32[16,3]{0,1:T(4,128)} %param.11) | copy-start | bytes 580
  24.6 9.3 %copy-start.7 = (s32[16,3]{0,1:T(4,128)S(1)}, s32[16,3]{0,1:T(4,128)}, u32[]{:S(2)}) copy-start(s32[16,3]{0,1:T(4,128)} %param.10) | copy-start | bytes 580
  24.6 7.9 %collective-permute-start.9 = (bf16[1,2,2,256,128]{4,3,2,1,0:T(8,128)(2,1)S(1)}, bf16[1,2,2,256,128]{4,3,2,1,0:T(8,128)(2,1)S(1)}, u32[]{:S(2)}, u32[]{:S(2)}) collective-permute-start(bf16[1,2,2,256,128]{4,3,2,1,0:T(8,128)(2,1)S(1)} %kv_for_far.3), channel_id=1, source_target_pairs={{0,2},{1,3},{2,0},{3,1},{4,6},{5,7},{6,4},{7,5},{8,10},{9,11},{10,... | collective-permute-start | bytes 786440 | tf_op jit(solution)/shard_map/ppermute | solution.py:235
  26.4 16.8 %collective-permute-start.4 = (bf16[2,2,2,256,128]{4,3,2,1,0:T(8,128)(2,1)}, bf16[2,2,2,256,128]{4,3,2,1,0:T(8,128)(2,1)}, u32[]{:S(2)}, u32[]{:S(2)}) collective-permute-start(bf16[2,2,2,256,128]{4,3,2,1,0:T(8,128)(2,1)} %collective-permute-done.3.refs_3_), channel_id=1, source_target_pairs={{0,4},{1,5},{2,6},{3,7},{4,0},{5,1},{6,2},{7,3},{8,12},{9,13},{10,... | collective-permute-start | bytes 1572872 | tf_op jit(solution)/shard_map/ppermute | solution.py:246
  28.0 15.3 %collective-permute-start.5 = (bf16[2,2,2,256,128]{4,3,2,1,0:T(8,128)(2,1)}, bf16[2,2,2,256,128]{4,3,2,1,0:T(8,128)(2,1)}, u32[]{:S(2)}, u32[]{:S(2)}) collective-permute-start(bf16[2,2,2,256,128]{4,3,2,1,0:T(8,128)(2,1)} %collective-permute-done.3.refs_3_), channel_id=1, source_target_pairs={{0,1},{1,0},{2,3},{3,2},{4,8},{5,9},{6,10},{7,11},{8,4},{9,5},{10,... | collective-permute-start | bytes 1572872 | tf_op jit(solution)/shard_map/ppermute | solution.py:246
  32.5 7.4 %collective-permute-start.7 = (bf16[1,2,2,256,128]{4,3,2,1,0:T(8,128)(2,1)}, bf16[1,2,2,256,128]{4,3,2,1,0:T(8,128)(2,1)}, u32[]{:S(2)}, u32[]{:S(2)}) collective-permute-start(bf16[1,2,2,256,128]{4,3,2,1,0:T(8,128)(2,1)} %qg_for_far.2), channel_id=1, source_target_pairs={{0,2},{1,3},{2,0},{3,1},{4,6},{5,7},{6,4},{7,5},{8,10},{9,11},{10,... | collective-permute-start | bytes 786440 | tf_op jit(solution)/shard_map/ppermute | solution.py:235
  39.9 12.2 %collective-permute-start.10 = (bf16[2,2,2,256,128]{4,3,2,1,0:T(8,128)(2,1)S(1)}, bf16[2,2,2,256,128]{4,3,2,1,0:T(8,128)(2,1)S(1)}, u32[]{:S(2)}, u32[]{:S(2)}) collective-permute-start(bf16[2,2,2,256,128]{4,3,2,1,0:T(8,128)(2,1)S(1)} %qg_for_far.3), channel_id=1, source_target_pairs={{0,2},{1,3},{2,0},{3,1},{4,6},{5,7},{6,4},{7,5},{8,10},{9,11},{10,... | collective-permute-start | bytes 1572872 | tf_op jit(solution)/shard_map/ppermute | solution.py:235
  40.9 17.0 %collective-permute-start.12 = (bf16[1,2,2,256,128]{4,3,2,1,0:T(8,128)(2,1)S(1)}, bf16[1,2,2,256,128]{4,3,2,1,0:T(8,128)(2,1)S(1)}, u32[]{:S(2)}, u32[]{:S(2)}) collective-permute-start(bf16[1,2,2,256,128]{4,3,2,1,0:T(8,128)(2,1)S(1)} %collective-permute-done.9.refs_3_), channel_id=1, source_target_pairs={{0,4},{1,5},{2,6},{3,7},{4,0},{5,1},{6,2},{7,3},{8,12},{9,13},{10,... | collective-permute-start | bytes 786440 | tf_op jit(solution)/shard_map/ppermute | solution.py:246
  42.5 17.8 %collective-permute-start.13 = (bf16[1,2,2,256,128]{4,3,2,1,0:T(8,128)(2,1)S(1)}, bf16[1,2,2,256,128]{4,3,2,1,0:T(8,128)(2,1)S(1)}, u32[]{:S(2)}, u32[]{:S(2)}) collective-permute-start(bf16[1,2,2,256,128]{4,3,2,1,0:T(8,128)(2,1)S(1)} %collective-permute-done.9.refs_3_), channel_id=1, source_target_pairs={{0,1},{1,0},{2,3},{3,2},{4,8},{5,9},{6,10},{7,11},{8,4},{9,5},{10,... | collective-permute-start | bytes 786440 | tf_op jit(solution)/shard_map/ppermute | solution.py:246
  49.2 11.1 %collective-permute-start.8 = (bf16[2,2,256,128]{3,2,1,0:T(8,128)(2,1)S(1)}, bf16[2,2,256,128]{3,2,1,0:T(8,128)(2,1)S(1)}, u32[]{:S(2)}, u32[]{:S(2)}) collective-permute-start(bf16[2,2,256,128]{3,2,1,0:T(8,128)(2,1)S(1)} %get-tuple-element.41), channel_id=1, source_target_pairs={{0,2},{1,3},{2,0},{3,1},{4,6},{5,7},{6,4},{7,5},{8,10},{9,11},{10,... | collective-permute-start | bytes 786440 | tf_op jit(solution)/shard_map/ppermute | solution.py:235
  49.3 19.8 %collective-permute-start.14 = (bf16[4,2,256,128]{3,2,1,0:T(8,128)(2,1)S(1)}, bf16[4,2,256,128]{3,2,1,0:T(8,128)(2,1)S(1)}, u32[]{:S(2)}, u32[]{:S(2)}) collective-permute-start(bf16[4,2,256,128]{3,2,1,0:T(8,128)(2,1)S(1)} %get-tuple-element.46), channel_id=1, source_target_pairs={{0,4},{1,5},{2,6},{3,7},{4,0},{5,1},{6,2},{7,3},{8,12},{9,13},{10,... | collective-permute-start | bytes 1572872 | tf_op jit(solution)/shard_map/ppermute | solution.py:246
  52.1 17.0 %collective-permute-start.15 = (bf16[4,2,256,128]{3,2,1,0:T(8,128)(2,1)S(1)}, bf16[4,2,256,128]{3,2,1,0:T(8,128)(2,1)S(1)}, u32[]{:S(2)}, u32[]{:S(2)}) collective-permute-start(bf16[4,2,256,128]{3,2,1,0:T(8,128)(2,1)S(1)} %get-tuple-element.47), channel_id=1, source_target_pairs={{0,1},{1,0},{2,3},{3,2},{4,8},{5,9},{6,10},{7,11},{8,4},{9,5},{10,... | collective-permute-start | bytes 1572872 | tf_op jit(solution)/shard_map/ppermute | solution.py:246
  58.0 17.4 %collective-permute-start.17 = (bf16[4,2,256,128]{3,2,1,0:T(8,128)(2,1)S(1)}, bf16[4,2,256,128]{3,2,1,0:T(8,128)(2,1)S(1)}, u32[]{:S(2)}, u32[]{:S(2)}) collective-permute-start(bf16[4,2,256,128]{3,2,1,0:T(8,128)(2,1)S(1)} %get-tuple-element.51), channel_id=1, source_target_pairs={{0,4},{1,5},{2,6},{3,7},{4,0},{5,1},{6,2},{7,3},{8,12},{9,13},{10,... | collective-permute-start | bytes 1572872 | tf_op jit(solution)/shard_map/ppermute | solution.py:246
  60.4 15.0 %collective-permute-start.18 = (bf16[4,2,256,128]{3,2,1,0:T(8,128)(2,1)S(1)}, bf16[4,2,256,128]{3,2,1,0:T(8,128)(2,1)S(1)}, u32[]{:S(2)}, u32[]{:S(2)}) collective-permute-start(bf16[4,2,256,128]{3,2,1,0:T(8,128)(2,1)S(1)} %get-tuple-element.52), channel_id=1, source_target_pairs={{0,1},{1,0},{2,3},{3,2},{4,8},{5,9},{6,10},{7,11},{8,4},{9,5},{10,... | collective-permute-start | bytes 1572872 | tf_op jit(solution)/shard_map/ppermute | solution.py:246
  60.4 8.7 %collective-permute-start.11 = (bf16[2,2,256,128]{3,2,1,0:T(8,128)(2,1)S(1)}, bf16[2,2,256,128]{3,2,1,0:T(8,128)(2,1)S(1)}, u32[]{:S(2)}, u32[]{:S(2)}) collective-permute-start(bf16[2,2,256,128]{3,2,1,0:T(8,128)(2,1)S(1)} %get-tuple-element.43), channel_id=1, source_target_pairs={{0,2},{1,3},{2,0},{3,1},{4,6},{5,7},{6,4},{7,5},{8,10},{9,11},{10,... | collective-permute-start | bytes 786440 | tf_op jit(solution)/shard_map/ppermute | solution.py:235
  69.9 14.9 %collective-permute-start.16 = (bf16[4,2,256,128]{3,2,1,0:T(8,128)(2,1)S(1)}, bf16[4,2,256,128]{3,2,1,0:T(8,128)(2,1)S(1)}, u32[]{:S(2)}, u32[]{:S(2)}) collective-permute-start(bf16[4,2,256,128]{3,2,1,0:T(8,128)(2,1)S(1)} %get-tuple-element.49), channel_id=1, source_target_pairs={{0,2},{1,3},{2,0},{3,1},{4,6},{5,7},{6,4},{7,5},{8,10},{9,11},{10,... | collective-permute-start | bytes 1572872 | tf_op jit(solution)/shard_map/ppermute | solution.py:235
  71.4 15.0 %collective-permute-start.20 = (bf16[4,2,256,128]{3,2,1,0:T(8,128)(2,1)S(1)}, bf16[4,2,256,128]{3,2,1,0:T(8,128)(2,1)S(1)}, u32[]{:S(2)}, u32[]{:S(2)}) collective-permute-start(bf16[4,2,256,128]{3,2,1,0:T(8,128)(2,1)S(1)} %get-tuple-element.60), channel_id=1, source_target_pairs={{0,4},{1,5},{2,6},{3,7},{4,0},{5,1},{6,2},{7,3},{8,12},{9,13},{10,... | collective-permute-start | bytes 1572872 | tf_op jit(solution)/shard_map/ppermute | solution.py:246
  73.3 13.2 %collective-permute-start.21 = (bf16[4,2,256,128]{3,2,1,0:T(8,128)(2,1)S(1)}, bf16[4,2,256,128]{3,2,1,0:T(8,128)(2,1)S(1)}, u32[]{:S(2)}, u32[]{:S(2)}) collective-permute-start(bf16[4,2,256,128]{3,2,1,0:T(8,128)(2,1)S(1)} %get-tuple-element.61), channel_id=1, source_target_pairs={{0,1},{1,0},{2,3},{3,2},{4,8},{5,9},{6,10},{7,11},{8,4},{9,5},{10,... | collective-permute-start | bytes 1572872 | tf_op jit(solution)/shard_map/ppermute | solution.py:246
  76.1 12.9 %collective-permute-start.25 = (bf16[2,2,256,128]{3,2,1,0:T(8,128)(2,1)S(1)}, bf16[2,2,256,128]{3,2,1,0:T(8,128)(2,1)S(1)}, u32[]{:S(2)}, u32[]{:S(2)}) collective-permute-start(bf16[2,2,256,128]{3,2,1,0:T(8,128)(2,1)S(1)} %get-tuple-element.67), channel_id=1, source_target_pairs={{0,2},{1,3},{2,0},{3,1},{4,6},{5,7},{6,4},{7,5},{8,10},{9,11},{10,... | collective-permute-start | bytes 786440 | tf_op jit(solution)/shard_map/ppermute | solution.py:235
  86.4 7.9 %collective-permute-start.19 = (bf16[3,2,2,256,128]{4,3,2,1,0:T(8,128)(2,1)S(1)}, bf16[3,2,2,256,128]{4,3,2,1,0:T(8,128)(2,1)S(1)}, u32[]{:S(2)}, u32[]{:S(2)}) collective-permute-start(bf16[3,2,2,256,128]{4,3,2,1,0:T(8,128)(2,1)S(1)} %odq_near.1), channel_id=1, source_target_pairs={{0,1},{1,0},{2,3},{3,2},{4,5},{5,4},{6,7},{7,6},{8,9},{9,8},{10,11... | collective-permute-start | bytes 2359304 | tf_op jit(solution)/shard_map/ppermute | solution.py:235
  90.3 2.3 %collective-permute-start.26 = (bf16[2,2,2,256,128]{4,3,2,1,0:T(8,128)(2,1)S(1)}, bf16[2,2,2,256,128]{4,3,2,1,0:T(8,128)(2,1)S(1)}, u32[]{:S(2)}, u32[]{:S(2)}) collective-permute-start(bf16[2,2,2,256,128]{4,3,2,1,0:T(8,128)(2,1)S(1)} %dkv_near.1), channel_id=1, source_target_pairs={{0,1},{1,0},{2,3},{3,2},{4,5},{5,4},{6,7},{7,6},{8,9},{9,8},{10,11... | collective-permute-start | bytes 1572872 | tf_op jit(solution)/shard_map/ppermute | solution.py:235
  90.4 6.4 %collective-permute-start.23 = (bf16[2,256,128]{2,1,0:T(8,128)(2,1)S(1)}, bf16[2,256,128]{2,1,0:T(8,128)(2,1)S(1)}, u32[]{:S(2)}, u32[]{:S(2)}) collective-permute-start(bf16[2,256,128]{2,1,0:T(8,128)(2,1)S(1)} %get-tuple-element.77), channel_id=1, source_target_pairs={{0,2},{1,3},{2,0},{3,1},{4,6},{5,7},{6,4},{7,5},{8,10},{9,11},{10,... | collective-permute-start | bytes 393224 | tf_op jit(solution)/shard_map/ppermute | solution.py:235
  92.0 6.8 %collective-permute-start.24 = (bf16[2,256,128]{2,1,0:T(8,128)(2,1)S(1)}, bf16[2,256,128]{2,1,0:T(8,128)(2,1)S(1)}, u32[]{:S(2)}, u32[]{:S(2)}) collective-permute-start(bf16[2,256,128]{2,1,0:T(8,128)(2,1)S(1)} %get-tuple-element.76), channel_id=1, source_target_pairs={{0,3},{1,2},{2,1},{3,0},{4,7},{5,6},{6,5},{7,4},{8,11},{9,10},{10,... | collective-permute-start | bytes 393224 | tf_op jit(solution)/shard_map/ppermute | solution.py:235
  92.3 6.5 %collective-permute-start.22 = (bf16[2,256,128]{2,1,0:T(8,128)(2,1)S(1)}, bf16[2,256,128]{2,1,0:T(8,128)(2,1)S(1)}, u32[]{:S(2)}, u32[]{:S(2)}) collective-permute-start(bf16[2,256,128]{2,1,0:T(8,128)(2,1)S(1)} %get-tuple-element.63), channel_id=1, source_target_pairs={{0,1},{1,0},{2,3},{3,2},{4,5},{5,4},{6,7},{7,6},{8,9},{9,8},{10,11... | collective-permute-start | bytes 393224 | tf_op jit(solution)/shard_map/ppermute | solution.py:235
  (3 other events, 3.6 us)

commit v4 on v3

--- a/solution.py
+++ b/solution.py
@@ -104,14 +104,10 @@
         nears, fars = refs[:3], refs[3:6]
         qg_near, qg_far = refs[6:8]
         first, near, far, halo_a, halo_b, sum_ref = refs[count : count + 6]
-        kv, qgs, odq, acc = refs[count + 6 :]
+        kv, acc = refs[count + 6 :]
         for n in range(3):
             kv[pl.ds(4 * n, 2)] = nears[n][0]
             kv[pl.ds(4 * n + 2, 2)] = fars[n][0]
-        qgs[0, 0] = q_ref[...]
-        qgs[0, 1] = g_ref[...]
-        qgs[1] = qg_near[0]
-        qgs[pl.ds(2, 2)] = qg_far[0]
         acc[...] = jnp.zeros_like(acc)
         seq, me = pos_ref[0], pos_ref[1]
 
@@ -120,9 +116,9 @@
             turn = jnp.where((rel // 4 > 1) ^ (seq % 2 > 0), 1, 2)
             return jnp.where(rel // 4 == 1, 0, turn) * 4 + ((rel % 4) ^ me)
 
-        def work(r, places):
-            q, g = qgs[r, 0], qgs[r, 1]
+        def work(q, g, places, bias, out):
             scores = [dot_nt(kv[p, 0], q) * SCALE for p in places]
+            scores = scores[:1] + [s + b for s, b in zip(scores[1:], bias)]
             peak = functools.reduce(
                 jnp.maximum, [jnp.max(s, axis=0, keepdims=True) for s in scores]
             )
@@ -141,33 +137,22 @@
                 dq_t = dq_t + dot_tn(kv[p, 0], sgrad)
                 acc[p, 0] += dot_nn(sgrad, q)
                 acc[p, 1] += dot_nn(low, g)
-            odq[r, 0] = att_t.T.astype(BF)
-            odq[r, 1] = dq_t.T.astype(BF)
-
-        def step(r, carry):
+            out[0] = att_t.T.astype(BF)
+            out[1] = dq_t.T.astype(BF)
+
+        tiles = [
+            (q_ref[...], g_ref[...], first),
+            (qg_near[0, 0], qg_near[0, 1], near),
+            (qg_far[0, 0, 0], qg_far[0, 0, 1], far.at[0]),
+            (qg_far[0, 1, 0], qg_far[0, 1, 1], far.at[1]),
+        ]
+        for r, (q, g, out) in enumerate(tiles):
             row = (seq * 4 + (r ^ me)) * 2 * SLOTS
-            live = [table_ref[row + SLOTS + n] > 0 for n in range(SLOTS)]
-            spots = [place(table_ref[row + n]) for n in range(SLOTS)]
-            second = jnp.where(live[1], spots[1], spots[2])
-
-            @pl.when(live[1] & live[2])
-            def _():
-                work(r, [spots[0], spots[1], spots[2]])
-
-            @pl.when(live[1] ^ live[2])
-            def _():
-                work(r, [spots[0], second])
-
-            @pl.when(jnp.logical_not(live[1] | live[2]))
-            def _():
-                work(r, [spots[0]])
-
-            return carry
-
-        lax.fori_loop(0, 4, step, 0)
-        first[...] = odq[0]
-        near[...] = odq[1]
-        far[...] = odq[pl.ds(2, 2)]
+            places = [r] + [place(table_ref[row + n]) for n in range(1, SLOTS)]
+            bias = [
+                jnp.where(table_ref[row + SLOTS + n] > 0, 0.0, -jnp.inf) for n in range(1, SLOTS)
+            ]
+            work(q, g, places, bias, out)
         sum_ref[...] = acc[pl.ds(0, 4)]
         halo_a[...] = acc[pl.ds(4, 4)].astype(BF)
         halo_b[...] = acc[pl.ds(8, 4)].astype(BF)
@@ -186,8 +171,6 @@
             out_specs=[full(shape) for shape in shapes + [plan.layer]],
             scratch_shapes=[
                 pltpu.VMEM((12,) + plan.piece, BF),
-                pltpu.VMEM(plan.layer, BF),
-                pltpu.VMEM(plan.layer, BF),
                 pltpu.VMEM((12,) + plan.piece, F32),
             ],
         ),

time: 101 us -> 101 us (level)
  no operation moved by 1% of the time
where the time goes in v4:
time: 101 us
  Pallas kernels  34.9 us (35%)
  waiting for transfers between devices  34 us (34%)
  starting transfers between devices  28.3 us (28%)
  local copies, waits for them, and re-layouts  2.49 us (2%)
  between operations  1.08 us (1%)
    ppermute x15, waiting for transfers between devices, swap(): return lax.ppermute(value, 'head', [(i, i ^ r) for i in range(4)])  31.8 us
    pallas_call x3, Pallas kernels, attend(): pl.pallas_call(kernel, out_shape=[jax.ShapeDtypeStruct(shape, BF) for sha...  17.9 us
    ppermute x15, starting transfers between devices, swap(): return lax.ppermute(value, 'head', [(i, i ^ r) for i in range(4)])  17.1 us
    pallas_call x12, Pallas kernels, move(): pl.pallas_call(kernel, out_shape=[jax.ShapeDtypeStruct(shape, BF) for sha...  14.7 us
    ppermute x12, starting transfers between devices, exchange(): return lax.ppermute(value, ('seq', 'head'), pairs)  11.2 us
    pallas_call x3, Pallas kernels, owned(): pl.pallas_call(kernel, out_shape=[jax.ShapeDtypeStruct(shape, BF) for sha...  2.33 us
    unnamed x16, local copies, waits for them, and re-layouts  2.3 us
    ppermute x12, waiting for transfers between devices, exchange(): return lax.ppermute(value, ('seq', 'head'), pairs)  2.24 us
  transfers between devices with their start and end apart: 27, of which 11 were waited for; matrix products, arithmetic and copies ran while one was open for 0% of the time, Pallas kernels for 32%

profile of v4, /device:TPU:0, one launch (start us, length us, event | category | flops | bytes accessed | tf_op | source)
XLA Modules:
  0.0 100.9 jit_solution(19651393188507975)
XLA Ops:
  0.7 1.1 %copy-done = bf16[256,1536]{1,0:T(8,128)(2,1)S(1)} copy-done((bf16[256,1536]{1,0:T(8,128)(2,1)S(1)}, bf16[256,1536]{1,0:T(8,128)(2,1)}, u32[]{:S(2)}) %copy-start) | copy-done | bytes 786456
  1.9 1.1 %copy-done.2 = bf16[256,1536]{1,0:T(8,128)(2,1)S(1)} copy-done((bf16[256,1536]{1,0:T(8,128)(2,1)S(1)}, bf16[256,1536]{1,0:T(8,128)(2,1)}, u32[]{:S(2)}) %copy-start.2) | copy-done | bytes 786456
  6.3 1.2 %kv_near.1.refs_3_.refs_0_ = bf16[3,2,2,256,128]{4,3,2,1,0:T(8,128)(2,1)S(1)} custom-call(s32[4]{0:T(128)S(1)} %pad_add_fusion.1.pos_ref, bf16[256,1536]{1,0:T(8,128)(2,1)S(1)} %copy-done.1, bf16[256,1536]{1,0:T(8,128)(2,1)S(1)} %copy-done.3, bf16[6,2,256,128]{3,2,1,0:T(8,128)(2,1)S(1)} %collective-permute-done.refs_2_), custom_call_target="tpu_custom_call" | custom-call | tf_op jit(solution)/shard_map/kv_near/pallas_call | solution.py:81
  8.5 2.9 %collective-permute-start.3 = (bf16[2,2,2,256,128]{4,3,2,1,0:T(8,128)(2,1)S(1)}, bf16[2,2,2,256,128]{4,3,2,1,0:T(8,128)(2,1)}, u32[]{:S(2)}, u32[]{:S(2)}) collective-permute-start(bf16[2,2,2,256,128]{4,3,2,1,0:T(8,128)(2,1)S(1)} %kv_for_far.2), channel_id=1, source_target_pairs={{0,2},{1,3},{2,0},{3,1},{4,6},{5,7},{6,4},{7,5},{8,10},{9,11},{10,... | collective-permute-start | bytes 1572872 | tf_op jit(solution)/shard_map/ppermute | solution.py:218
  11.5 1.6 %collective-permute-start.1 = (bf16[3,2,2,256,128]{4,3,2,1,0:T(8,128)(2,1)S(1)}, bf16[3,2,2,256,128]{4,3,2,1,0:T(8,128)(2,1)}, u32[]{:S(2)}, u32[]{:S(2)}) collective-permute-start(bf16[3,2,2,256,128]{4,3,2,1,0:T(8,128)(2,1)S(1)} %kv_near.1.refs_3_.refs_0_), channel_id=1, source_target_pairs={{0,4},{1,5},{2,6},{3,7},{4,0},{5,1},{6,2},{7,3},{8,12},{9,13},{10,... | collective-permute-start | bytes 2359304 | tf_op jit(solution)/shard_map/ppermute | solution.py:229
  13.0 10.8 %collective-permute-done.3.refs_3_ = bf16[2,2,2,256,128]{4,3,2,1,0:T(8,128)(2,1)} collective-permute-done((bf16[2,2,2,256,128]{4,3,2,1,0:T(8,128)(2,1)S(1)}, bf16[2,2,2,256,128]{4,3,2,1,0:T(8,128)(2,1)}, u32[]{:S(2)}, u32[]{:S(2)}) %collective-permute-start.3) | collective-permute-done | bytes 524320 | tf_op jit(solution)/shard_map/ppermute | solution.py:218
  24.6 1.8 %collective-permute-start.9 = (bf16[1,2,2,256,128]{4,3,2,1,0:T(8,128)(2,1)S(1)}, bf16[1,2,2,256,128]{4,3,2,1,0:T(8,128)(2,1)S(1)}, u32[]{:S(2)}, u32[]{:S(2)}) collective-permute-start(bf16[1,2,2,256,128]{4,3,2,1,0:T(8,128)(2,1)S(1)} %kv_for_far.3), channel_id=1, source_target_pairs={{0,2},{1,3},{2,0},{3,1},{4,6},{5,7},{6,4},{7,5},{8,10},{9,11},{10,... | collective-permute-start | bytes 786440 | tf_op jit(solution)/shard_map/ppermute | solution.py:218
  26.4 1.6 %collective-permute-start.4 = (bf16[2,2,2,256,128]{4,3,2,1,0:T(8,128)(2,1)}, bf16[2,2,2,256,128]{4,3,2,1,0:T(8,128)(2,1)}, u32[]{:S(2)}, u32[]{:S(2)}) collective-permute-start(bf16[2,2,2,256,128]{4,3,2,1,0:T(8,128)(2,1)} %collective-permute-done.3.refs_3_), channel_id=1, source_target_pairs={{0,4},{1,5},{2,6},{3,7},{4,0},{5,1},{6,2},{7,3},{8,12},{9,13},{10,... | collective-permute-start | bytes 1572872 | tf_op jit(solution)/shard_map/ppermute | solution.py:229
  28.0 1.3 %qg_for_far.2 = bf16[1,2,2,256,128]{4,3,2,1,0:T(8,128)(2,1)} custom-call(s32[4]{0:T(128)S(1)} %pad_add_fusion.1.pos_ref, bf16[256,1536]{1,0:T(8,128)(2,1)S(1)} %copy-done.4, bf16[256,1536]{1,0:T(8,128)(2,1)S(1)} %copy-done.5, bf16[6,2,256,128]{3,2,1,0:T(8,128)(2,1)S(1)} %collective-permute-done.6.refs_2_.refs_6_, ...), custom_call_target="tpu_custom_call" | custom-call | tf_op jit(solution)/shard_map/qg_for_far/pallas_call | solution.py:81
  29.3 3.2 %collective-permute-done.9.refs_3_ = bf16[1,2,2,256,128]{4,3,2,1,0:T(8,128)(2,1)S(1)} collective-permute-done((bf16[1,2,2,256,128]{4,3,2,1,0:T(8,128)(2,1)S(1)}, bf16[1,2,2,256,128]{4,3,2,1,0:T(8,128)(2,1)S(1)}, u32[]{:S(2)}, u32[]{:S(2)}) %collective-permute-start.9) | collective-permute-done | bytes 262176 | tf_op jit(solution)/shard_map/ppermute | solution.py:218
  32.5 1.4 %collective-permute-start.7 = (bf16[1,2,2,256,128]{4,3,2,1,0:T(8,128)(2,1)}, bf16[1,2,2,256,128]{4,3,2,1,0:T(8,128)(2,1)}, u32[]{:S(2)}, u32[]{:S(2)}) collective-permute-start(bf16[1,2,2,256,128]{4,3,2,1,0:T(8,128)(2,1)} %qg_for_far.2), channel_id=1, source_target_pairs={{0,2},{1,3},{2,0},{3,1},{4,6},{5,7},{6,4},{7,5},{8,10},{9,11},{10,... | collective-permute-start | bytes 786440 | tf_op jit(solution)/shard_map/ppermute | solution.py:218
  35.1 4.7 %collective-permute-done.7.refs_7_ = bf16[1,2,2,256,128]{4,3,2,1,0:T(8,128)(2,1)} collective-permute-done((bf16[1,2,2,256,128]{4,3,2,1,0:T(8,128)(2,1)}, bf16[1,2,2,256,128]{4,3,2,1,0:T(8,128)(2,1)}, u32[]{:S(2)}, u32[]{:S(2)}) %collective-permute-start.7) | collective-permute-done | bytes 262176 | tf_op jit(solution)/shard_map/ppermute | solution.py:218
  40.9 1.6 %collective-permute-start.12 = (bf16[1,2,2,256,128]{4,3,2,1,0:T(8,128)(2,1)S(1)}, bf16[1,2,2,256,128]{4,3,2,1,0:T(8,128)(2,1)S(1)}, u32[]{:S(2)}, u32[]{:S(2)}) collective-permute-start(bf16[1,2,2,256,128]{4,3,2,1,0:T(8,128)(2,1)S(1)} %collective-permute-done.9.refs_3_), channel_id=1, source_target_pairs={{0,4},{1,5},{2,6},{3,7},{4,0},{5,1},{6,2},{7,3},{8,12},{9,13},{10,... | collective-permute-start | bytes 786440 | tf_op jit(solution)/shard_map/ppermute | solution.py:229
  43.2 6.0 %attend.3 = (bf16[2,256,128]{2,1,0:T(8,128)(2,1)S(1)}, bf16[2,256,128]{2,1,0:T(8,128)(2,1)S(1)}, bf16[2,2,256,128]{3,2,1,0:T(8,128)(2,1)S(1)}, bf16[4,2,256,128]...) custom-call(s32[4]{0:T(128)S(1)} %pad_add_fusion.1.pos_ref, ...), custom_call_target="tpu_custom_call" | custom-call | flops 6039797760 | bytes 5242880 | tf_op jit(solution)/shard_map/attend/pallas_call | solution.py:163
  49.4 3.2 %collective-permute-start.14 = (bf16[4,2,256,128]{3,2,1,0:T(8,128)(2,1)S(1)}, bf16[4,2,256,128]{3,2,1,0:T(8,128)(2,1)S(1)}, u32[]{:S(2)}, u32[]{:S(2)}) collective-permute-start(bf16[4,2,256,128]{3,2,1,0:T(8,128)(2,1)S(1)} %get-tuple-element.46), channel_id=1, source_target_pairs={{0,4},{1,5},{2,6},{3,7},{4,0},{5,1},{6,2},{7,3},{8,12},{9,13},{10,... | collective-permute-start | bytes 1572872 | tf_op jit(solution)/shard_map/ppermute | solution.py:229
  52.6 6.0 %attend.4 = (bf16[2,256,128]{2,1,0:T(8,128)(2,1)S(1)}, bf16[2,256,128]{2,1,0:T(8,128)(2,1)S(1)}, bf16[2,2,256,128]{3,2,1,0:T(8,128)(2,1)S(1)}, bf16[4,2,256,128]...) custom-call(s32[4]{0:T(128)S(1)} %pad_add_fusion.1.pos_ref, ...), custom_call_target="tpu_custom_call" | custom-call | flops 6039797760 | bytes 5242880 | tf_op jit(solution)/shard_map/attend/pallas_call | solution.py:163
  58.6 2.1 %collective-permute-start.17 = (bf16[4,2,256,128]{3,2,1,0:T(8,128)(2,1)S(1)}, bf16[4,2,256,128]{3,2,1,0:T(8,128)(2,1)S(1)}, u32[]{:S(2)}, u32[]{:S(2)}) collective-permute-start(bf16[4,2,256,128]{3,2,1,0:T(8,128)(2,1)S(1)} %get-tuple-element.51), channel_id=1, source_target_pairs={{0,4},{1,5},{2,6},{3,7},{4,0},{5,1},{6,2},{7,3},{8,12},{9,13},{10,... | collective-permute-start | bytes 1572872 | tf_op jit(solution)/shard_map/ppermute | solution.py:229
  60.7 1.9 %collective-permute-start.11 = (bf16[2,2,256,128]{3,2,1,0:T(8,128)(2,1)S(1)}, bf16[2,2,256,128]{3,2,1,0:T(8,128)(2,1)S(1)}, u32[]{:S(2)}, u32[]{:S(2)}) collective-permute-start(bf16[2,2,256,128]{3,2,1,0:T(8,128)(2,1)S(1)} %get-tuple-element.43), channel_id=1, source_target_pairs={{0,2},{1,3},{2,0},{3,1},{4,6},{5,7},{6,4},{7,5},{8,10},{9,11},{10,... | collective-permute-start | bytes 786440 | tf_op jit(solution)/shard_map/ppermute | solution.py:218
  62.6 5.9 %attend.5 = (bf16[2,256,128]{2,1,0:T(8,128)(2,1)S(1)}, bf16[2,256,128]{2,1,0:T(8,128)(2,1)S(1)}, bf16[2,2,256,128]{3,2,1,0:T(8,128)(2,1)S(1)}, bf16[4,2,256,128]...) custom-call(s32[4]{0:T(128)S(1)} %pad_add_fusion.1.pos_ref, ...), custom_call_target="tpu_custom_call" | custom-call | flops 6039797760 | bytes 5242880 | tf_op jit(solution)/shard_map/attend/pallas_call | solution.py:163
  70.3 1.8 %collective-permute-start.16 = (bf16[4,2,256,128]{3,2,1,0:T(8,128)(2,1)S(1)}, bf16[4,2,256,128]{3,2,1,0:T(8,128)(2,1)S(1)}, u32[]{:S(2)}, u32[]{:S(2)}) collective-permute-start(bf16[4,2,256,128]{3,2,1,0:T(8,128)(2,1)S(1)} %get-tuple-element.49), channel_id=1, source_target_pairs={{0,2},{1,3},{2,0},{3,1},{4,6},{5,7},{6,4},{7,5},{8,10},{9,11},{10,... | collective-permute-start | bytes 1572872 | tf_op jit(solution)/shard_map/ppermute | solution.py:218
  72.1 1.2 %collective-permute-start.20 = (bf16[4,2,256,128]{3,2,1,0:T(8,128)(2,1)S(1)}, bf16[4,2,256,128]{3,2,1,0:T(8,128)(2,1)S(1)}, u32[]{:S(2)}, u32[]{:S(2)}) collective-permute-start(bf16[4,2,256,128]{3,2,1,0:T(8,128)(2,1)S(1)} %get-tuple-element.60), channel_id=1, source_target_pairs={{0,4},{1,5},{2,6},{3,7},{4,0},{5,1},{6,2},{7,3},{8,12},{9,13},{10,... | collective-permute-start | bytes 1572872 | tf_op jit(solution)/shard_map/ppermute | solution.py:229
  73.3 1.5 %collective-permute-done.17.halo_a = bf16[4,2,256,128]{3,2,1,0:T(8,128)(2,1)S(1)} collective-permute-done((bf16[4,2,256,128]{3,2,1,0:T(8,128)(2,1)S(1)}, bf16[4,2,256,128]{3,2,1,0:T(8,128)(2,1)S(1)}, u32[]{:S(2)}, u32[]{:S(2)}) %collective-permute-start.17) | collective-permute-done | bytes 524320 | tf_op jit(solution)/shard_map/ppermute | solution.py:229
  75.6 2.7 %collective-permute-start.25 = (bf16[2,2,256,128]{3,2,1,0:T(8,128)(2,1)S(1)}, bf16[2,2,256,128]{3,2,1,0:T(8,128)(2,1)S(1)}, u32[]{:S(2)}, u32[]{:S(2)}) collective-permute-start(bf16[2,2,256,128]{3,2,1,0:T(8,128)(2,1)S(1)} %get-tuple-element.67), channel_id=1, source_target_pairs={{0,2},{1,3},{2,0},{3,1},{4,6},{5,7},{6,4},{7,5},{8,10},{9,11},{10,... | collective-permute-start | bytes 786440 | tf_op jit(solution)/shard_map/ppermute | solution.py:218
  78.2 7.0 %collective-permute-done.16.refs_5_.refs_6_.refs_1_.refs_2_ = bf16[4,2,256,128]{3,2,1,0:T(8,128)(2,1)S(1)} collective-permute-done((bf16[4,2,256,128]{3,2,1,0:T(8,128)(2,1)S(1)}, bf16[4,2,256,128]{3,2,1,0:T(8,128)(2,1)S(1)}, u32[]{:S(2)}, u32[]{:S(2)}) %collective-permute-start.16) | collective-permute-done | bytes 524320 | tf_op jit(solution)/shard_map/ppermute | solution.py:218
  85.2 1.6 %odq_near.1 = bf16[3,2,2,256,128]{4,3,2,1,0:T(8,128)(2,1)S(1)} custom-call(s32[4]{0:T(128)S(1)} %pad_add_fusion.1.pos_ref, bf16[2,256,128]{2,1,0:T(8,128)(2,1)S(1)} %get-tuple-element.40.refs_0_, bf16[2,2,256,128]{3,2,1,0:T(8,128)(2,1)S(1)} %collective-permute-done.8.refs_8_.refs_1_.refs_2_, bf16[2,256,128]{2,1,0:T(8,128)(2,1)S(1)} %get-tuple-element.42.refs_2_, ...), custom_call_target="tpu_custom_call" | custom-call | tf_op jit(solution)/shard_map/odq_near/pallas_call | solution.py:81
  87.7 1.9 %collective-permute-done.25.refs_3_.refs_4_ = bf16[2,2,256,128]{3,2,1,0:T(8,128)(2,1)S(1)} collective-permute-done((bf16[2,2,256,128]{3,2,1,0:T(8,128)(2,1)S(1)}, bf16[2,2,256,128]{3,2,1,0:T(8,128)(2,1)S(1)}, u32[]{:S(2)}, u32[]{:S(2)}) %collective-permute-start.25) | collective-permute-done | bytes 262176 | tf_op jit(solution)/shard_map/ppermute | solution.py:218
  89.6 1.3 %dkv_near.1 = bf16[2,2,2,256,128]{4,3,2,1,0:T(8,128)(2,1)S(1)} custom-call(s32[4]{0:T(128)S(1)} %pad_add_fusion.1.pos_ref, bf16[2,256,128]{2,1,0:T(8,128)(2,1)S(1)} %get-tuple-element.65.refs_0_, bf16[4,2,256,128]{3,2,1,0:T(8,128)(2,1)S(1)} %collective-permute-done.16.refs_5_.refs_6_.refs_1_.refs_2_, bf16[2,256,128]{2,1,0:T(8,128)(2,1)S(1)} %get-tuple-element.66.refs_2_, ...), custom_call_target="tpu_custom_call" | custom-call | tf_op jit(solution)/shard_map/dkv_near/pallas_call | solution.py:81
  91.0 1.7 %collective-permute-start.23 = (bf16[2,256,128]{2,1,0:T(8,128)(2,1)S(1)}, bf16[2,256,128]{2,1,0:T(8,128)(2,1)S(1)}, u32[]{:S(2)}, u32[]{:S(2)}) collective-permute-start(bf16[2,256,128]{2,1,0:T(8,128)(2,1)S(1)} %get-tuple-element.77), channel_id=1, source_target_pairs={{0,2},{1,3},{2,0},{3,1},{4,6},{5,7},{6,4},{7,5},{8,10},{9,11},{10,... | collective-permute-start | bytes 393224 | tf_op jit(solution)/shard_map/ppermute | solution.py:218
  93.2 1.6 %dkv_early.1 = (bf16[256,1536]{1,0:T(8,128)(2,1)}, bf16[256,1536]{1,0:T(8,128)(2,1)}) custom-call(s32[4]{0:T(128)S(1)} %pad_add_fusion.1.pos_ref, bf16[2,2,2,256,128]{4,3,2,1,0:T(8,128)(2,1)S(1)} %collective-permute-done.26.refs_0_, bf16[2,256,128]{2,1,0:T(8,128)(2,1)S(1)} %get-tuple-element.69.refs_1_, ...), custom_call_target="tpu_custom_call" | custom-call | tf_op jit(solution)/shard_map/dkv_early/pallas_call | solution.py:81
  94.8 1.9 %odq_out.1 = (bf16[256,1536]{1,0:T(8,128)(2,1)}, bf16[256,1536]{1,0:T(8,128)(2,1)}, bf16[16,128]{1,0:T(8,128)(2,1)S(1)}) custom-call(s32[4]{0:T(128)S(1)} %pad_add_fusion.1.pos_ref, bf16[3,2,2,256,128]{4,3,2,1,0:T(8,128)(2,1)S(1)} %collective-permute-done.19.refs_0_, bf16[2,256,128]{2,1,0:T(8,128)(2,1)S(1)} %get-tuple-element.54.refs_1_, ...), custom_call_target="tpu_custom_call" | custom-call | tf_op jit(solution)/shard_map/odq_out/pallas_call | solution.py:81
  97.3 2.0 %collective-permute-done.24.refs_3_ = bf16[2,256,128]{2,1,0:T(8,128)(2,1)S(1)} collective-permute-done((bf16[2,256,128]{2,1,0:T(8,128)(2,1)S(1)}, bf16[2,256,128]{2,1,0:T(8,128)(2,1)S(1)}, u32[]{:S(2)}, u32[]{:S(2)}) %collective-permute-start.24) | collective-permute-done | bytes 131104 | tf_op jit(solution)/shard_map/ppermute | solution.py:218
  99.3 1.4 %dkv_out.1 = (bf16[256,1536]{1,0:T(8,128)(2,1)}, bf16[256,1536]{1,0:T(8,128)(2,1)}) custom-call(s32[4]{0:T(128)S(1)} %pad_add_fusion.1.pos_ref, bf16[2,256,128]{2,1,0:T(8,128)(2,1)S(1)} %get-tuple-element.62.refs_0_, bf16[2,256,128]{2,1,0:T(8,128)(2,1)S(1)} %collective-permute-done.22.refs_1_, ...), custom_call_target="tpu_custom_call", output_to_operand_aliasing={{0}: (5, {}), {1}: (6, {})} | custom-call | tf_op jit(solution)/shard_map/dkv_out/pallas_call | solution.py:81
  (61 shorter events, 12.8 us)
Async XLA Ops:
  3.0 1.4 %copy-start.5 = (bf16[256,1536]{1,0:T(8,128)(2,1)S(1)}, bf16[256,1536]{1,0:T(8,128)(2,1)}, u32[]{:S(2)}) copy-start(bf16[256,1536]{1,0:T(8,128)(2,1)} %g_ref.5) | copy-start | bytes 2359300
  3.8 2.5 %copy-start.1 = (bf16[256,1536]{1,0:T(8,128)(2,1)S(1)}, bf16[256,1536]{1,0:T(8,128)(2,1)}, u32[]{:S(2)}) copy-start(bf16[256,1536]{1,0:T(8,128)(2,1)} %refs_0_.12) | copy-start | bytes 2359300
  3.9 2.4 %copy-start.3 = (bf16[256,1536]{1,0:T(8,128)(2,1)S(1)}, bf16[256,1536]{1,0:T(8,128)(2,1)}, u32[]{:S(2)}) copy-start(bf16[256,1536]{1,0:T(8,128)(2,1)} %refs_1_.12) | copy-start | bytes 2359300
  3.9 2.4 %collective-permute-start = (bf16[6,2,256,128]{3,2,1,0:T(8,128)(2,1)S(1)}, bf16[6,2,256,128]{3,2,1,0:T(8,128)(2,1)S(1)}, u32[]{:S(2)}, u32[]{:S(2)}) collective-permute-start(bf16[6,2,256,128]{3,2,1,0:T(8,128)(2,1)S(1)} %kv_for_near.1), channel_id=1, source_target_pairs={{0,1},{1,0},{2,3},{3,2},{4,5},{5,4},{6,7},{7,6},{8,9},{9,8},{10,11... | collective-permute-start | bytes 2359304 | tf_op jit(solution)/shard_map/ppermute | solution.py:218
  5.2 22.8 %collective-permute-start.6 = (bf16[6,2,256,128]{3,2,1,0:T(8,128)(2,1)S(1)}, bf16[6,2,256,128]{3,2,1,0:T(8,128)(2,1)S(1)}, u32[]{:S(2)}, u32[]{:S(2)}) collective-permute-start(bf16[6,2,256,128]{3,2,1,0:T(8,128)(2,1)S(1)} %qg_for_near.1), channel_id=1, source_target_pairs={{0,1},{1,0},{2,3},{3,2},{4,5},{5,4},{6,7},{7,6},{8,9},{9,8},{10,11... | collective-permute-start | bytes 2359304 | tf_op jit(solution)/shard_map/ppermute | solution.py:218
  8.5 15.3 %collective-permute-start.3 = (bf16[2,2,2,256,128]{4,3,2,1,0:T(8,128)(2,1)S(1)}, bf16[2,2,2,256,128]{4,3,2,1,0:T(8,128)(2,1)}, u32[]{:S(2)}, u32[]{:S(2)}) collective-permute-start(bf16[2,2,2,256,128]{4,3,2,1,0:T(8,128)(2,1)S(1)} %kv_for_far.2), channel_id=1, source_target_pairs={{0,2},{1,3},{2,0},{3,1},{4,6},{5,7},{6,4},{7,5},{8,10},{9,11},{10,... | collective-permute-start | bytes 1572872 | tf_op jit(solution)/shard_map/ppermute | solution.py:218
  11.5 29.5 %collective-permute-start.1 = (bf16[3,2,2,256,128]{4,3,2,1,0:T(8,128)(2,1)S(1)}, bf16[3,2,2,256,128]{4,3,2,1,0:T(8,128)(2,1)}, u32[]{:S(2)}, u32[]{:S(2)}) collective-permute-start(bf16[3,2,2,256,128]{4,3,2,1,0:T(8,128)(2,1)S(1)} %kv_near.1.refs_3_.refs_0_), channel_id=1, source_target_pairs={{0,4},{1,5},{2,6},{3,7},{4,0},{5,1},{6,2},{7,3},{8,12},{9,13},{10,... | collective-permute-start | bytes 2359304 | tf_op jit(solution)/shard_map/ppermute | solution.py:229
  13.0 29.5 %collective-permute-start.2 = (bf16[3,2,2,256,128]{4,3,2,1,0:T(8,128)(2,1)S(1)}, bf16[3,2,2,256,128]{4,3,2,1,0:T(8,128)(2,1)}, u32[]{:S(2)}, u32[]{:S(2)}) collective-permute-start(bf16[3,2,2,256,128]{4,3,2,1,0:T(8,128)(2,1)S(1)} %kv_near.1.refs_3_.refs_0_), channel_id=1, source_target_pairs={{0,1},{1,0},{2,3},{3,2},{4,8},{5,9},{6,10},{7,11},{8,4},{9,5},{10,... | collective-permute-start | bytes 2359304 | tf_op jit(solution)/shard_map/ppermute | solution.py:229
  24.6 9.4 %copy-start.6 = (s32[16,3]{0,1:T(4,128)S(1)}, s32[16,3]{0,1:T(4,128)}, u32[]{:S(2)}) copy-start(s32[16,3]{0,1:T(4,128)} %param.11) | copy-start | bytes 580
  24.6 9.3 %copy-start.7 = (s32[16,3]{0,1:T(4,128)S(1)}, s32[16,3]{0,1:T(4,128)}, u32[]{:S(2)}) copy-start(s32[16,3]{0,1:T(4,128)} %param.10) | copy-start | bytes 580
  24.6 7.9 %collective-permute-start.9 = (bf16[1,2,2,256,128]{4,3,2,1,0:T(8,128)(2,1)S(1)}, bf16[1,2,2,256,128]{4,3,2,1,0:T(8,128)(2,1)S(1)}, u32[]{:S(2)}, u32[]{:S(2)}) collective-permute-start(bf16[1,2,2,256,128]{4,3,2,1,0:T(8,128)(2,1)S(1)} %kv_for_far.3), channel_id=1, source_target_pairs={{0,2},{1,3},{2,0},{3,1},{4,6},{5,7},{6,4},{7,5},{8,10},{9,11},{10,... | collective-permute-start | bytes 786440 | tf_op jit(solution)/shard_map/ppermute | solution.py:218
  26.4 16.8 %collective-permute-start.4 = (bf16[2,2,2,256,128]{4,3,2,1,0:T(8,128)(2,1)}, bf16[2,2,2,256,128]{4,3,2,1,0:T(8,128)(2,1)}, u32[]{:S(2)}, u32[]{:S(2)}) collective-permute-start(bf16[2,2,2,256,128]{4,3,2,1,0:T(8,128)(2,1)} %collective-permute-done.3.refs_3_), channel_id=1, source_target_pairs={{0,4},{1,5},{2,6},{3,7},{4,0},{5,1},{6,2},{7,3},{8,12},{9,13},{10,... | collective-permute-start | bytes 1572872 | tf_op jit(solution)/shard_map/ppermute | solution.py:229
  28.0 15.3 %collective-permute-start.5 = (bf16[2,2,2,256,128]{4,3,2,1,0:T(8,128)(2,1)}, bf16[2,2,2,256,128]{4,3,2,1,0:T(8,128)(2,1)}, u32[]{:S(2)}, u32[]{:S(2)}) collective-permute-start(bf16[2,2,2,256,128]{4,3,2,1,0:T(8,128)(2,1)} %collective-permute-done.3.refs_3_), channel_id=1, source_target_pairs={{0,1},{1,0},{2,3},{3,2},{4,8},{5,9},{6,10},{7,11},{8,4},{9,5},{10,... | collective-permute-start | bytes 1572872 | tf_op jit(solution)/shard_map/ppermute | solution.py:229
  32.5 7.4 %collective-permute-start.7 = (bf16[1,2,2,256,128]{4,3,2,1,0:T(8,128)(2,1)}, bf16[1,2,2,256,128]{4,3,2,1,0:T(8,128)(2,1)}, u32[]{:S(2)}, u32[]{:S(2)}) collective-permute-start(bf16[1,2,2,256,128]{4,3,2,1,0:T(8,128)(2,1)} %qg_for_far.2), channel_id=1, source_target_pairs={{0,2},{1,3},{2,0},{3,1},{4,6},{5,7},{6,4},{7,5},{8,10},{9,11},{10,... | collective-permute-start | bytes 786440 | tf_op jit(solution)/shard_map/ppermute | solution.py:218
  39.9 12.7 %collective-permute-start.10 = (bf16[2,2,2,256,128]{4,3,2,1,0:T(8,128)(2,1)S(1)}, bf16[2,2,2,256,128]{4,3,2,1,0:T(8,128)(2,1)S(1)}, u32[]{:S(2)}, u32[]{:S(2)}) collective-permute-start(bf16[2,2,2,256,128]{4,3,2,1,0:T(8,128)(2,1)S(1)} %qg_for_far.3), channel_id=1, source_target_pairs={{0,2},{1,3},{2,0},{3,1},{4,6},{5,7},{6,4},{7,5},{8,10},{9,11},{10,... | collective-permute-start | bytes 1572872 | tf_op jit(solution)/shard_map/ppermute | solution.py:218
  40.9 17.6 %collective-permute-start.12 = (bf16[1,2,2,256,128]{4,3,2,1,0:T(8,128)(2,1)S(1)}, bf16[1,2,2,256,128]{4,3,2,1,0:T(8,128)(2,1)S(1)}, u32[]{:S(2)}, u32[]{:S(2)}) collective-permute-start(bf16[1,2,2,256,128]{4,3,2,1,0:T(8,128)(2,1)S(1)} %collective-permute-done.9.refs_3_), channel_id=1, source_target_pairs={{0,4},{1,5},{2,6},{3,7},{4,0},{5,1},{6,2},{7,3},{8,12},{9,13},{10,... | collective-permute-start | bytes 786440 | tf_op jit(solution)/shard_map/ppermute | solution.py:229
  42.5 18.1 %collective-permute-start.13 = (bf16[1,2,2,256,128]{4,3,2,1,0:T(8,128)(2,1)S(1)}, bf16[1,2,2,256,128]{4,3,2,1,0:T(8,128)(2,1)S(1)}, u32[]{:S(2)}, u32[]{:S(2)}) collective-permute-start(bf16[1,2,2,256,128]{4,3,2,1,0:T(8,128)(2,1)S(1)} %collective-permute-done.9.refs_3_), channel_id=1, source_target_pairs={{0,1},{1,0},{2,3},{3,2},{4,8},{5,9},{6,10},{7,11},{8,4},{9,5},{10,... | collective-permute-start | bytes 786440 | tf_op jit(solution)/shard_map/ppermute | solution.py:229
  49.3 11.4 %collective-permute-start.8 = (bf16[2,2,256,128]{3,2,1,0:T(8,128)(2,1)S(1)}, bf16[2,2,256,128]{3,2,1,0:T(8,128)(2,1)S(1)}, u32[]{:S(2)}, u32[]{:S(2)}) collective-permute-start(bf16[2,2,256,128]{3,2,1,0:T(8,128)(2,1)S(1)} %get-tuple-element.41), channel_id=1, source_target_pairs={{0,2},{1,3},{2,0},{3,1},{4,6},{5,7},{6,4},{7,5},{8,10},{9,11},{10,... | collective-permute-start | bytes 786440 | tf_op jit(solution)/shard_map/ppermute | solution.py:218
  49.4 20.2 %collective-permute-start.14 = (bf16[4,2,256,128]{3,2,1,0:T(8,128)(2,1)S(1)}, bf16[4,2,256,128]{3,2,1,0:T(8,128)(2,1)S(1)}, u32[]{:S(2)}, u32[]{:S(2)}) collective-permute-start(bf16[4,2,256,128]{3,2,1,0:T(8,128)(2,1)S(1)} %get-tuple-element.46), channel_id=1, source_target_pairs={{0,4},{1,5},{2,6},{3,7},{4,0},{5,1},{6,2},{7,3},{8,12},{9,13},{10,... | collective-permute-start | bytes 1572872 | tf_op jit(solution)/shard_map/ppermute | solution.py:229
  52.6 16.9 %collective-permute-start.15 = (bf16[4,2,256,128]{3,2,1,0:T(8,128)(2,1)S(1)}, bf16[4,2,256,128]{3,2,1,0:T(8,128)(2,1)S(1)}, u32[]{:S(2)}, u32[]{:S(2)}) collective-permute-start(bf16[4,2,256,128]{3,2,1,0:T(8,128)(2,1)S(1)} %get-tuple-element.47), channel_id=1, source_target_pairs={{0,1},{1,0},{2,3},{3,2},{4,8},{5,9},{6,10},{7,11},{8,4},{9,5},{10,... | collective-permute-start | bytes 1572872 | tf_op jit(solution)/shard_map/ppermute | solution.py:229
  58.6 16.2 %collective-permute-start.17 = (bf16[4,2,256,128]{3,2,1,0:T(8,128)(2,1)S(1)}, bf16[4,2,256,128]{3,2,1,0:T(8,128)(2,1)S(1)}, u32[]{:S(2)}, u32[]{:S(2)}) collective-permute-start(bf16[4,2,256,128]{3,2,1,0:T(8,128)(2,1)S(1)} %get-tuple-element.51), channel_id=1, source_target_pairs={{0,4},{1,5},{2,6},{3,7},{4,0},{5,1},{6,2},{7,3},{8,12},{9,13},{10,... | collective-permute-start | bytes 1572872 | tf_op jit(solution)/shard_map/ppermute | solution.py:229
  60.7 14.1 %collective-permute-start.18 = (bf16[4,2,256,128]{3,2,1,0:T(8,128)(2,1)S(1)}, bf16[4,2,256,128]{3,2,1,0:T(8,128)(2,1)S(1)}, u32[]{:S(2)}, u32[]{:S(2)}) collective-permute-start(bf16[4,2,256,128]{3,2,1,0:T(8,128)(2,1)S(1)} %get-tuple-element.52), channel_id=1, source_target_pairs={{0,1},{1,0},{2,3},{3,2},{4,8},{5,9},{6,10},{7,11},{8,4},{9,5},{10,... | collective-permute-start | bytes 1572872 | tf_op jit(solution)/shard_map/ppermute | solution.py:229
  60.7 8.8 %collective-permute-start.11 = (bf16[2,2,256,128]{3,2,1,0:T(8,128)(2,1)S(1)}, bf16[2,2,256,128]{3,2,1,0:T(8,128)(2,1)S(1)}, u32[]{:S(2)}, u32[]{:S(2)}) collective-permute-start(bf16[2,2,256,128]{3,2,1,0:T(8,128)(2,1)S(1)} %get-tuple-element.43), channel_id=1, source_target_pairs={{0,2},{1,3},{2,0},{3,1},{4,6},{5,7},{6,4},{7,5},{8,10},{9,11},{10,... | collective-permute-start | bytes 786440 | tf_op jit(solution)/shard_map/ppermute | solution.py:218
  70.3 14.9 %collective-permute-start.16 = (bf16[4,2,256,128]{3,2,1,0:T(8,128)(2,1)S(1)}, bf16[4,2,256,128]{3,2,1,0:T(8,128)(2,1)S(1)}, u32[]{:S(2)}, u32[]{:S(2)}) collective-permute-start(bf16[4,2,256,128]{3,2,1,0:T(8,128)(2,1)S(1)} %get-tuple-element.49), channel_id=1, source_target_pairs={{0,2},{1,3},{2,0},{3,1},{4,6},{5,7},{6,4},{7,5},{8,10},{9,11},{10,... | collective-permute-start | bytes 1572872 | tf_op jit(solution)/shard_map/ppermute | solution.py:218
  72.1 14.8 %collective-permute-start.20 = (bf16[4,2,256,128]{3,2,1,0:T(8,128)(2,1)S(1)}, bf16[4,2,256,128]{3,2,1,0:T(8,128)(2,1)S(1)}, u32[]{:S(2)}, u32[]{:S(2)}) collective-permute-start(bf16[4,2,256,128]{3,2,1,0:T(8,128)(2,1)S(1)} %get-tuple-element.60), channel_id=1, source_target_pairs={{0,4},{1,5},{2,6},{3,7},{4,0},{5,1},{6,2},{7,3},{8,12},{9,13},{10,... | collective-permute-start | bytes 1572872 | tf_op jit(solution)/shard_map/ppermute | solution.py:229
  73.3 13.6 %collective-permute-start.21 = (bf16[4,2,256,128]{3,2,1,0:T(8,128)(2,1)S(1)}, bf16[4,2,256,128]{3,2,1,0:T(8,128)(2,1)S(1)}, u32[]{:S(2)}, u32[]{:S(2)}) collective-permute-start(bf16[4,2,256,128]{3,2,1,0:T(8,128)(2,1)S(1)} %get-tuple-element.61), channel_id=1, source_target_pairs={{0,1},{1,0},{2,3},{3,2},{4,8},{5,9},{6,10},{7,11},{8,4},{9,5},{10,... | collective-permute-start | bytes 1572872 | tf_op jit(solution)/shard_map/ppermute | solution.py:229
  75.6 14.0 %collective-permute-start.25 = (bf16[2,2,256,128]{3,2,1,0:T(8,128)(2,1)S(1)}, bf16[2,2,256,128]{3,2,1,0:T(8,128)(2,1)S(1)}, u32[]{:S(2)}, u32[]{:S(2)}) collective-permute-start(bf16[2,2,256,128]{3,2,1,0:T(8,128)(2,1)S(1)} %get-tuple-element.67), channel_id=1, source_target_pairs={{0,2},{1,3},{2,0},{3,1},{4,6},{5,7},{6,4},{7,5},{8,10},{9,11},{10,... | collective-permute-start | bytes 786440 | tf_op jit(solution)/shard_map/ppermute | solution.py:218
  86.8 8.0 %collective-permute-start.19 = (bf16[3,2,2,256,128]{4,3,2,1,0:T(8,128)(2,1)S(1)}, bf16[3,2,2,256,128]{4,3,2,1,0:T(8,128)(2,1)S(1)}, u32[]{:S(2)}, u32[]{:S(2)}) collective-permute-start(bf16[3,2,2,256,128]{4,3,2,1,0:T(8,128)(2,1)S(1)} %odq_near.1), channel_id=1, source_target_pairs={{0,1},{1,0},{2,3},{3,2},{4,5},{5,4},{6,7},{7,6},{8,9},{9,8},{10,11... | collective-permute-start | bytes 2359304 | tf_op jit(solution)/shard_map/ppermute | solution.py:218
  90.9 2.3 %collective-permute-start.26 = (bf16[2,2,2,256,128]{4,3,2,1,0:T(8,128)(2,1)S(1)}, bf16[2,2,2,256,128]{4,3,2,1,0:T(8,128)(2,1)S(1)}, u32[]{:S(2)}, u32[]{:S(2)}) collective-permute-start(bf16[2,2,2,256,128]{4,3,2,1,0:T(8,128)(2,1)S(1)} %dkv_near.1), channel_id=1, source_target_pairs={{0,1},{1,0},{2,3},{3,2},{4,5},{5,4},{6,7},{7,6},{8,9},{9,8},{10,11... | collective-permute-start | bytes 1572872 | tf_op jit(solution)/shard_map/ppermute | solution.py:218
  91.0 6.4 %collective-permute-start.23 = (bf16[2,256,128]{2,1,0:T(8,128)(2,1)S(1)}, bf16[2,256,128]{2,1,0:T(8,128)(2,1)S(1)}, u32[]{:S(2)}, u32[]{:S(2)}) collective-permute-start(bf16[2,256,128]{2,1,0:T(8,128)(2,1)S(1)} %get-tuple-element.77), channel_id=1, source_target_pairs={{0,2},{1,3},{2,0},{3,1},{4,6},{5,7},{6,4},{7,5},{8,10},{9,11},{10,... | collective-permute-start | bytes 393224 | tf_op jit(solution)/shard_map/ppermute | solution.py:218
  92.7 6.7 %collective-permute-start.24 = (bf16[2,256,128]{2,1,0:T(8,128)(2,1)S(1)}, bf16[2,256,128]{2,1,0:T(8,128)(2,1)S(1)}, u32[]{:S(2)}, u32[]{:S(2)}) collective-permute-start(bf16[2,256,128]{2,1,0:T(8,128)(2,1)S(1)} %get-tuple-element.76), channel_id=1, source_target_pairs={{0,3},{1,2},{2,1},{3,0},{4,7},{5,6},{6,5},{7,4},{8,11},{9,10},{10,... | collective-permute-start | bytes 393224 | tf_op jit(solution)/shard_map/ppermute | solution.py:218
  92.9 6.5 %collective-permute-start.22 = (bf16[2,256,128]{2,1,0:T(8,128)(2,1)S(1)}, bf16[2,256,128]{2,1,0:T(8,128)(2,1)S(1)}, u32[]{:S(2)}, u32[]{:S(2)}) collective-permute-start(bf16[2,256,128]{2,1,0:T(8,128)(2,1)S(1)} %get-tuple-element.63), channel_id=1, source_target_pairs={{0,1},{1,0},{2,3},{3,2},{4,5},{5,4},{6,7},{7,6},{8,9},{9,8},{10,11... | collective-permute-start | bytes 393224 | tf_op jit(solution)/shard_map/ppermute | solution.py:218
  (3 other events, 3.6 us)

commit v5 on v4

--- a/solution.py
+++ b/solution.py
@@ -180,23 +180,27 @@
     )(pos, table, query, grad_out, *[array for array, _ in blocks])
 
 
-def owned(plan, pos, total, halos, riders=(), after=()):
-    count = len(riders)
+def owned(plan, pos, total, halos, riders=(), beside=(), after=()):
+    count, extra = len(riders), len(beside)
 
     def kernel(pos_ref, total_ref, halo_a, halo_b, *refs):
         first, near, far = refs[-4:-1]
         for n in range(count):
             far[pl.ds(2 * n, 2)] = refs[n][...]
+        for n in range(extra):
+            near[n] = refs[count + n][...]
         for r in range(4):
             grads = total_ref[r]
             for n, halo in enumerate((halo_a, halo_b)):
                 grads += jnp.where(pos_ref[2 + n] > 0, halo[r].astype(F32), 0.0)
-            if r < 2:
-                (first, near)[r][...] = grads.astype(BF)
+            if r == 0:
+                first[...] = grads.astype(BF)
+            elif r == 1:
+                near[extra] = grads.astype(BF)
             else:
                 far[2 * count + r - 2] = grads.astype(BF)
 
-    shapes = [plan.piece, plan.piece, (2 * count + 2,) + plan.piece]
+    shapes = [plan.piece, (extra + 1,) + plan.piece, (2 * count + 2,) + plan.piece]
     return pl.pallas_call(
         kernel,
         out_shape=[jax.ShapeDtypeStruct(shape, BF) for shape in shapes + [TOKEN]],
@@ -205,13 +209,14 @@
             grid=(1,),
             in_specs=[full(plan.layer)] * 3
             + [full((2,) + plan.piece)] * count
+            + [full(plan.piece)] * extra
             + [ANYWHERE] * len(after),
             out_specs=[full(shape) for shape in shapes] + [ANYWHERE],
         ),
         compiler_params=PARAMS,
         cost_estimate=cost(0, 0),
         name="owned",
-    )(pos, total, *halos, *riders, *after)
+    )(pos, total, *halos, *riders, *beside, *after)
 
 
 def swap(value, r):
@@ -292,7 +297,8 @@
     for c in every:
         riders = [odq[-1][2]] if c == 0 else []
         wait = [odq[-2][2][0]] if c == 0 else []
-        first, near, far, token = owned(plan, pos, *sums[c], riders, wait)
+        beside = [dkv[-1][1][0]] if c == every[-1] else []
+        first, near, far, token = owned(plan, pos, *sums[c], riders, beside, wait)
         if c < every[-1]:
             far = swap(far, 2)
         if c == 0:
@@ -300,38 +306,38 @@
         dkv.append([first, near, [far, 2 * len(riders)]])
         tokens.append(token)
 
-    def onward(group, name, after):
+    def onward(groups, name, after):
         moves, inputs = [], []
-        for c, (_, near, (far, at)) in enumerate(group):
-            moves += [(2 * c, (), 0, (c, 0)), (2 * c + 1, (at + 1,), 0, (c, 1))]
-            inputs += [near, far]
-        shapes = [(len(group), 2) + piece]
-        return swap(move(plan, pos, inputs, shapes, moves, name, after=after)[0], 1)
-
-    def columns(where):
-        return [
-            (a, view + (b,), b, ("head", r, c)) for a, view, r, c in where for b in range(2)
-        ]
-
-    shapes = [(plan.tile, HEADS * HEAD_DIM)] * 2
-
-    def spread(group, got):
-        inputs, where = [got], []
-        for c, (first, _, (far, at)) in enumerate(group):
-            where += [(0, (c, 0), 1, c), (0, (c, 1), 3, c)]
-            where += [(len(inputs), (), 0, c), (len(inputs) + 1, (at,), 2, c)]
-            inputs += [first, far]
-        return inputs, where
-
-    inputs, where = spread(odq, onward(odq, "odq_near", tokens[-2:-1]))
-    attended, query_grad, token = move(plan, pos, inputs, shapes + [TOKEN], columns(where), "odq_out")
-
-    inputs, where = spread(dkv[:-1], onward(dkv[:-1], "dkv_near", tokens[-1:]))
-    grads = move(plan, pos, inputs, shapes, columns(where), "dkv_early")
-    first, near, (far, _) = dkv[-1]
-    inputs = [first, swap(near, 1), swap(far[0], 2), swap(far[1], 3)]
-    where = [(r, (), r, per - 1) for r in range(4)]
-    key_grad, value_grad = move(plan, pos, inputs, shapes, columns(where), "dkv_out", into=grads, after=[token])
+        for n, group in enumerate(groups):
+            for c, (_, near, (far, at)) in enumerate(group):
+                view = (0,) if near.ndim > len(piece) else ()
+                moves += [(len(inputs), view, n, (c, 0)), (len(inputs) + 1, (at + 1,), n, (c, 1))]
+                inputs += [near, far]
+        shapes = [(len(group), 2) + piece for group in groups]
+        return [swap(x, 1) for x in move(plan, pos, inputs, shapes, moves, name, after=after)]
+
+    got = onward([odq[:-1]], "odq_near", [])
+    got += onward([odq[-1:], dkv[:1]], "late_near", tokens[1:2])
+
+    shapes = [(plan.tile, HEADS * HEAD_DIM)] * 4
+    inputs, moves = list(got), []
+    for n, (first, _, (far, at)) in enumerate(odq + dkv[:1]):
+        m, c = divmod(n, per)
+        source, at_c = (0, n) if n < per - 1 else (n - per + 2, 0)
+        pieces = [(len(inputs), ()), (source, (at_c, 0)), (len(inputs) + 1, (at,)), (source, (at_c, 1))]
+        for r, (a, view) in enumerate(pieces):
+            moves += [(a, view + (b,), 2 * m + b, ("head", r, c)) for b in range(2)]
+        inputs += [first, far]
+    attended, query_grad, *grads = move(plan, pos, inputs, shapes, moves, "outputs")
+
+    (first_1, _, (far_1, at)), (first_2, near_2, (far_2, _)) = dkv[1:]
+    beside = swap(near_2, 1)
+    inputs = [first_1, beside, far_1, swap(far_1[at + 1], 1)]
+    inputs += [first_2, swap(far_2[0], 2), swap(far_2[1], 3)]
+    where = [(0, (), 0, 1), (1, (0,), 1, 1), (2, (at,), 2, 1), (3, (), 3, 1)]
+    where += [(4, (), 0, 2), (1, (1,), 1, 2), (5, (), 2, 2), (6, (), 3, 2)]
+    moves = [(a, view + (b,), b, ("head", r, c)) for a, view, r, c in where for b in range(2)]
+    key_grad, value_grad = move(plan, pos, inputs, shapes[:2], moves, "last", into=grads)
     return attended, query_grad, key_grad, value_grad
 
 

time: 101 us -> 99.4 us (0.984)
  starting transfers between devices: 28.3 us -> 25.9 us
  waiting for transfers between devices: 34 us -> 36.1 us
  Pallas kernels: 34.9 us -> 33.4 us
    ppermute x12, waiting for transfers between devices: 2.24 us -> 11.9 us  [exchange(): return lax.ppermute(value, ('seq', 'head'), pairs)]
    ppermute x15 -> x17, waiting for transfers between devices: 31.8 us -> 24.2 us  [swap(): return lax.ppermute(value, 'head', [(i, i ^ r) for i in range(4)])]
    ppermute x15 -> x17, starting transfers between devices: 17.1 us -> 14.6 us  [swap(): return lax.ppermute(value, 'head', [(i, i ^ r) for i in range(4)])]
    pallas_call x12 -> x11, Pallas kernels: 14.7 us -> 13.2 us  [move(): pl.pallas_call(kernel, out_shape=[jax.ShapeDtypeStruct(shape, BF) for sha...]
  transfers between devices with their start and end apart: 27 -> 29, of which waited for: 11 -> 10; matrix products, arithmetic and copies ran while one was open for 0% -> 0% of each run, Pallas kernels for 32% -> 31%
where the time goes in v5:
time: 99.4 us; the launch traced here: 99.1 us
  waiting for transfers between devices  36.1 us (36%)
  Pallas kernels  33.4 us (34%)
  starting transfers between devices  25.9 us (26%)
  local copies, waits for them, and re-layouts  2.5 us (3%)
  between operations  1.08 us (1%)
    ppermute x17, waiting for transfers between devices, swap(): return lax.ppermute(value, 'head', [(i, i ^ r) for i in range(4)])  24.2 us
    pallas_call x3, Pallas kernels, attend(): pl.pallas_call(kernel, out_shape=[jax.ShapeDtypeStruct(shape, BF) for sha...  17.9 us
    ppermute x17, starting transfers between devices, swap(): return lax.ppermute(value, 'head', [(i, i ^ r) for i in range(4)])  14.6 us
    pallas_call x11, Pallas kernels, move(): pl.pallas_call(kernel, out_shape=[jax.ShapeDtypeStruct(shape, BF) for sha...  13.2 us
    ppermute x12, waiting for transfers between devices, exchange(): return lax.ppermute(value, ('seq', 'head'), pairs)  11.9 us
    ppermute x12, starting transfers between devices, exchange(): return lax.ppermute(value, ('seq', 'head'), pairs)  11.2 us
    pallas_call x3, Pallas kernels, owned(): pl.pallas_call(kernel, out_shape=[jax.ShapeDtypeStruct(shape, BF) for sha...  2.34 us
    unnamed x16, local copies, waits for them, and re-layouts  2.3 us
  transfers between devices with their start and end apart: 29, of which 10 were waited for; matrix products, arithmetic and copies ran while one was open for 0% of the time, Pallas kernels for 31%

profile of v5, /device:TPU:0, one launch (start us, length us, event | category | flops | bytes accessed | tf_op | source)
XLA Modules:
  0.0 99.1 jit_solution(11102311870607949018)
XLA Ops:
  0.7 1.1 %copy-done = bf16[256,1536]{1,0:T(8,128)(2,1)S(1)} copy-done((bf16[256,1536]{1,0:T(8,128)(2,1)S(1)}, bf16[256,1536]{1,0:T(8,128)(2,1)}, u32[]{:S(2)}) %copy-start) | copy-done | bytes 786456
  1.9 1.1 %copy-done.2 = bf16[256,1536]{1,0:T(8,128)(2,1)S(1)} copy-done((bf16[256,1536]{1,0:T(8,128)(2,1)S(1)}, bf16[256,1536]{1,0:T(8,128)(2,1)}, u32[]{:S(2)}) %copy-start.2) | copy-done | bytes 786456
  6.3 1.2 %kv_near.1.refs_3_.refs_0_ = bf16[3,2,2,256,128]{4,3,2,1,0:T(8,128)(2,1)S(1)} custom-call(s32[4]{0:T(128)S(1)} %pad_add_fusion.1.pos_ref, bf16[256,1536]{1,0:T(8,128)(2,1)S(1)} %copy-done.1, bf16[256,1536]{1,0:T(8,128)(2,1)S(1)} %copy-done.3, bf16[6,2,256,128]{3,2,1,0:T(8,128)(2,1)S(1)} %collective-permute-done.refs_2_), custom_call_target="tpu_custom_call" | custom-call | tf_op jit(solution)/shard_map/kv_near/pallas_call | solution.py:81
  8.5 2.9 %collective-permute-start.3 = (bf16[2,2,2,256,128]{4,3,2,1,0:T(8,128)(2,1)S(1)}, bf16[2,2,2,256,128]{4,3,2,1,0:T(8,128)(2,1)}, u32[]{:S(2)}, u32[]{:S(2)}) collective-permute-start(bf16[2,2,2,256,128]{4,3,2,1,0:T(8,128)(2,1)S(1)} %kv_for_far.2), channel_id=1, source_target_pairs={{0,2},{1,3},{2,0},{3,1},{4,6},{5,7},{6,4},{7,5},{8,10},{9,11},{10,... | collective-permute-start | bytes 1572872 | tf_op jit(solution)/shard_map/ppermute | solution.py:223
  11.5 1.6 %collective-permute-start.1 = (bf16[3,2,2,256,128]{4,3,2,1,0:T(8,128)(2,1)S(1)}, bf16[3,2,2,256,128]{4,3,2,1,0:T(8,128)(2,1)}, u32[]{:S(2)}, u32[]{:S(2)}) collective-permute-start(bf16[3,2,2,256,128]{4,3,2,1,0:T(8,128)(2,1)S(1)} %kv_near.1.refs_3_.refs_0_), channel_id=1, source_target_pairs={{0,4},{1,5},{2,6},{3,7},{4,0},{5,1},{6,2},{7,3},{8,12},{9,13},{10,... | collective-permute-start | bytes 2359304 | tf_op jit(solution)/shard_map/ppermute | solution.py:234
  13.0 10.8 %collective-permute-done.3.refs_3_ = bf16[2,2,2,256,128]{4,3,2,1,0:T(8,128)(2,1)} collective-permute-done((bf16[2,2,2,256,128]{4,3,2,1,0:T(8,128)(2,1)S(1)}, bf16[2,2,2,256,128]{4,3,2,1,0:T(8,128)(2,1)}, u32[]{:S(2)}, u32[]{:S(2)}) %collective-permute-start.3) | collective-permute-done | bytes 524320 | tf_op jit(solution)/shard_map/ppermute | solution.py:223
  24.6 1.8 %collective-permute-start.9 = (bf16[1,2,2,256,128]{4,3,2,1,0:T(8,128)(2,1)S(1)}, bf16[1,2,2,256,128]{4,3,2,1,0:T(8,128)(2,1)S(1)}, u32[]{:S(2)}, u32[]{:S(2)}) collective-permute-start(bf16[1,2,2,256,128]{4,3,2,1,0:T(8,128)(2,1)S(1)} %kv_for_far.3), channel_id=1, source_target_pairs={{0,2},{1,3},{2,0},{3,1},{4,6},{5,7},{6,4},{7,5},{8,10},{9,11},{10,... | collective-permute-start | bytes 786440 | tf_op jit(solution)/shard_map/ppermute | solution.py:223
  26.4 1.6 %collective-permute-start.4 = (bf16[2,2,2,256,128]{4,3,2,1,0:T(8,128)(2,1)}, bf16[2,2,2,256,128]{4,3,2,1,0:T(8,128)(2,1)}, u32[]{:S(2)}, u32[]{:S(2)}) collective-permute-start(bf16[2,2,2,256,128]{4,3,2,1,0:T(8,128)(2,1)} %collective-permute-done.3.refs_3_), channel_id=1, source_target_pairs={{0,4},{1,5},{2,6},{3,7},{4,0},{5,1},{6,2},{7,3},{8,12},{9,13},{10,... | collective-permute-start | bytes 1572872 | tf_op jit(solution)/shard_map/ppermute | solution.py:234
  28.0 1.3 %qg_for_far.2 = bf16[1,2,2,256,128]{4,3,2,1,0:T(8,128)(2,1)} custom-call(s32[4]{0:T(128)S(1)} %pad_add_fusion.1.pos_ref, bf16[256,1536]{1,0:T(8,128)(2,1)S(1)} %copy-done.4, bf16[256,1536]{1,0:T(8,128)(2,1)S(1)} %copy-done.5, bf16[6,2,256,128]{3,2,1,0:T(8,128)(2,1)S(1)} %collective-permute-done.6.refs_2_.refs_6_, ...), custom_call_target="tpu_custom_call" | custom-call | tf_op jit(solution)/shard_map/qg_for_far/pallas_call | solution.py:81
  29.3 3.2 %collective-permute-done.9.refs_3_ = bf16[1,2,2,256,128]{4,3,2,1,0:T(8,128)(2,1)S(1)} collective-permute-done((bf16[1,2,2,256,128]{4,3,2,1,0:T(8,128)(2,1)S(1)}, bf16[1,2,2,256,128]{4,3,2,1,0:T(8,128)(2,1)S(1)}, u32[]{:S(2)}, u32[]{:S(2)}) %collective-permute-start.9) | collective-permute-done | bytes 262176 | tf_op jit(solution)/shard_map/ppermute | solution.py:223
  32.5 1.4 %collective-permute-start.7 = (bf16[1,2,2,256,128]{4,3,2,1,0:T(8,128)(2,1)}, bf16[1,2,2,256,128]{4,3,2,1,0:T(8,128)(2,1)}, u32[]{:S(2)}, u32[]{:S(2)}) collective-permute-start(bf16[1,2,2,256,128]{4,3,2,1,0:T(8,128)(2,1)} %qg_for_far.2), channel_id=1, source_target_pairs={{0,2},{1,3},{2,0},{3,1},{4,6},{5,7},{6,4},{7,5},{8,10},{9,11},{10,... | collective-permute-start | bytes 786440 | tf_op jit(solution)/shard_map/ppermute | solution.py:223
  35.8 1.5 %collective-permute-start.13 = (bf16[1,2,2,256,128]{4,3,2,1,0:T(8,128)(2,1)S(1)}, bf16[1,2,2,256,128]{4,3,2,1,0:T(8,128)(2,1)S(1)}, u32[]{:S(2)}, u32[]{:S(2)}) collective-permute-start(bf16[1,2,2,256,128]{4,3,2,1,0:T(8,128)(2,1)S(1)} %collective-permute-done.9.refs_3_), channel_id=1, source_target_pairs={{0,4},{1,5},{2,6},{3,7},{4,0},{5,1},{6,2},{7,3},{8,12},{9,13},{10,... | collective-permute-start | bytes 786440 | tf_op jit(solution)/shard_map/ppermute | solution.py:234
  37.3 4.7 %collective-permute-done.7.refs_7_ = bf16[1,2,2,256,128]{4,3,2,1,0:T(8,128)(2,1)} collective-permute-done((bf16[1,2,2,256,128]{4,3,2,1,0:T(8,128)(2,1)}, bf16[1,2,2,256,128]{4,3,2,1,0:T(8,128)(2,1)}, u32[]{:S(2)}, u32[]{:S(2)}) %collective-permute-start.7) | collective-permute-done | bytes 262176 | tf_op jit(solution)/shard_map/ppermute | solution.py:223
  42.1 1.2 %collective-permute-done.4.refs_4_ = bf16[2,2,2,256,128]{4,3,2,1,0:T(8,128)(2,1)} collective-permute-done((bf16[2,2,2,256,128]{4,3,2,1,0:T(8,128)(2,1)}, bf16[2,2,2,256,128]{4,3,2,1,0:T(8,128)(2,1)}, u32[]{:S(2)}, u32[]{:S(2)}) %collective-permute-start.4) | collective-permute-done | bytes 524320 | tf_op jit(solution)/shard_map/ppermute | solution.py:234
  43.2 6.0 %attend.3 = (bf16[2,256,128]{2,1,0:T(8,128)(2,1)S(1)}, bf16[2,256,128]{2,1,0:T(8,128)(2,1)S(1)}, bf16[2,2,256,128]{3,2,1,0:T(8,128)(2,1)S(1)}, bf16[4,2,256,128]...) custom-call(s32[4]{0:T(128)S(1)} %pad_add_fusion.1.pos_ref, ...), custom_call_target="tpu_custom_call" | custom-call | flops 6039797760 | bytes 5242880 | tf_op jit(solution)/shard_map/attend/pallas_call | solution.py:163
  49.6 3.1 %collective-permute-start.15 = (bf16[4,2,256,128]{3,2,1,0:T(8,128)(2,1)S(1)}, bf16[4,2,256,128]{3,2,1,0:T(8,128)(2,1)S(1)}, u32[]{:S(2)}, u32[]{:S(2)}) collective-permute-start(bf16[4,2,256,128]{3,2,1,0:T(8,128)(2,1)S(1)} %get-tuple-element.46), channel_id=1, source_target_pairs={{0,4},{1,5},{2,6},{3,7},{4,0},{5,1},{6,2},{7,3},{8,12},{9,13},{10,... | collective-permute-start | bytes 1572872 | tf_op jit(solution)/shard_map/ppermute | solution.py:234
  52.8 6.0 %attend.4 = (bf16[2,256,128]{2,1,0:T(8,128)(2,1)S(1)}, bf16[2,256,128]{2,1,0:T(8,128)(2,1)S(1)}, bf16[2,2,256,128]{3,2,1,0:T(8,128)(2,1)S(1)}, bf16[4,2,256,128]...) custom-call(s32[4]{0:T(128)S(1)} %pad_add_fusion.1.pos_ref, ...), custom_call_target="tpu_custom_call" | custom-call | flops 6039797760 | bytes 5242880 | tf_op jit(solution)/shard_map/attend/pallas_call | solution.py:163
  58.7 2.0 %collective-permute-start.18 = (bf16[4,2,256,128]{3,2,1,0:T(8,128)(2,1)S(1)}, bf16[4,2,256,128]{3,2,1,0:T(8,128)(2,1)S(1)}, u32[]{:S(2)}, u32[]{:S(2)}) collective-permute-start(bf16[4,2,256,128]{3,2,1,0:T(8,128)(2,1)S(1)} %get-tuple-element.52), channel_id=1, source_target_pairs={{0,4},{1,5},{2,6},{3,7},{4,0},{5,1},{6,2},{7,3},{8,12},{9,13},{10,... | collective-permute-start | bytes 1572872 | tf_op jit(solution)/shard_map/ppermute | solution.py:234
  60.7 1.6 %collective-permute-start.11 = (bf16[2,2,256,128]{3,2,1,0:T(8,128)(2,1)S(1)}, bf16[2,2,256,128]{3,2,1,0:T(8,128)(2,1)S(1)}, u32[]{:S(2)}, u32[]{:S(2)}) collective-permute-start(bf16[2,2,256,128]{3,2,1,0:T(8,128)(2,1)S(1)} %get-tuple-element.43), channel_id=1, source_target_pairs={{0,2},{1,3},{2,0},{3,1},{4,6},{5,7},{6,4},{7,5},{8,10},{9,11},{10,... | collective-permute-start | bytes 786440 | tf_op jit(solution)/shard_map/ppermute | solution.py:223
  62.3 5.9 %attend.5 = (bf16[2,256,128]{2,1,0:T(8,128)(2,1)S(1)}, bf16[2,256,128]{2,1,0:T(8,128)(2,1)S(1)}, bf16[2,2,256,128]{3,2,1,0:T(8,128)(2,1)S(1)}, bf16[4,2,256,128]...) custom-call(s32[4]{0:T(128)S(1)} %pad_add_fusion.1.pos_ref, ...), custom_call_target="tpu_custom_call" | custom-call | flops 6039797760 | bytes 5242880 | tf_op jit(solution)/shard_map/attend/pallas_call | solution.py:163
  68.2 1.2 %collective-permute-done.11.refs_3_.refs_1_.refs_6_ = bf16[2,2,256,128]{3,2,1,0:T(8,128)(2,1)S(1)} collective-permute-done((bf16[2,2,256,128]{3,2,1,0:T(8,128)(2,1)S(1)}, bf16[2,2,256,128]{3,2,1,0:T(8,128)(2,1)S(1)}, u32[]{:S(2)}, u32[]{:S(2)}) %collective-permute-start.11) | collective-permute-done | bytes 262176 | tf_op jit(solution)/shard_map/ppermute | solution.py:223
  69.4 1.5 %collective-permute-start.22 = (bf16[4,2,256,128]{3,2,1,0:T(8,128)(2,1)S(1)}, bf16[4,2,256,128]{3,2,1,0:T(8,128)(2,1)S(1)}, u32[]{:S(2)}, u32[]{:S(2)}) collective-permute-start(bf16[4,2,256,128]{3,2,1,0:T(8,128)(2,1)S(1)} %get-tuple-element.65), channel_id=1, source_target_pairs={{0,4},{1,5},{2,6},{3,7},{4,0},{5,1},{6,2},{7,3},{8,12},{9,13},{10,... | collective-permute-start | bytes 1572872 | tf_op jit(solution)/shard_map/ppermute | solution.py:234
  71.7 1.6 %collective-permute-start.17 = (bf16[4,2,256,128]{3,2,1,0:T(8,128)(2,1)S(1)}, bf16[4,2,256,128]{3,2,1,0:T(8,128)(2,1)S(1)}, u32[]{:S(2)}, u32[]{:S(2)}) collective-permute-start(bf16[4,2,256,128]{3,2,1,0:T(8,128)(2,1)S(1)} %get-tuple-element.49), channel_id=1, source_target_pairs={{0,2},{1,3},{2,0},{3,1},{4,6},{5,7},{6,4},{7,5},{8,10},{9,11},{10,... | collective-permute-start | bytes 1572872 | tf_op jit(solution)/shard_map/ppermute | solution.py:223
  73.3 1.3 %odq_near.1 = bf16[2,2,2,256,128]{4,3,2,1,0:T(8,128)(2,1)S(1)} custom-call(s32[4]{0:T(128)S(1)} %pad_add_fusion.1.pos_ref, bf16[2,256,128]{2,1,0:T(8,128)(2,1)S(1)} %get-tuple-element.40.refs_0_, bf16[2,2,256,128]{3,2,1,0:T(8,128)(2,1)S(1)} %collective-permute-done.8.refs_1_.refs_8_.refs_4_, bf16[2,256,128]{2,1,0:T(8,128)(2,1)S(1)} %get-tuple-element.42.refs_2_, ...), custom_call_target="tpu_custom_call" | custom-call | tf_op jit(solution)/shard_map/odq_near/pallas_call | solution.py:81
  74.5 2.0 %collective-permute-done.18.halo_a = bf16[4,2,256,128]{3,2,1,0:T(8,128)(2,1)S(1)} collective-permute-done((bf16[4,2,256,128]{3,2,1,0:T(8,128)(2,1)S(1)}, bf16[4,2,256,128]{3,2,1,0:T(8,128)(2,1)S(1)}, u32[]{:S(2)}, u32[]{:S(2)}) %collective-permute-start.18) | collective-permute-done | bytes 524320 | tf_op jit(solution)/shard_map/ppermute | solution.py:234
  77.4 8.7 %collective-permute-done.22.halo_a = bf16[4,2,256,128]{3,2,1,0:T(8,128)(2,1)S(1)} collective-permute-done((bf16[4,2,256,128]{3,2,1,0:T(8,128)(2,1)S(1)}, bf16[4,2,256,128]{3,2,1,0:T(8,128)(2,1)S(1)}, u32[]{:S(2)}, u32[]{:S(2)}) %collective-permute-start.22) | collective-permute-done | bytes 524320 | tf_op jit(solution)/shard_map/ppermute | solution.py:234
  86.9 1.3 %late_near.1 = (bf16[1,2,2,256,128]{4,3,2,1,0:T(8,128)(2,1)S(1)}, bf16[1,2,2,256,128]{4,3,2,1,0:T(8,128)(2,1)S(1)}) custom-call(s32[4]{0:T(128)S(1)} %pad_add_fusion.1.pos_ref, bf16[2,256,128]{2,1,0:T(8,128)(2,1)S(1)} %get-tuple-element.44.refs_0_, bf16[4,2,256,128]{3,2,1,0:T(8,128)(2,1)S(1)} %collective-permute-done.17.refs_1_.refs_3_.refs_8_.refs_10_, ...), custom_call_target="tpu_custom_call" | custom-call | tf_op jit(solution)/shard_map/late_near/pallas_call | solution.py:81
  89.6 2.3 %collective-permute-done.25.refs_2_ = bf16[2,2,256,128]{3,2,1,0:T(8,128)(2,1)S(1)} collective-permute-done((bf16[2,2,256,128]{3,2,1,0:T(8,128)(2,1)S(1)}, bf16[2,2,256,128]{3,2,1,0:T(8,128)(2,1)S(1)}, u32[]{:S(2)}, u32[]{:S(2)}) %collective-permute-start.25) | collective-permute-done | bytes 262176 | tf_op jit(solution)/shard_map/ppermute | solution.py:223
  92.0 1.8 %collective-permute-start.28 = (bf16[2,256,128]{2,1,0:T(8,128)(2,1)S(1)}, bf16[2,256,128]{2,1,0:T(8,128)(2,1)S(1)}, u32[]{:S(2)}, u32[]{:S(2)}) collective-permute-start(bf16[2,256,128]{2,1,0:T(8,128)(2,1)S(1)} %get-tuple-element.76), channel_id=1, source_target_pairs={{0,3},{1,2},{2,1},{3,0},{4,7},{5,6},{6,5},{7,4},{8,11},{9,10},{10,... | collective-permute-start | bytes 393224 | tf_op jit(solution)/shard_map/ppermute | solution.py:223
  93.8 2.1 %outputs.1 = (bf16[256,1536]{1,0:T(8,128)(2,1)}, bf16[256,1536]{1,0:T(8,128)(2,1)}, bf16[256,1536]{1,0:T(8,128)(2,1)}, bf16[256,1536]{1,0:T(8,128)(2,1)}) custom-call(s32[4]{0:T(128)S(1)} %pad_add_fusion.1.pos_ref, bf16[2,2,2,256,128]{4,3,2,1,0:T(8,128)(2,1)S(1)} %collective-permute-done.12.refs_0_, ...), custom_call_target="tpu_custom_call" | custom-call | tf_op jit(solution)/shard_map/outputs/pallas_call | solution.py:81
  96.0 1.3 %collective-permute-done.28.refs_6_ = bf16[2,256,128]{2,1,0:T(8,128)(2,1)S(1)} collective-permute-done((bf16[2,256,128]{2,1,0:T(8,128)(2,1)S(1)}, bf16[2,256,128]{2,1,0:T(8,128)(2,1)S(1)}, u32[]{:S(2)}, u32[]{:S(2)}) %collective-permute-start.28) | collective-permute-done | bytes 131104 | tf_op jit(solution)/shard_map/ppermute | solution.py:223
  97.3 1.6 %last.1 = (bf16[256,1536]{1,0:T(8,128)(2,1)}, bf16[256,1536]{1,0:T(8,128)(2,1)}) custom-call(s32[4]{0:T(128)S(1)} %pad_add_fusion.1.pos_ref, bf16[2,256,128]{2,1,0:T(8,128)(2,1)S(1)} %get-tuple-element.63.refs_0_, bf16[2,2,256,128]{3,2,1,0:T(8,128)(2,1)S(1)} %collective-permute-done.24.refs_1_, ...), custom_call_target="tpu_custom_call", output_to_operand_aliasing={{0}: (8, {}), {1}: (9, {})} | custom-call | tf_op jit(solution)/shard_map/last/pallas_call | solution.py:81
  (65 shorter events, 11.2 us)
Async XLA Ops:
  3.8 2.5 %copy-start.1 = (bf16[256,1536]{1,0:T(8,128)(2,1)S(1)}, bf16[256,1536]{1,0:T(8,128)(2,1)}, u32[]{:S(2)}) copy-start(bf16[256,1536]{1,0:T(8,128)(2,1)} %refs_0_.12) | copy-start | bytes 2359300
  3.9 2.4 %collective-permute-start = (bf16[6,2,256,128]{3,2,1,0:T(8,128)(2,1)S(1)}, bf16[6,2,256,128]{3,2,1,0:T(8,128)(2,1)S(1)}, u32[]{:S(2)}, u32[]{:S(2)}) collective-permute-start(bf16[6,2,256,128]{3,2,1,0:T(8,128)(2,1)S(1)} %kv_for_near.1), channel_id=1, source_target_pairs={{0,1},{1,0},{2,3},{3,2},{4,5},{5,4},{6,7},{7,6},{8,9},{9,8},{10,11... | collective-permute-start | bytes 2359304 | tf_op jit(solution)/shard_map/ppermute | solution.py:223
  5.2 22.8 %collective-permute-start.6 = (bf16[6,2,256,128]{3,2,1,0:T(8,128)(2,1)S(1)}, bf16[6,2,256,128]{3,2,1,0:T(8,128)(2,1)S(1)}, u32[]{:S(2)}, u32[]{:S(2)}) collective-permute-start(bf16[6,2,256,128]{3,2,1,0:T(8,128)(2,1)S(1)} %qg_for_near.1), channel_id=1, source_target_pairs={{0,1},{1,0},{2,3},{3,2},{4,5},{5,4},{6,7},{7,6},{8,9},{9,8},{10,11... | collective-permute-start | bytes 2359304 | tf_op jit(solution)/shard_map/ppermute | solution.py:223
  8.5 15.3 %collective-permute-start.3 = (bf16[2,2,2,256,128]{4,3,2,1,0:T(8,128)(2,1)S(1)}, bf16[2,2,2,256,128]{4,3,2,1,0:T(8,128)(2,1)}, u32[]{:S(2)}, u32[]{:S(2)}) collective-permute-start(bf16[2,2,2,256,128]{4,3,2,1,0:T(8,128)(2,1)S(1)} %kv_for_far.2), channel_id=1, source_target_pairs={{0,2},{1,3},{2,0},{3,1},{4,6},{5,7},{6,4},{7,5},{8,10},{9,11},{10,... | collective-permute-start | bytes 1572872 | tf_op jit(solution)/shard_map/ppermute | solution.py:223
  11.5 23.7 %collective-permute-start.1 = (bf16[3,2,2,256,128]{4,3,2,1,0:T(8,128)(2,1)S(1)}, bf16[3,2,2,256,128]{4,3,2,1,0:T(8,128)(2,1)}, u32[]{:S(2)}, u32[]{:S(2)}) collective-permute-start(bf16[3,2,2,256,128]{4,3,2,1,0:T(8,128)(2,1)S(1)} %kv_near.1.refs_3_.refs_0_), channel_id=1, source_target_pairs={{0,4},{1,5},{2,6},{3,7},{4,0},{5,1},{6,2},{7,3},{8,12},{9,13},{10,... | collective-permute-start | bytes 2359304 | tf_op jit(solution)/shard_map/ppermute | solution.py:234
  13.0 22.8 %collective-permute-start.2 = (bf16[3,2,2,256,128]{4,3,2,1,0:T(8,128)(2,1)S(1)}, bf16[3,2,2,256,128]{4,3,2,1,0:T(8,128)(2,1)}, u32[]{:S(2)}, u32[]{:S(2)}) collective-permute-start(bf16[3,2,2,256,128]{4,3,2,1,0:T(8,128)(2,1)S(1)} %kv_near.1.refs_3_.refs_0_), channel_id=1, source_target_pairs={{0,1},{1,0},{2,3},{3,2},{4,8},{5,9},{6,10},{7,11},{8,4},{9,5},{10,... | collective-permute-start | bytes 2359304 | tf_op jit(solution)/shard_map/ppermute | solution.py:234
  24.6 9.4 %copy-start.6 = (s32[16,3]{0,1:T(4,128)S(1)}, s32[16,3]{0,1:T(4,128)}, u32[]{:S(2)}) copy-start(s32[16,3]{0,1:T(4,128)} %param.11) | copy-start | bytes 580
  24.6 9.3 %copy-start.7 = (s32[16,3]{0,1:T(4,128)S(1)}, s32[16,3]{0,1:T(4,128)}, u32[]{:S(2)}) copy-start(s32[16,3]{0,1:T(4,128)} %param.10) | copy-start | bytes 580
  24.6 7.9 %collective-permute-start.9 = (bf16[1,2,2,256,128]{4,3,2,1,0:T(8,128)(2,1)S(1)}, bf16[1,2,2,256,128]{4,3,2,1,0:T(8,128)(2,1)S(1)}, u32[]{:S(2)}, u32[]{:S(2)}) collective-permute-start(bf16[1,2,2,256,128]{4,3,2,1,0:T(8,128)(2,1)S(1)} %kv_for_far.3), channel_id=1, source_target_pairs={{0,2},{1,3},{2,0},{3,1},{4,6},{5,7},{6,4},{7,5},{8,10},{9,11},{10,... | collective-permute-start | bytes 786440 | tf_op jit(solution)/shard_map/ppermute | solution.py:223
  26.4 16.8 %collective-permute-start.4 = (bf16[2,2,2,256,128]{4,3,2,1,0:T(8,128)(2,1)}, bf16[2,2,2,256,128]{4,3,2,1,0:T(8,128)(2,1)}, u32[]{:S(2)}, u32[]{:S(2)}) collective-permute-start(bf16[2,2,2,256,128]{4,3,2,1,0:T(8,128)(2,1)} %collective-permute-done.3.refs_3_), channel_id=1, source_target_pairs={{0,4},{1,5},{2,6},{3,7},{4,0},{5,1},{6,2},{7,3},{8,12},{9,13},{10,... | collective-permute-start | bytes 1572872 | tf_op jit(solution)/shard_map/ppermute | solution.py:234
  28.0 15.3 %collective-permute-start.5 = (bf16[2,2,2,256,128]{4,3,2,1,0:T(8,128)(2,1)}, bf16[2,2,2,256,128]{4,3,2,1,0:T(8,128)(2,1)}, u32[]{:S(2)}, u32[]{:S(2)}) collective-permute-start(bf16[2,2,2,256,128]{4,3,2,1,0:T(8,128)(2,1)} %collective-permute-done.3.refs_3_), channel_id=1, source_target_pairs={{0,1},{1,0},{2,3},{3,2},{4,8},{5,9},{6,10},{7,11},{8,4},{9,5},{10,... | collective-permute-start | bytes 1572872 | tf_op jit(solution)/shard_map/ppermute | solution.py:234
  32.5 9.6 %collective-permute-start.7 = (bf16[1,2,2,256,128]{4,3,2,1,0:T(8,128)(2,1)}, bf16[1,2,2,256,128]{4,3,2,1,0:T(8,128)(2,1)}, u32[]{:S(2)}, u32[]{:S(2)}) collective-permute-start(bf16[1,2,2,256,128]{4,3,2,1,0:T(8,128)(2,1)} %qg_for_far.2), channel_id=1, source_target_pairs={{0,2},{1,3},{2,0},{3,1},{4,6},{5,7},{6,4},{7,5},{8,10},{9,11},{10,... | collective-permute-start | bytes 786440 | tf_op jit(solution)/shard_map/ppermute | solution.py:223
  35.1 17.6 %collective-permute-start.10 = (bf16[2,2,2,256,128]{4,3,2,1,0:T(8,128)(2,1)S(1)}, bf16[2,2,2,256,128]{4,3,2,1,0:T(8,128)(2,1)S(1)}, u32[]{:S(2)}, u32[]{:S(2)}) collective-permute-start(bf16[2,2,2,256,128]{4,3,2,1,0:T(8,128)(2,1)S(1)} %qg_for_far.3), channel_id=1, source_target_pairs={{0,2},{1,3},{2,0},{3,1},{4,6},{5,7},{6,4},{7,5},{8,10},{9,11},{10,... | collective-permute-start | bytes 1572872 | tf_op jit(solution)/shard_map/ppermute | solution.py:223
  35.8 22.9 %collective-permute-start.13 = (bf16[1,2,2,256,128]{4,3,2,1,0:T(8,128)(2,1)S(1)}, bf16[1,2,2,256,128]{4,3,2,1,0:T(8,128)(2,1)S(1)}, u32[]{:S(2)}, u32[]{:S(2)}) collective-permute-start(bf16[1,2,2,256,128]{4,3,2,1,0:T(8,128)(2,1)S(1)} %collective-permute-done.9.refs_3_), channel_id=1, source_target_pairs={{0,4},{1,5},{2,6},{3,7},{4,0},{5,1},{6,2},{7,3},{8,12},{9,13},{10,... | collective-permute-start | bytes 786440 | tf_op jit(solution)/shard_map/ppermute | solution.py:234
  42.1 18.6 %collective-permute-start.14 = (bf16[1,2,2,256,128]{4,3,2,1,0:T(8,128)(2,1)S(1)}, bf16[1,2,2,256,128]{4,3,2,1,0:T(8,128)(2,1)S(1)}, u32[]{:S(2)}, u32[]{:S(2)}) collective-permute-start(bf16[1,2,2,256,128]{4,3,2,1,0:T(8,128)(2,1)S(1)} %collective-permute-done.9.refs_3_), channel_id=1, source_target_pairs={{0,1},{1,0},{2,3},{3,2},{4,8},{5,9},{6,10},{7,11},{8,4},{9,5},{10,... | collective-permute-start | bytes 786440 | tf_op jit(solution)/shard_map/ppermute | solution.py:234
  49.3 11.4 %collective-permute-start.8 = (bf16[2,2,256,128]{3,2,1,0:T(8,128)(2,1)S(1)}, bf16[2,2,256,128]{3,2,1,0:T(8,128)(2,1)S(1)}, u32[]{:S(2)}, u32[]{:S(2)}) collective-permute-start(bf16[2,2,256,128]{3,2,1,0:T(8,128)(2,1)S(1)} %get-tuple-element.41), channel_id=1, source_target_pairs={{0,2},{1,3},{2,0},{3,1},{4,6},{5,7},{6,4},{7,5},{8,10},{9,11},{10,... | collective-permute-start | bytes 786440 | tf_op jit(solution)/shard_map/ppermute | solution.py:223
  49.6 21.3 %collective-permute-start.15 = (bf16[4,2,256,128]{3,2,1,0:T(8,128)(2,1)S(1)}, bf16[4,2,256,128]{3,2,1,0:T(8,128)(2,1)S(1)}, u32[]{:S(2)}, u32[]{:S(2)}) collective-permute-start(bf16[4,2,256,128]{3,2,1,0:T(8,128)(2,1)S(1)} %get-tuple-element.46), channel_id=1, source_target_pairs={{0,4},{1,5},{2,6},{3,7},{4,0},{5,1},{6,2},{7,3},{8,12},{9,13},{10,... | collective-permute-start | bytes 1572872 | tf_op jit(solution)/shard_map/ppermute | solution.py:234
  52.8 18.2 %collective-permute-start.16 = (bf16[4,2,256,128]{3,2,1,0:T(8,128)(2,1)S(1)}, bf16[4,2,256,128]{3,2,1,0:T(8,128)(2,1)S(1)}, u32[]{:S(2)}, u32[]{:S(2)}) collective-permute-start(bf16[4,2,256,128]{3,2,1,0:T(8,128)(2,1)S(1)} %get-tuple-element.47), channel_id=1, source_target_pairs={{0,1},{1,0},{2,3},{3,2},{4,8},{5,9},{6,10},{7,11},{8,4},{9,5},{10,... | collective-permute-start | bytes 1572872 | tf_op jit(solution)/shard_map/ppermute | solution.py:234
  58.7 17.8 %collective-permute-start.18 = (bf16[4,2,256,128]{3,2,1,0:T(8,128)(2,1)S(1)}, bf16[4,2,256,128]{3,2,1,0:T(8,128)(2,1)S(1)}, u32[]{:S(2)}, u32[]{:S(2)}) collective-permute-start(bf16[4,2,256,128]{3,2,1,0:T(8,128)(2,1)S(1)} %get-tuple-element.52), channel_id=1, source_target_pairs={{0,4},{1,5},{2,6},{3,7},{4,0},{5,1},{6,2},{7,3},{8,12},{9,13},{10,... | collective-permute-start | bytes 1572872 | tf_op jit(solution)/shard_map/ppermute | solution.py:234
  60.7 15.9 %collective-permute-start.19 = (bf16[4,2,256,128]{3,2,1,0:T(8,128)(2,1)S(1)}, bf16[4,2,256,128]{3,2,1,0:T(8,128)(2,1)S(1)}, u32[]{:S(2)}, u32[]{:S(2)}) collective-permute-start(bf16[4,2,256,128]{3,2,1,0:T(8,128)(2,1)S(1)} %get-tuple-element.53), channel_id=1, source_target_pairs={{0,1},{1,0},{2,3},{3,2},{4,8},{5,9},{6,10},{7,11},{8,4},{9,5},{10,... | collective-permute-start | bytes 1572872 | tf_op jit(solution)/shard_map/ppermute | solution.py:234
  60.7 8.7 %collective-permute-start.11 = (bf16[2,2,256,128]{3,2,1,0:T(8,128)(2,1)S(1)}, bf16[2,2,256,128]{3,2,1,0:T(8,128)(2,1)S(1)}, u32[]{:S(2)}, u32[]{:S(2)}) collective-permute-start(bf16[2,2,256,128]{3,2,1,0:T(8,128)(2,1)S(1)} %get-tuple-element.43), channel_id=1, source_target_pairs={{0,2},{1,3},{2,0},{3,1},{4,6},{5,7},{6,4},{7,5},{8,10},{9,11},{10,... | collective-permute-start | bytes 786440 | tf_op jit(solution)/shard_map/ppermute | solution.py:223
  69.4 16.7 %collective-permute-start.22 = (bf16[4,2,256,128]{3,2,1,0:T(8,128)(2,1)S(1)}, bf16[4,2,256,128]{3,2,1,0:T(8,128)(2,1)S(1)}, u32[]{:S(2)}, u32[]{:S(2)}) collective-permute-start(bf16[4,2,256,128]{3,2,1,0:T(8,128)(2,1)S(1)} %get-tuple-element.65), channel_id=1, source_target_pairs={{0,4},{1,5},{2,6},{3,7},{4,0},{5,1},{6,2},{7,3},{8,12},{9,13},{10,... | collective-permute-start | bytes 1572872 | tf_op jit(solution)/shard_map/ppermute | solution.py:234
  70.9 15.2 %collective-permute-start.23 = (bf16[4,2,256,128]{3,2,1,0:T(8,128)(2,1)S(1)}, bf16[4,2,256,128]{3,2,1,0:T(8,128)(2,1)S(1)}, u32[]{:S(2)}, u32[]{:S(2)}) collective-permute-start(bf16[4,2,256,128]{3,2,1,0:T(8,128)(2,1)S(1)} %get-tuple-element.66), channel_id=1, source_target_pairs={{0,1},{1,0},{2,3},{3,2},{4,8},{5,9},{6,10},{7,11},{8,4},{9,5},{10,... | collective-permute-start | bytes 1572872 | tf_op jit(solution)/shard_map/ppermute | solution.py:234
  71.7 15.2 %collective-permute-start.17 = (bf16[4,2,256,128]{3,2,1,0:T(8,128)(2,1)S(1)}, bf16[4,2,256,128]{3,2,1,0:T(8,128)(2,1)S(1)}, u32[]{:S(2)}, u32[]{:S(2)}) collective-permute-start(bf16[4,2,256,128]{3,2,1,0:T(8,128)(2,1)S(1)} %get-tuple-element.49), channel_id=1, source_target_pairs={{0,2},{1,3},{2,0},{3,1},{4,6},{5,7},{6,4},{7,5},{8,10},{9,11},{10,... | collective-permute-start | bytes 1572872 | tf_op jit(solution)/shard_map/ppermute | solution.py:223
  76.6 15.4 %collective-permute-start.12 = (bf16[2,2,2,256,128]{4,3,2,1,0:T(8,128)(2,1)S(1)}, bf16[2,2,2,256,128]{4,3,2,1,0:T(8,128)(2,1)S(1)}, u32[]{:S(2)}, u32[]{:S(2)}) collective-permute-start(bf16[2,2,2,256,128]{4,3,2,1,0:T(8,128)(2,1)S(1)} %odq_near.1), channel_id=1, source_target_pairs={{0,1},{1,0},{2,3},{3,2},{4,5},{5,4},{6,7},{7,6},{8,9},{9,8},{10,11... | collective-permute-start | bytes 1572872 | tf_op jit(solution)/shard_map/ppermute | solution.py:223
  77.3 14.6 %collective-permute-start.25 = (bf16[2,2,256,128]{3,2,1,0:T(8,128)(2,1)S(1)}, bf16[2,2,256,128]{3,2,1,0:T(8,128)(2,1)S(1)}, u32[]{:S(2)}, u32[]{:S(2)}) collective-permute-start(bf16[2,2,256,128]{3,2,1,0:T(8,128)(2,1)S(1)} %get-tuple-element.69), channel_id=1, source_target_pairs={{0,2},{1,3},{2,0},{3,1},{4,6},{5,7},{6,4},{7,5},{8,10},{9,11},{10,... | collective-permute-start | bytes 786440 | tf_op jit(solution)/shard_map/ppermute | solution.py:223
  88.2 5.6 %collective-permute-start.20 = (bf16[1,2,2,256,128]{4,3,2,1,0:T(8,128)(2,1)S(1)}, bf16[1,2,2,256,128]{4,3,2,1,0:T(8,128)(2,1)S(1)}, u32[]{:S(2)}, u32[]{:S(2)}) collective-permute-start(bf16[1,2,2,256,128]{4,3,2,1,0:T(8,128)(2,1)S(1)} %get-tuple-element.55), channel_id=1, source_target_pairs={{0,1},{1,0},{2,3},{3,2},{4,5},{5,4},{6,7},{7,6},{8,9},{9,8},{10,11... | collective-permute-start | bytes 786440 | tf_op jit(solution)/shard_map/ppermute | solution.py:223
  88.3 7.7 %collective-permute-start.27 = (bf16[2,256,128]{2,1,0:T(8,128)(2,1)S(1)}, bf16[2,256,128]{2,1,0:T(8,128)(2,1)S(1)}, u32[]{:S(2)}, u32[]{:S(2)}) collective-permute-start(bf16[2,256,128]{2,1,0:T(8,128)(2,1)S(1)} %get-tuple-element.77), channel_id=1, source_target_pairs={{0,2},{1,3},{2,0},{3,1},{4,6},{5,7},{6,4},{7,5},{8,10},{9,11},{10,... | collective-permute-start | bytes 393224 | tf_op jit(solution)/shard_map/ppermute | solution.py:223
  89.4 7.8 %collective-permute-start.24 = (bf16[2,2,256,128]{3,2,1,0:T(8,128)(2,1)S(1)}, bf16[2,2,256,128]{3,2,1,0:T(8,128)(2,1)S(1)}, u32[]{:S(2)}, u32[]{:S(2)}) collective-permute-start(bf16[2,2,256,128]{3,2,1,0:T(8,128)(2,1)S(1)} %get-tuple-element.68), channel_id=1, source_target_pairs={{0,1},{1,0},{2,3},{3,2},{4,5},{5,4},{6,7},{7,6},{8,9},{9,8},{10,11... | collective-permute-start | bytes 786440 | tf_op jit(solution)/shard_map/ppermute | solution.py:223
  91.9 1.9 %collective-permute-start.21 = (bf16[1,2,2,256,128]{4,3,2,1,0:T(8,128)(2,1)S(1)}, bf16[1,2,2,256,128]{4,3,2,1,0:T(8,128)(2,1)S(1)}, u32[]{:S(2)}, u32[]{:S(2)}) collective-permute-start(bf16[1,2,2,256,128]{4,3,2,1,0:T(8,128)(2,1)S(1)} %get-tuple-element.56), channel_id=1, source_target_pairs={{0,1},{1,0},{2,3},{3,2},{4,5},{5,4},{6,7},{7,6},{8,9},{9,8},{10,11... | collective-permute-start | bytes 786440 | tf_op jit(solution)/shard_map/ppermute | solution.py:223
  92.0 5.3 %collective-permute-start.28 = (bf16[2,256,128]{2,1,0:T(8,128)(2,1)S(1)}, bf16[2,256,128]{2,1,0:T(8,128)(2,1)S(1)}, u32[]{:S(2)}, u32[]{:S(2)}) collective-permute-start(bf16[2,256,128]{2,1,0:T(8,128)(2,1)S(1)} %get-tuple-element.76), channel_id=1, source_target_pairs={{0,3},{1,2},{2,1},{3,0},{4,7},{5,6},{6,5},{7,4},{8,11},{9,10},{10,... | collective-permute-start | bytes 393224 | tf_op jit(solution)/shard_map/ppermute | solution.py:223
  93.8 3.5 %collective-permute-start.26 = (bf16[2,256,128]{2,1,0:T(8,128)(2,1)S(1)}, bf16[2,256,128]{2,1,0:T(8,128)(2,1)S(1)}, u32[]{:S(2)}, u32[]{:S(2)}) collective-permute-start(bf16[2,256,128]{2,1,0:T(8,128)(2,1)S(1)} %slice_bitcast_fusion), channel_id=1, source_target_pairs={{0,1},{1,0},{2,3},{3,2},{4,5},{5,4},{6,7},{7,6},{8,9},{9,8},{10,11... | collective-permute-start | bytes 393224 | tf_op jit(solution)/shard_map/ppermute | solution.py:223
  (5 other events, 7.5 us)

commit v6 on v5

--- a/solution.py
+++ b/solution.py
@@ -274,7 +274,7 @@
     qg_got = for_near(there, "qg_for_near")
     qg_fars = [for_far(there, qg_got, qg_parts[0], "qg_for_far", after=far)]
     far.append(for_far(here, kv_got, kv_parts[1], "kv_for_far", after=far))
-    qg_fars.append(for_far(there, qg_got, qg_parts[1], "qg_for_far", after=far[1:]))
+    qg_fars.append(for_far(there, qg_got, qg_parts[1], "qg_for_far", after=far[1:] + nears[1:]))
     fars = [[m] + [exchange(m, turn) for turn in range(2)] for m in far]
 
     odq, sums = [], []

time: 99.4 us -> 99.4 us (level)
  no operation moved by 1% of the time
where the time goes in v6:
time: 99.4 us; the launch traced here: 99.1 us
  waiting for transfers between devices  36.1 us (36%)
  Pallas kernels  33.4 us (34%)
  starting transfers between devices  25.9 us (26%)
  local copies, waits for them, and re-layouts  2.5 us (3%)
  between operations  1.09 us (1%)
    ppermute x17, waiting for transfers between devices, swap(): return lax.ppermute(value, 'head', [(i, i ^ r) for i in range(4)])  24.2 us
    pallas_call x3, Pallas kernels, attend(): pl.pallas_call(kernel, out_shape=[jax.ShapeDtypeStruct(shape, BF) for sha...  17.9 us
    ppermute x17, starting transfers between devices, swap(): return lax.ppermute(value, 'head', [(i, i ^ r) for i in range(4)])  14.6 us
    pallas_call x11, Pallas kernels, move(): pl.pallas_call(kernel, out_shape=[jax.ShapeDtypeStruct(shape, BF) for sha...  13.2 us
    ppermute x12, waiting for transfers between devices, exchange(): return lax.ppermute(value, ('seq', 'head'), pairs)  11.9 us
    ppermute x12, starting transfers between devices, exchange(): return lax.ppermute(value, ('seq', 'head'), pairs)  11.2 us
    pallas_call x3, Pallas kernels, owned(): pl.pallas_call(kernel, out_shape=[jax.ShapeDtypeStruct(shape, BF) for sha...  2.34 us
    unnamed x16, local copies, waits for them, and re-layouts  2.3 us
  transfers between devices with their start and end apart: 29, of which 10 were waited for; matrix products, arithmetic and copies ran while one was open for 0% of the time, Pallas kernels for 31%

profile of v6, /device:TPU:0, one launch (start us, length us, event | category | flops | bytes accessed | tf_op | source)
XLA Modules:
  0.0 99.1 jit_solution(5855505017620971105)
XLA Ops:
  0.7 1.1 %copy-done = bf16[256,1536]{1,0:T(8,128)(2,1)S(1)} copy-done((bf16[256,1536]{1,0:T(8,128)(2,1)S(1)}, bf16[256,1536]{1,0:T(8,128)(2,1)}, u32[]{:S(2)}) %copy-start) | copy-done | bytes 786456
  1.9 1.1 %copy-done.2 = bf16[256,1536]{1,0:T(8,128)(2,1)S(1)} copy-done((bf16[256,1536]{1,0:T(8,128)(2,1)S(1)}, bf16[256,1536]{1,0:T(8,128)(2,1)}, u32[]{:S(2)}) %copy-start.2) | copy-done | bytes 786456
  6.3 1.2 %kv_near.1.refs_3_.refs_0_ = bf16[3,2,2,256,128]{4,3,2,1,0:T(8,128)(2,1)S(1)} custom-call(s32[4]{0:T(128)S(1)} %pad_add_fusion.1.pos_ref, bf16[256,1536]{1,0:T(8,128)(2,1)S(1)} %copy-done.1, bf16[256,1536]{1,0:T(8,128)(2,1)S(1)} %copy-done.3, bf16[6,2,256,128]{3,2,1,0:T(8,128)(2,1)S(1)} %collective-permute-done.refs_2_), custom_call_target="tpu_custom_call" | custom-call | tf_op jit(solution)/shard_map/kv_near/pallas_call | solution.py:81
  8.5 2.9 %collective-permute-start.3 = (bf16[2,2,2,256,128]{4,3,2,1,0:T(8,128)(2,1)S(1)}, bf16[2,2,2,256,128]{4,3,2,1,0:T(8,128)(2,1)}, u32[]{:S(2)}, u32[]{:S(2)}) collective-permute-start(bf16[2,2,2,256,128]{4,3,2,1,0:T(8,128)(2,1)S(1)} %kv_for_far.2), channel_id=1, source_target_pairs={{0,2},{1,3},{2,0},{3,1},{4,6},{5,7},{6,4},{7,5},{8,10},{9,11},{10,... | collective-permute-start | bytes 1572872 | tf_op jit(solution)/shard_map/ppermute | solution.py:223
  11.5 1.6 %collective-permute-start.1 = (bf16[3,2,2,256,128]{4,3,2,1,0:T(8,128)(2,1)S(1)}, bf16[3,2,2,256,128]{4,3,2,1,0:T(8,128)(2,1)}, u32[]{:S(2)}, u32[]{:S(2)}) collective-permute-start(bf16[3,2,2,256,128]{4,3,2,1,0:T(8,128)(2,1)S(1)} %kv_near.1.refs_3_.refs_0_), channel_id=1, source_target_pairs={{0,4},{1,5},{2,6},{3,7},{4,0},{5,1},{6,2},{7,3},{8,12},{9,13},{10,... | collective-permute-start | bytes 2359304 | tf_op jit(solution)/shard_map/ppermute | solution.py:234
  13.0 10.8 %collective-permute-done.3.refs_3_ = bf16[2,2,2,256,128]{4,3,2,1,0:T(8,128)(2,1)} collective-permute-done((bf16[2,2,2,256,128]{4,3,2,1,0:T(8,128)(2,1)S(1)}, bf16[2,2,2,256,128]{4,3,2,1,0:T(8,128)(2,1)}, u32[]{:S(2)}, u32[]{:S(2)}) %collective-permute-start.3) | collective-permute-done | bytes 524320 | tf_op jit(solution)/shard_map/ppermute | solution.py:223
  24.6 1.8 %collective-permute-start.9 = (bf16[1,2,2,256,128]{4,3,2,1,0:T(8,128)(2,1)S(1)}, bf16[1,2,2,256,128]{4,3,2,1,0:T(8,128)(2,1)S(1)}, u32[]{:S(2)}, u32[]{:S(2)}) collective-permute-start(bf16[1,2,2,256,128]{4,3,2,1,0:T(8,128)(2,1)S(1)} %kv_for_far.3), channel_id=1, source_target_pairs={{0,2},{1,3},{2,0},{3,1},{4,6},{5,7},{6,4},{7,5},{8,10},{9,11},{10,... | collective-permute-start | bytes 786440 | tf_op jit(solution)/shard_map/ppermute | solution.py:223
  26.4 1.6 %collective-permute-start.4 = (bf16[2,2,2,256,128]{4,3,2,1,0:T(8,128)(2,1)}, bf16[2,2,2,256,128]{4,3,2,1,0:T(8,128)(2,1)}, u32[]{:S(2)}, u32[]{:S(2)}) collective-permute-start(bf16[2,2,2,256,128]{4,3,2,1,0:T(8,128)(2,1)} %collective-permute-done.3.refs_3_), channel_id=1, source_target_pairs={{0,4},{1,5},{2,6},{3,7},{4,0},{5,1},{6,2},{7,3},{8,12},{9,13},{10,... | collective-permute-start | bytes 1572872 | tf_op jit(solution)/shard_map/ppermute | solution.py:234
  28.0 1.3 %qg_for_far.2 = bf16[1,2,2,256,128]{4,3,2,1,0:T(8,128)(2,1)} custom-call(s32[4]{0:T(128)S(1)} %pad_add_fusion.1.pos_ref, bf16[256,1536]{1,0:T(8,128)(2,1)S(1)} %copy-done.4, bf16[256,1536]{1,0:T(8,128)(2,1)S(1)} %copy-done.5, bf16[6,2,256,128]{3,2,1,0:T(8,128)(2,1)S(1)} %collective-permute-done.6.refs_2_.refs_6_, ...), custom_call_target="tpu_custom_call" | custom-call | tf_op jit(solution)/shard_map/qg_for_far/pallas_call | solution.py:81
  29.3 3.2 %collective-permute-done.9.refs_3_ = bf16[1,2,2,256,128]{4,3,2,1,0:T(8,128)(2,1)S(1)} collective-permute-done((bf16[1,2,2,256,128]{4,3,2,1,0:T(8,128)(2,1)S(1)}, bf16[1,2,2,256,128]{4,3,2,1,0:T(8,128)(2,1)S(1)}, u32[]{:S(2)}, u32[]{:S(2)}) %collective-permute-start.9) | collective-permute-done | bytes 262176 | tf_op jit(solution)/shard_map/ppermute | solution.py:223
  32.5 1.4 %collective-permute-start.7 = (bf16[1,2,2,256,128]{4,3,2,1,0:T(8,128)(2,1)}, bf16[1,2,2,256,128]{4,3,2,1,0:T(8,128)(2,1)}, u32[]{:S(2)}, u32[]{:S(2)}) collective-permute-start(bf16[1,2,2,256,128]{4,3,2,1,0:T(8,128)(2,1)} %qg_for_far.2), channel_id=1, source_target_pairs={{0,2},{1,3},{2,0},{3,1},{4,6},{5,7},{6,4},{7,5},{8,10},{9,11},{10,... | collective-permute-start | bytes 786440 | tf_op jit(solution)/shard_map/ppermute | solution.py:223
  35.8 1.5 %collective-permute-start.13 = (bf16[1,2,2,256,128]{4,3,2,1,0:T(8,128)(2,1)S(1)}, bf16[1,2,2,256,128]{4,3,2,1,0:T(8,128)(2,1)S(1)}, u32[]{:S(2)}, u32[]{:S(2)}) collective-permute-start(bf16[1,2,2,256,128]{4,3,2,1,0:T(8,128)(2,1)S(1)} %collective-permute-done.9.refs_3_), channel_id=1, source_target_pairs={{0,4},{1,5},{2,6},{3,7},{4,0},{5,1},{6,2},{7,3},{8,12},{9,13},{10,... | collective-permute-start | bytes 786440 | tf_op jit(solution)/shard_map/ppermute | solution.py:234
  37.3 4.7 %collective-permute-done.7.refs_7_ = bf16[1,2,2,256,128]{4,3,2,1,0:T(8,128)(2,1)} collective-permute-done((bf16[1,2,2,256,128]{4,3,2,1,0:T(8,128)(2,1)}, bf16[1,2,2,256,128]{4,3,2,1,0:T(8,128)(2,1)}, u32[]{:S(2)}, u32[]{:S(2)}) %collective-permute-start.7) | collective-permute-done | bytes 262176 | tf_op jit(solution)/shard_map/ppermute | solution.py:223
  42.1 1.2 %collective-permute-done.4.refs_4_ = bf16[2,2,2,256,128]{4,3,2,1,0:T(8,128)(2,1)} collective-permute-done((bf16[2,2,2,256,128]{4,3,2,1,0:T(8,128)(2,1)}, bf16[2,2,2,256,128]{4,3,2,1,0:T(8,128)(2,1)}, u32[]{:S(2)}, u32[]{:S(2)}) %collective-permute-start.4) | collective-permute-done | bytes 524320 | tf_op jit(solution)/shard_map/ppermute | solution.py:234
  43.2 6.0 %attend.3 = (bf16[2,256,128]{2,1,0:T(8,128)(2,1)S(1)}, bf16[2,256,128]{2,1,0:T(8,128)(2,1)S(1)}, bf16[2,2,256,128]{3,2,1,0:T(8,128)(2,1)S(1)}, bf16[4,2,256,128]...) custom-call(s32[4]{0:T(128)S(1)} %pad_add_fusion.1.pos_ref, ...), custom_call_target="tpu_custom_call" | custom-call | flops 6039797760 | bytes 5242880 | tf_op jit(solution)/shard_map/attend/pallas_call | solution.py:163
  49.6 3.1 %collective-permute-start.15 = (bf16[4,2,256,128]{3,2,1,0:T(8,128)(2,1)S(1)}, bf16[4,2,256,128]{3,2,1,0:T(8,128)(2,1)S(1)}, u32[]{:S(2)}, u32[]{:S(2)}) collective-permute-start(bf16[4,2,256,128]{3,2,1,0:T(8,128)(2,1)S(1)} %get-tuple-element.46), channel_id=1, source_target_pairs={{0,4},{1,5},{2,6},{3,7},{4,0},{5,1},{6,2},{7,3},{8,12},{9,13},{10,... | collective-permute-start | bytes 1572872 | tf_op jit(solution)/shard_map/ppermute | solution.py:234
  52.8 6.0 %attend.4 = (bf16[2,256,128]{2,1,0:T(8,128)(2,1)S(1)}, bf16[2,256,128]{2,1,0:T(8,128)(2,1)S(1)}, bf16[2,2,256,128]{3,2,1,0:T(8,128)(2,1)S(1)}, bf16[4,2,256,128]...) custom-call(s32[4]{0:T(128)S(1)} %pad_add_fusion.1.pos_ref, ...), custom_call_target="tpu_custom_call" | custom-call | flops 6039797760 | bytes 5242880 | tf_op jit(solution)/shard_map/attend/pallas_call | solution.py:163
  58.7 2.0 %collective-permute-start.18 = (bf16[4,2,256,128]{3,2,1,0:T(8,128)(2,1)S(1)}, bf16[4,2,256,128]{3,2,1,0:T(8,128)(2,1)S(1)}, u32[]{:S(2)}, u32[]{:S(2)}) collective-permute-start(bf16[4,2,256,128]{3,2,1,0:T(8,128)(2,1)S(1)} %get-tuple-element.52), channel_id=1, source_target_pairs={{0,4},{1,5},{2,6},{3,7},{4,0},{5,1},{6,2},{7,3},{8,12},{9,13},{10,... | collective-permute-start | bytes 1572872 | tf_op jit(solution)/shard_map/ppermute | solution.py:234
  60.7 1.6 %collective-permute-start.11 = (bf16[2,2,256,128]{3,2,1,0:T(8,128)(2,1)S(1)}, bf16[2,2,256,128]{3,2,1,0:T(8,128)(2,1)S(1)}, u32[]{:S(2)}, u32[]{:S(2)}) collective-permute-start(bf16[2,2,256,128]{3,2,1,0:T(8,128)(2,1)S(1)} %get-tuple-element.43), channel_id=1, source_target_pairs={{0,2},{1,3},{2,0},{3,1},{4,6},{5,7},{6,4},{7,5},{8,10},{9,11},{10,... | collective-permute-start | bytes 786440 | tf_op jit(solution)/shard_map/ppermute | solution.py:223
  62.3 5.9 %attend.5 = (bf16[2,256,128]{2,1,0:T(8,128)(2,1)S(1)}, bf16[2,256,128]{2,1,0:T(8,128)(2,1)S(1)}, bf16[2,2,256,128]{3,2,1,0:T(8,128)(2,1)S(1)}, bf16[4,2,256,128]...) custom-call(s32[4]{0:T(128)S(1)} %pad_add_fusion.1.pos_ref, ...), custom_call_target="tpu_custom_call" | custom-call | flops 6039797760 | bytes 5242880 | tf_op jit(solution)/shard_map/attend/pallas_call | solution.py:163
  68.2 1.2 %collective-permute-done.11.refs_3_.refs_1_.refs_6_ = bf16[2,2,256,128]{3,2,1,0:T(8,128)(2,1)S(1)} collective-permute-done((bf16[2,2,256,128]{3,2,1,0:T(8,128)(2,1)S(1)}, bf16[2,2,256,128]{3,2,1,0:T(8,128)(2,1)S(1)}, u32[]{:S(2)}, u32[]{:S(2)}) %collective-permute-start.11) | collective-permute-done | bytes 262176 | tf_op jit(solution)/shard_map/ppermute | solution.py:223
  69.4 1.5 %collective-permute-start.22 = (bf16[4,2,256,128]{3,2,1,0:T(8,128)(2,1)S(1)}, bf16[4,2,256,128]{3,2,1,0:T(8,128)(2,1)S(1)}, u32[]{:S(2)}, u32[]{:S(2)}) collective-permute-start(bf16[4,2,256,128]{3,2,1,0:T(8,128)(2,1)S(1)} %get-tuple-element.65), channel_id=1, source_target_pairs={{0,4},{1,5},{2,6},{3,7},{4,0},{5,1},{6,2},{7,3},{8,12},{9,13},{10,... | collective-permute-start | bytes 1572872 | tf_op jit(solution)/shard_map/ppermute | solution.py:234
  71.7 1.6 %collective-permute-start.17 = (bf16[4,2,256,128]{3,2,1,0:T(8,128)(2,1)S(1)}, bf16[4,2,256,128]{3,2,1,0:T(8,128)(2,1)S(1)}, u32[]{:S(2)}, u32[]{:S(2)}) collective-permute-start(bf16[4,2,256,128]{3,2,1,0:T(8,128)(2,1)S(1)} %get-tuple-element.49), channel_id=1, source_target_pairs={{0,2},{1,3},{2,0},{3,1},{4,6},{5,7},{6,4},{7,5},{8,10},{9,11},{10,... | collective-permute-start | bytes 1572872 | tf_op jit(solution)/shard_map/ppermute | solution.py:223
  73.3 1.3 %odq_near.1 = bf16[2,2,2,256,128]{4,3,2,1,0:T(8,128)(2,1)S(1)} custom-call(s32[4]{0:T(128)S(1)} %pad_add_fusion.1.pos_ref, bf16[2,256,128]{2,1,0:T(8,128)(2,1)S(1)} %get-tuple-element.40.refs_0_, bf16[2,2,256,128]{3,2,1,0:T(8,128)(2,1)S(1)} %collective-permute-done.8.refs_1_.refs_8_.refs_4_, bf16[2,256,128]{2,1,0:T(8,128)(2,1)S(1)} %get-tuple-element.42.refs_2_, ...), custom_call_target="tpu_custom_call" | custom-call | tf_op jit(solution)/shard_map/odq_near/pallas_call | solution.py:81
  74.5 2.0 %collective-permute-done.18.halo_a = bf16[4,2,256,128]{3,2,1,0:T(8,128)(2,1)S(1)} collective-permute-done((bf16[4,2,256,128]{3,2,1,0:T(8,128)(2,1)S(1)}, bf16[4,2,256,128]{3,2,1,0:T(8,128)(2,1)S(1)}, u32[]{:S(2)}, u32[]{:S(2)}) %collective-permute-start.18) | collective-permute-done | bytes 524320 | tf_op jit(solution)/shard_map/ppermute | solution.py:234
  77.4 8.7 %collective-permute-done.22.halo_a = bf16[4,2,256,128]{3,2,1,0:T(8,128)(2,1)S(1)} collective-permute-done((bf16[4,2,256,128]{3,2,1,0:T(8,128)(2,1)S(1)}, bf16[4,2,256,128]{3,2,1,0:T(8,128)(2,1)S(1)}, u32[]{:S(2)}, u32[]{:S(2)}) %collective-permute-start.22) | collective-permute-done | bytes 524320 | tf_op jit(solution)/shard_map/ppermute | solution.py:234
  86.9 1.3 %late_near.1 = (bf16[1,2,2,256,128]{4,3,2,1,0:T(8,128)(2,1)S(1)}, bf16[1,2,2,256,128]{4,3,2,1,0:T(8,128)(2,1)S(1)}) custom-call(s32[4]{0:T(128)S(1)} %pad_add_fusion.1.pos_ref, bf16[2,256,128]{2,1,0:T(8,128)(2,1)S(1)} %get-tuple-element.44.refs_0_, bf16[4,2,256,128]{3,2,1,0:T(8,128)(2,1)S(1)} %collective-permute-done.17.refs_1_.refs_3_.refs_8_.refs_10_, ...), custom_call_target="tpu_custom_call" | custom-call | tf_op jit(solution)/shard_map/late_near/pallas_call | solution.py:81
  89.6 2.3 %collective-permute-done.25.refs_2_ = bf16[2,2,256,128]{3,2,1,0:T(8,128)(2,1)S(1)} collective-permute-done((bf16[2,2,256,128]{3,2,1,0:T(8,128)(2,1)S(1)}, bf16[2,2,256,128]{3,2,1,0:T(8,128)(2,1)S(1)}, u32[]{:S(2)}, u32[]{:S(2)}) %collective-permute-start.25) | collective-permute-done | bytes 262176 | tf_op jit(solution)/shard_map/ppermute | solution.py:223
  92.0 1.8 %collective-permute-start.28 = (bf16[2,256,128]{2,1,0:T(8,128)(2,1)S(1)}, bf16[2,256,128]{2,1,0:T(8,128)(2,1)S(1)}, u32[]{:S(2)}, u32[]{:S(2)}) collective-permute-start(bf16[2,256,128]{2,1,0:T(8,128)(2,1)S(1)} %get-tuple-element.76), channel_id=1, source_target_pairs={{0,3},{1,2},{2,1},{3,0},{4,7},{5,6},{6,5},{7,4},{8,11},{9,10},{10,... | collective-permute-start | bytes 393224 | tf_op jit(solution)/shard_map/ppermute | solution.py:223
  93.8 2.1 %outputs.1 = (bf16[256,1536]{1,0:T(8,128)(2,1)}, bf16[256,1536]{1,0:T(8,128)(2,1)}, bf16[256,1536]{1,0:T(8,128)(2,1)}, bf16[256,1536]{1,0:T(8,128)(2,1)}) custom-call(s32[4]{0:T(128)S(1)} %pad_add_fusion.1.pos_ref, bf16[2,2,2,256,128]{4,3,2,1,0:T(8,128)(2,1)S(1)} %collective-permute-done.12.refs_0_, ...), custom_call_target="tpu_custom_call" | custom-call | tf_op jit(solution)/shard_map/outputs/pallas_call | solution.py:81
  96.0 1.3 %collective-permute-done.28.refs_6_ = bf16[2,256,128]{2,1,0:T(8,128)(2,1)S(1)} collective-permute-done((bf16[2,256,128]{2,1,0:T(8,128)(2,1)S(1)}, bf16[2,256,128]{2,1,0:T(8,128)(2,1)S(1)}, u32[]{:S(2)}, u32[]{:S(2)}) %collective-permute-start.28) | collective-permute-done | bytes 131104 | tf_op jit(solution)/shard_map/ppermute | solution.py:223
  97.3 1.6 %last.1 = (bf16[256,1536]{1,0:T(8,128)(2,1)}, bf16[256,1536]{1,0:T(8,128)(2,1)}) custom-call(s32[4]{0:T(128)S(1)} %pad_add_fusion.1.pos_ref, bf16[2,256,128]{2,1,0:T(8,128)(2,1)S(1)} %get-tuple-element.63.refs_0_, bf16[2,2,256,128]{3,2,1,0:T(8,128)(2,1)S(1)} %collective-permute-done.24.refs_1_, ...), custom_call_target="tpu_custom_call", output_to_operand_aliasing={{0}: (8, {}), {1}: (9, {})} | custom-call | tf_op jit(solution)/shard_map/last/pallas_call | solution.py:81
  (65 shorter events, 11.2 us)
Async XLA Ops:
  3.8 2.5 %copy-start.1 = (bf16[256,1536]{1,0:T(8,128)(2,1)S(1)}, bf16[256,1536]{1,0:T(8,128)(2,1)}, u32[]{:S(2)}) copy-start(bf16[256,1536]{1,0:T(8,128)(2,1)} %refs_0_.12) | copy-start | bytes 2359300
  3.9 2.4 %collective-permute-start = (bf16[6,2,256,128]{3,2,1,0:T(8,128)(2,1)S(1)}, bf16[6,2,256,128]{3,2,1,0:T(8,128)(2,1)S(1)}, u32[]{:S(2)}, u32[]{:S(2)}) collective-permute-start(bf16[6,2,256,128]{3,2,1,0:T(8,128)(2,1)S(1)} %kv_for_near.1), channel_id=1, source_target_pairs={{0,1},{1,0},{2,3},{3,2},{4,5},{5,4},{6,7},{7,6},{8,9},{9,8},{10,11... | collective-permute-start | bytes 2359304 | tf_op jit(solution)/shard_map/ppermute | solution.py:223
  5.2 22.8 %collective-permute-start.6 = (bf16[6,2,256,128]{3,2,1,0:T(8,128)(2,1)S(1)}, bf16[6,2,256,128]{3,2,1,0:T(8,128)(2,1)S(1)}, u32[]{:S(2)}, u32[]{:S(2)}) collective-permute-start(bf16[6,2,256,128]{3,2,1,0:T(8,128)(2,1)S(1)} %qg_for_near.1), channel_id=1, source_target_pairs={{0,1},{1,0},{2,3},{3,2},{4,5},{5,4},{6,7},{7,6},{8,9},{9,8},{10,11... | collective-permute-start | bytes 2359304 | tf_op jit(solution)/shard_map/ppermute | solution.py:223
  8.5 15.3 %collective-permute-start.3 = (bf16[2,2,2,256,128]{4,3,2,1,0:T(8,128)(2,1)S(1)}, bf16[2,2,2,256,128]{4,3,2,1,0:T(8,128)(2,1)}, u32[]{:S(2)}, u32[]{:S(2)}) collective-permute-start(bf16[2,2,2,256,128]{4,3,2,1,0:T(8,128)(2,1)S(1)} %kv_for_far.2), channel_id=1, source_target_pairs={{0,2},{1,3},{2,0},{3,1},{4,6},{5,7},{6,4},{7,5},{8,10},{9,11},{10,... | collective-permute-start | bytes 1572872 | tf_op jit(solution)/shard_map/ppermute | solution.py:223
  11.5 22.7 %collective-permute-start.1 = (bf16[3,2,2,256,128]{4,3,2,1,0:T(8,128)(2,1)S(1)}, bf16[3,2,2,256,128]{4,3,2,1,0:T(8,128)(2,1)}, u32[]{:S(2)}, u32[]{:S(2)}) collective-permute-start(bf16[3,2,2,256,128]{4,3,2,1,0:T(8,128)(2,1)S(1)} %kv_near.1.refs_3_.refs_0_), channel_id=1, source_target_pairs={{0,4},{1,5},{2,6},{3,7},{4,0},{5,1},{6,2},{7,3},{8,12},{9,13},{10,... | collective-permute-start | bytes 2359304 | tf_op jit(solution)/shard_map/ppermute | solution.py:234
  13.0 21.1 %collective-permute-start.2 = (bf16[3,2,2,256,128]{4,3,2,1,0:T(8,128)(2,1)S(1)}, bf16[3,2,2,256,128]{4,3,2,1,0:T(8,128)(2,1)}, u32[]{:S(2)}, u32[]{:S(2)}) collective-permute-start(bf16[3,2,2,256,128]{4,3,2,1,0:T(8,128)(2,1)S(1)} %kv_near.1.refs_3_.refs_0_), channel_id=1, source_target_pairs={{0,1},{1,0},{2,3},{3,2},{4,8},{5,9},{6,10},{7,11},{8,4},{9,5},{10,... | collective-permute-start | bytes 2359304 | tf_op jit(solution)/shard_map/ppermute | solution.py:234
  24.6 9.4 %copy-start.6 = (s32[16,3]{0,1:T(4,128)S(1)}, s32[16,3]{0,1:T(4,128)}, u32[]{:S(2)}) copy-start(s32[16,3]{0,1:T(4,128)} %param.11) | copy-start | bytes 580
  24.6 9.3 %copy-start.7 = (s32[16,3]{0,1:T(4,128)S(1)}, s32[16,3]{0,1:T(4,128)}, u32[]{:S(2)}) copy-start(s32[16,3]{0,1:T(4,128)} %param.10) | copy-start | bytes 580
  24.6 7.9 %collective-permute-start.9 = (bf16[1,2,2,256,128]{4,3,2,1,0:T(8,128)(2,1)S(1)}, bf16[1,2,2,256,128]{4,3,2,1,0:T(8,128)(2,1)S(1)}, u32[]{:S(2)}, u32[]{:S(2)}) collective-permute-start(bf16[1,2,2,256,128]{4,3,2,1,0:T(8,128)(2,1)S(1)} %kv_for_far.3), channel_id=1, source_target_pairs={{0,2},{1,3},{2,0},{3,1},{4,6},{5,7},{6,4},{7,5},{8,10},{9,11},{10,... | collective-permute-start | bytes 786440 | tf_op jit(solution)/shard_map/ppermute | solution.py:223
  26.4 16.8 %collective-permute-start.4 = (bf16[2,2,2,256,128]{4,3,2,1,0:T(8,128)(2,1)}, bf16[2,2,2,256,128]{4,3,2,1,0:T(8,128)(2,1)}, u32[]{:S(2)}, u32[]{:S(2)}) collective-permute-start(bf16[2,2,2,256,128]{4,3,2,1,0:T(8,128)(2,1)} %collective-permute-done.3.refs_3_), channel_id=1, source_target_pairs={{0,4},{1,5},{2,6},{3,7},{4,0},{5,1},{6,2},{7,3},{8,12},{9,13},{10,... | collective-permute-start | bytes 1572872 | tf_op jit(solution)/shard_map/ppermute | solution.py:234
  28.0 15.3 %collective-permute-start.5 = (bf16[2,2,2,256,128]{4,3,2,1,0:T(8,128)(2,1)}, bf16[2,2,2,256,128]{4,3,2,1,0:T(8,128)(2,1)}, u32[]{:S(2)}, u32[]{:S(2)}) collective-permute-start(bf16[2,2,2,256,128]{4,3,2,1,0:T(8,128)(2,1)} %collective-permute-done.3.refs_3_), channel_id=1, source_target_pairs={{0,1},{1,0},{2,3},{3,2},{4,8},{5,9},{6,10},{7,11},{8,4},{9,5},{10,... | collective-permute-start | bytes 1572872 | tf_op jit(solution)/shard_map/ppermute | solution.py:234
  32.5 9.6 %collective-permute-start.7 = (bf16[1,2,2,256,128]{4,3,2,1,0:T(8,128)(2,1)}, bf16[1,2,2,256,128]{4,3,2,1,0:T(8,128)(2,1)}, u32[]{:S(2)}, u32[]{:S(2)}) collective-permute-start(bf16[1,2,2,256,128]{4,3,2,1,0:T(8,128)(2,1)} %qg_for_far.2), channel_id=1, source_target_pairs={{0,2},{1,3},{2,0},{3,1},{4,6},{5,7},{6,4},{7,5},{8,10},{9,11},{10,... | collective-permute-start | bytes 786440 | tf_op jit(solution)/shard_map/ppermute | solution.py:223
  35.1 17.6 %collective-permute-start.10 = (bf16[2,2,2,256,128]{4,3,2,1,0:T(8,128)(2,1)S(1)}, bf16[2,2,2,256,128]{4,3,2,1,0:T(8,128)(2,1)S(1)}, u32[]{:S(2)}, u32[]{:S(2)}) collective-permute-start(bf16[2,2,2,256,128]{4,3,2,1,0:T(8,128)(2,1)S(1)} %qg_for_far.3), channel_id=1, source_target_pairs={{0,2},{1,3},{2,0},{3,1},{4,6},{5,7},{6,4},{7,5},{8,10},{9,11},{10,... | collective-permute-start | bytes 1572872 | tf_op jit(solution)/shard_map/ppermute | solution.py:223
  35.8 22.9 %collective-permute-start.13 = (bf16[1,2,2,256,128]{4,3,2,1,0:T(8,128)(2,1)S(1)}, bf16[1,2,2,256,128]{4,3,2,1,0:T(8,128)(2,1)S(1)}, u32[]{:S(2)}, u32[]{:S(2)}) collective-permute-start(bf16[1,2,2,256,128]{4,3,2,1,0:T(8,128)(2,1)S(1)} %collective-permute-done.9.refs_3_), channel_id=1, source_target_pairs={{0,4},{1,5},{2,6},{3,7},{4,0},{5,1},{6,2},{7,3},{8,12},{9,13},{10,... | collective-permute-start | bytes 786440 | tf_op jit(solution)/shard_map/ppermute | solution.py:234
  42.1 18.6 %collective-permute-start.14 = (bf16[1,2,2,256,128]{4,3,2,1,0:T(8,128)(2,1)S(1)}, bf16[1,2,2,256,128]{4,3,2,1,0:T(8,128)(2,1)S(1)}, u32[]{:S(2)}, u32[]{:S(2)}) collective-permute-start(bf16[1,2,2,256,128]{4,3,2,1,0:T(8,128)(2,1)S(1)} %collective-permute-done.9.refs_3_), channel_id=1, source_target_pairs={{0,1},{1,0},{2,3},{3,2},{4,8},{5,9},{6,10},{7,11},{8,4},{9,5},{10,... | collective-permute-start | bytes 786440 | tf_op jit(solution)/shard_map/ppermute | solution.py:234
  49.3 11.4 %collective-permute-start.8 = (bf16[2,2,256,128]{3,2,1,0:T(8,128)(2,1)S(1)}, bf16[2,2,256,128]{3,2,1,0:T(8,128)(2,1)S(1)}, u32[]{:S(2)}, u32[]{:S(2)}) collective-permute-start(bf16[2,2,256,128]{3,2,1,0:T(8,128)(2,1)S(1)} %get-tuple-element.41), channel_id=1, source_target_pairs={{0,2},{1,3},{2,0},{3,1},{4,6},{5,7},{6,4},{7,5},{8,10},{9,11},{10,... | collective-permute-start | bytes 786440 | tf_op jit(solution)/shard_map/ppermute | solution.py:223
  49.6 21.3 %collective-permute-start.15 = (bf16[4,2,256,128]{3,2,1,0:T(8,128)(2,1)S(1)}, bf16[4,2,256,128]{3,2,1,0:T(8,128)(2,1)S(1)}, u32[]{:S(2)}, u32[]{:S(2)}) collective-permute-start(bf16[4,2,256,128]{3,2,1,0:T(8,128)(2,1)S(1)} %get-tuple-element.46), channel_id=1, source_target_pairs={{0,4},{1,5},{2,6},{3,7},{4,0},{5,1},{6,2},{7,3},{8,12},{9,13},{10,... | collective-permute-start | bytes 1572872 | tf_op jit(solution)/shard_map/ppermute | solution.py:234
  52.8 18.2 %collective-permute-start.16 = (bf16[4,2,256,128]{3,2,1,0:T(8,128)(2,1)S(1)}, bf16[4,2,256,128]{3,2,1,0:T(8,128)(2,1)S(1)}, u32[]{:S(2)}, u32[]{:S(2)}) collective-permute-start(bf16[4,2,256,128]{3,2,1,0:T(8,128)(2,1)S(1)} %get-tuple-element.47), channel_id=1, source_target_pairs={{0,1},{1,0},{2,3},{3,2},{4,8},{5,9},{6,10},{7,11},{8,4},{9,5},{10,... | collective-permute-start | bytes 1572872 | tf_op jit(solution)/shard_map/ppermute | solution.py:234
  58.7 17.8 %collective-permute-start.18 = (bf16[4,2,256,128]{3,2,1,0:T(8,128)(2,1)S(1)}, bf16[4,2,256,128]{3,2,1,0:T(8,128)(2,1)S(1)}, u32[]{:S(2)}, u32[]{:S(2)}) collective-permute-start(bf16[4,2,256,128]{3,2,1,0:T(8,128)(2,1)S(1)} %get-tuple-element.52), channel_id=1, source_target_pairs={{0,4},{1,5},{2,6},{3,7},{4,0},{5,1},{6,2},{7,3},{8,12},{9,13},{10,... | collective-permute-start | bytes 1572872 | tf_op jit(solution)/shard_map/ppermute | solution.py:234
  60.7 15.9 %collective-permute-start.19 = (bf16[4,2,256,128]{3,2,1,0:T(8,128)(2,1)S(1)}, bf16[4,2,256,128]{3,2,1,0:T(8,128)(2,1)S(1)}, u32[]{:S(2)}, u32[]{:S(2)}) collective-permute-start(bf16[4,2,256,128]{3,2,1,0:T(8,128)(2,1)S(1)} %get-tuple-element.53), channel_id=1, source_target_pairs={{0,1},{1,0},{2,3},{3,2},{4,8},{5,9},{6,10},{7,11},{8,4},{9,5},{10,... | collective-permute-start | bytes 1572872 | tf_op jit(solution)/shard_map/ppermute | solution.py:234
  60.7 8.7 %collective-permute-start.11 = (bf16[2,2,256,128]{3,2,1,0:T(8,128)(2,1)S(1)}, bf16[2,2,256,128]{3,2,1,0:T(8,128)(2,1)S(1)}, u32[]{:S(2)}, u32[]{:S(2)}) collective-permute-start(bf16[2,2,256,128]{3,2,1,0:T(8,128)(2,1)S(1)} %get-tuple-element.43), channel_id=1, source_target_pairs={{0,2},{1,3},{2,0},{3,1},{4,6},{5,7},{6,4},{7,5},{8,10},{9,11},{10,... | collective-permute-start | bytes 786440 | tf_op jit(solution)/shard_map/ppermute | solution.py:223
  69.4 16.7 %collective-permute-start.22 = (bf16[4,2,256,128]{3,2,1,0:T(8,128)(2,1)S(1)}, bf16[4,2,256,128]{3,2,1,0:T(8,128)(2,1)S(1)}, u32[]{:S(2)}, u32[]{:S(2)}) collective-permute-start(bf16[4,2,256,128]{3,2,1,0:T(8,128)(2,1)S(1)} %get-tuple-element.65), channel_id=1, source_target_pairs={{0,4},{1,5},{2,6},{3,7},{4,0},{5,1},{6,2},{7,3},{8,12},{9,13},{10,... | collective-permute-start | bytes 1572872 | tf_op jit(solution)/shard_map/ppermute | solution.py:234
  70.9 15.2 %collective-permute-start.23 = (bf16[4,2,256,128]{3,2,1,0:T(8,128)(2,1)S(1)}, bf16[4,2,256,128]{3,2,1,0:T(8,128)(2,1)S(1)}, u32[]{:S(2)}, u32[]{:S(2)}) collective-permute-start(bf16[4,2,256,128]{3,2,1,0:T(8,128)(2,1)S(1)} %get-tuple-element.66), channel_id=1, source_target_pairs={{0,1},{1,0},{2,3},{3,2},{4,8},{5,9},{6,10},{7,11},{8,4},{9,5},{10,... | collective-permute-start | bytes 1572872 | tf_op jit(solution)/shard_map/ppermute | solution.py:234
  71.7 15.2 %collective-permute-start.17 = (bf16[4,2,256,128]{3,2,1,0:T(8,128)(2,1)S(1)}, bf16[4,2,256,128]{3,2,1,0:T(8,128)(2,1)S(1)}, u32[]{:S(2)}, u32[]{:S(2)}) collective-permute-start(bf16[4,2,256,128]{3,2,1,0:T(8,128)(2,1)S(1)} %get-tuple-element.49), channel_id=1, source_target_pairs={{0,2},{1,3},{2,0},{3,1},{4,6},{5,7},{6,4},{7,5},{8,10},{9,11},{10,... | collective-permute-start | bytes 1572872 | tf_op jit(solution)/shard_map/ppermute | solution.py:223
  76.6 15.4 %collective-permute-start.12 = (bf16[2,2,2,256,128]{4,3,2,1,0:T(8,128)(2,1)S(1)}, bf16[2,2,2,256,128]{4,3,2,1,0:T(8,128)(2,1)S(1)}, u32[]{:S(2)}, u32[]{:S(2)}) collective-permute-start(bf16[2,2,2,256,128]{4,3,2,1,0:T(8,128)(2,1)S(1)} %odq_near.1), channel_id=1, source_target_pairs={{0,1},{1,0},{2,3},{3,2},{4,5},{5,4},{6,7},{7,6},{8,9},{9,8},{10,11... | collective-permute-start | bytes 1572872 | tf_op jit(solution)/shard_map/ppermute | solution.py:223
  77.3 14.6 %collective-permute-start.25 = (bf16[2,2,256,128]{3,2,1,0:T(8,128)(2,1)S(1)}, bf16[2,2,256,128]{3,2,1,0:T(8,128)(2,1)S(1)}, u32[]{:S(2)}, u32[]{:S(2)}) collective-permute-start(bf16[2,2,256,128]{3,2,1,0:T(8,128)(2,1)S(1)} %get-tuple-element.69), channel_id=1, source_target_pairs={{0,2},{1,3},{2,0},{3,1},{4,6},{5,7},{6,4},{7,5},{8,10},{9,11},{10,... | collective-permute-start | bytes 786440 | tf_op jit(solution)/shard_map/ppermute | solution.py:223
  88.2 5.6 %collective-permute-start.20 = (bf16[1,2,2,256,128]{4,3,2,1,0:T(8,128)(2,1)S(1)}, bf16[1,2,2,256,128]{4,3,2,1,0:T(8,128)(2,1)S(1)}, u32[]{:S(2)}, u32[]{:S(2)}) collective-permute-start(bf16[1,2,2,256,128]{4,3,2,1,0:T(8,128)(2,1)S(1)} %get-tuple-element.55), channel_id=1, source_target_pairs={{0,1},{1,0},{2,3},{3,2},{4,5},{5,4},{6,7},{7,6},{8,9},{9,8},{10,11... | collective-permute-start | bytes 786440 | tf_op jit(solution)/shard_map/ppermute | solution.py:223
  88.3 7.7 %collective-permute-start.27 = (bf16[2,256,128]{2,1,0:T(8,128)(2,1)S(1)}, bf16[2,256,128]{2,1,0:T(8,128)(2,1)S(1)}, u32[]{:S(2)}, u32[]{:S(2)}) collective-permute-start(bf16[2,256,128]{2,1,0:T(8,128)(2,1)S(1)} %get-tuple-element.77), channel_id=1, source_target_pairs={{0,2},{1,3},{2,0},{3,1},{4,6},{5,7},{6,4},{7,5},{8,10},{9,11},{10,... | collective-permute-start | bytes 393224 | tf_op jit(solution)/shard_map/ppermute | solution.py:223
  89.4 7.8 %collective-permute-start.24 = (bf16[2,2,256,128]{3,2,1,0:T(8,128)(2,1)S(1)}, bf16[2,2,256,128]{3,2,1,0:T(8,128)(2,1)S(1)}, u32[]{:S(2)}, u32[]{:S(2)}) collective-permute-start(bf16[2,2,256,128]{3,2,1,0:T(8,128)(2,1)S(1)} %get-tuple-element.68), channel_id=1, source_target_pairs={{0,1},{1,0},{2,3},{3,2},{4,5},{5,4},{6,7},{7,6},{8,9},{9,8},{10,11... | collective-permute-start | bytes 786440 | tf_op jit(solution)/shard_map/ppermute | solution.py:223
  91.9 1.9 %collective-permute-start.21 = (bf16[1,2,2,256,128]{4,3,2,1,0:T(8,128)(2,1)S(1)}, bf16[1,2,2,256,128]{4,3,2,1,0:T(8,128)(2,1)S(1)}, u32[]{:S(2)}, u32[]{:S(2)}) collective-permute-start(bf16[1,2,2,256,128]{4,3,2,1,0:T(8,128)(2,1)S(1)} %get-tuple-element.56), channel_id=1, source_target_pairs={{0,1},{1,0},{2,3},{3,2},{4,5},{5,4},{6,7},{7,6},{8,9},{9,8},{10,11... | collective-permute-start | bytes 786440 | tf_op jit(solution)/shard_map/ppermute | solution.py:223
  92.0 5.3 %collective-permute-start.28 = (bf16[2,256,128]{2,1,0:T(8,128)(2,1)S(1)}, bf16[2,256,128]{2,1,0:T(8,128)(2,1)S(1)}, u32[]{:S(2)}, u32[]{:S(2)}) collective-permute-start(bf16[2,256,128]{2,1,0:T(8,128)(2,1)S(1)} %get-tuple-element.76), channel_id=1, source_target_pairs={{0,3},{1,2},{2,1},{3,0},{4,7},{5,6},{6,5},{7,4},{8,11},{9,10},{10,... | collective-permute-start | bytes 393224 | tf_op jit(solution)/shard_map/ppermute | solution.py:223
  93.8 3.5 %collective-permute-start.26 = (bf16[2,256,128]{2,1,0:T(8,128)(2,1)S(1)}, bf16[2,256,128]{2,1,0:T(8,128)(2,1)S(1)}, u32[]{:S(2)}, u32[]{:S(2)}) collective-permute-start(bf16[2,256,128]{2,1,0:T(8,128)(2,1)S(1)} %slice_bitcast_fusion), channel_id=1, source_target_pairs={{0,1},{1,0},{2,3},{3,2},{4,5},{5,4},{6,7},{7,6},{8,9},{9,8},{10,11... | collective-permute-start | bytes 393224 | tf_op jit(solution)/shard_map/ppermute | solution.py:223
  (5 other events, 7.5 us)
